TPU v7x, 768 devices: a whole 4x8x12 slice. The times are simulated.
768 devices in a mesh: dom: 96 (over x, z, core), sub: 8 (over y).
Axes of the slice: x: 4, y: 8, z: 12, core: 2. Of those that a mesh axis runs over, the one named last changes fastest.
Arguments:
- state: float32 [5, 64, 24576], P(None, None, ('dom', 'sub')), may hold values from -0.9 to 0.9
- adjoint_final: float32 [5, 64, 24576], P(None, None, ('dom', 'sub')), may hold values from -6 to 6
- send_slot: int32 [768, 384], P(('dom', 'sub')), may hold values from 0 to 192, as said below
- ext_index: int32 [6, 24576], P(None, ('dom', 'sub')), may hold values from 0 to 576, as said below
- ext_perm: int32 [6, 24576], P(None, ('dom', 'sub')), may hold values from 0 to 7
Outputs:
- state_end: float32 [5, 64, 24576], P(None, None, ('dom', 'sub'))
- adjoint_start: float32 [5, 64, 24576], P(None, None, ('dom', 'sub'))
Inputs may be any that keep to these rules, and one draw needn't show every extreme that they name: `send_slot`: A value of 192 marks an empty slot, which carries zeros; the share of occupied slots differs from device to device, and device 0 fills all its slots. `ext_index`: values below 192 name a face of the same device, values from 192 to 575 a received slot, and 576 a wall.
All inputs are finite; a program needn't handle non-finite values.
Results may differ from a plain program's by a relative error of at most 0.0006.
Values may be sent and summed in bfloat16 or wider, within the bound.
No kernel may reach another device: no remote copies, remote signals or barrier semaphores. Data moves between devices by JAX's collectives and lax.ppermute only.
A program may use at most 64 MiB of HBM per device.

v0:
```python
import jax
import jax.numpy as jnp
import numpy as np
from jax import lax
from jax.sharding import PartitionSpec as P

step_size = 0.02
mean_flow = 0.3
penalty = 2.0
metric = 2.0
lift_factor = 12.0


def as_sent(x):

    def short(part):
        return part.astype(jnp.bfloat16) if part.dtype == jnp.float32 else part

    return jax.tree.map(short, x)


def from_behind(value, axis, steps):
    count = lax.axis_size(axis)
    pairs = [(source, (source + steps) % count) for source in range(count)]
    return lax.ppermute(value, axis, pairs)


def derivative_table():
    points = np.array([-1.0, -1.0 / np.sqrt(5.0), 1.0 / np.sqrt(5.0), 1.0])
    products = np.array(
        [
            np.prod([points[target] - points[source] for source in range(4) if source != target])
            for target in range(4)
        ]
    )
    result = np.zeros((4, 4))
    for target in range(4):
        for source in range(4):
            if target != source:
                result[target, source] = products[target] / (
                    products[source] * (points[target] - points[source])
                )
        result[target, target] = -np.sum(result[target])
    return result.astype(np.float32)


def symmetry_table():
    result = np.zeros((8, 16), np.int32)
    for symmetry in range(8):
        layout = np.arange(16).reshape(4, 4)
        if symmetry & 4:
            layout = layout.T
        if symmetry & 1:
            layout = layout[::-1]
        if symmetry & 2:
            layout = layout[:, ::-1]
        result[symmetry] = layout.reshape(-1)
    return result


def normal_table():
    result = np.zeros((3, 6), np.float32)
    for facet in range(6):
        result[facet // 2, facet] = 2.0 * (facet % 2) - 1.0
    return result


def flux_along(fields, drift, normal_speed, pressure_weights):
    density = fields[0]
    pressure = fields[4]
    components = [drift * density + (1.0 + density) * normal_speed]
    for member in range(3):
        velocity = fields[1 + member]
        components.append(
            drift * velocity + velocity * normal_speed + pressure_weights[member] * pressure
        )
    components.append(drift * pressure + (1.0 + pressure) * normal_speed)
    return jnp.stack(components)


def volume_term(field):
    elements = field.shape[2]
    derivative = derivative_table()
    table = jnp.asarray(derivative, jnp.float32)
    merged = 4 * elements
    total = jnp.zeros((5, 4, 4, merged), jnp.float32)
    for direction in range(3):
        drift = mean_flow if direction == 0 else 0.0
        weights = [1.0 if member == direction else 0.0 for member in range(3)]
        flux = flux_along(field, drift, field[1 + direction], weights).reshape(5, 4, 4, merged)
        if direction == 0:
            total = total + jnp.einsum(
                "ai,vijm->vajm", table, flux, precision=lax.Precision.HIGHEST
            )
        elif direction == 1:
            total = total + jnp.einsum(
                "aj,vijm->viam", table, flux, precision=lax.Precision.HIGHEST
            )
        else:
            blocks = [flux[..., index * elements : (index + 1) * elements] for index in range(4)]
            outputs = []
            for target in range(4):
                accum = float(derivative[target, 0]) * blocks[0]
                for index in range(1, 4):
                    accum = accum + float(derivative[target, index]) * blocks[index]
                outputs.append(accum)
            total = total + jnp.concatenate(outputs, axis=3)
    return -metric * total.reshape(5, 64, elements)


def normal_flux(trace):
    normals = normal_table()
    weights = [jnp.asarray(normals[member], jnp.float32)[:, None] for member in range(3)]
    normal_speed = weights[0] * trace[1] + weights[1] * trace[2] + weights[2] * trace[3]
    return flux_along(trace, mean_flow * weights[0], normal_speed, weights)


def face_traces(field):
    elements = field.shape[2]
    cube = field.reshape(5, 4, 4, 4, elements)
    surfaces = [
        cube[:, 0],
        cube[:, 3],
        cube[:, :, 0],
        cube[:, :, 3],
        cube[:, :, :, 0],
        cube[:, :, :, 3],
    ]
    return jnp.stack([surface.reshape(5, 16, elements) for surface in surfaces], axis=2).reshape(
        5, 16, 6 * elements
    )


def pack_sends(field, slots, n_sub):
    traces = face_traces(field)
    padded = jnp.concatenate([traces, jnp.zeros((5, 16, 1), traces.dtype)], axis=2)
    picked = jnp.take(padded, slots, axis=2)
    return picked.transpose(2, 0, 1).reshape(3, n_sub, -1)


def residual(field, arrived, ext_index, ext_perm):
    elements = field.shape[2]
    symmetries = symmetry_table()
    traces = face_traces(field)
    incoming = arrived.reshape(-1, 5, 16).transpose(1, 2, 0)
    lookup = jnp.concatenate([traces, incoming, jnp.zeros((5, 16, 1), traces.dtype)], axis=2)
    count = lookup.shape[2]
    flattened = ext_index.reshape(-1)
    orient = ext_perm.reshape(-1)
    matches = orient[None, None, :] == jnp.arange(8, dtype=jnp.int32)[:, None, None]
    node_map = jnp.sum(jnp.where(matches, jnp.asarray(symmetries)[:, :, None], 0), axis=0).astype(
        jnp.int32
    )
    gather_index = node_map * count + flattened[None, :]
    exterior = jnp.take(lookup.reshape(5, -1), gather_index, axis=1)
    direction = jnp.arange(6 * elements, dtype=jnp.int32) // elements // 2
    component = jnp.arange(5, dtype=jnp.int32)[:, None]
    mirror_sign = jnp.where(component == 1 + direction[None, :], -1.0, 1.0).astype(jnp.float32)[
        :, None, :
    ]
    at_wall = (flattened == count - 1)[None, None, :]
    exterior = jnp.where(at_wall, traces * mirror_sign, exterior)
    interior = traces.reshape(5, 16, 6, elements)
    exterior = exterior.reshape(5, 16, 6, elements)
    penalty_jump = 0.5 * (normal_flux(interior) - normal_flux(exterior)) + 0.5 * penalty * (
        exterior - interior
    )
    jumps = penalty_jump.reshape(5, 4, 4, 6, elements)
    lifted = jnp.zeros((5, 4, 4, 4, elements), jnp.float32)
    lifted = lifted.at[:, 0].add(jumps[:, :, :, 0])
    lifted = lifted.at[:, 3].add(jumps[:, :, :, 1])
    lifted = lifted.at[:, :, 0].add(jumps[:, :, :, 2])
    lifted = lifted.at[:, :, 3].add(jumps[:, :, :, 3])
    lifted = lifted.at[:, :, :, 0].add(jumps[:, :, :, 4])
    lifted = lifted.at[:, :, :, 3].add(jumps[:, :, :, 5])
    return volume_term(field) + lift_factor * lifted.reshape(5, 64, elements)


def sub_forward(buffer):
    return lax.all_to_all(buffer, "sub", split_axis=1, concat_axis=1, tiled=True)


def sub_backward(buffer):
    return lax.all_to_all(as_sent(buffer), "sub", split_axis=1, concat_axis=1, tiled=True).astype(
        buffer.dtype
    )


def dom_forward(buffer):
    pieces = [buffer[0:1], buffer[1:2], buffer[2:3]]
    for group_id, offset in ((0, -1), (2, 1)):
        pieces[group_id] = from_behind(buffer[group_id : group_id + 1], "dom", offset)
    return jnp.concatenate(pieces, axis=0)


def dom_backward(buffer):
    pieces = [buffer[0:1], buffer[1:2], buffer[2:3]]
    for group_id, offset in ((0, 1), (2, -1)):
        pieces[group_id] = from_behind(
            buffer[group_id : group_id + 1].astype(jnp.bfloat16), "dom", offset
        ).astype(jnp.float32)
    return jnp.concatenate(pieces, axis=0)


def forward_move(buffer):
    return dom_forward(sub_forward(buffer))


def backward_move(buffer):
    return sub_backward(dom_backward(buffer))


def shards(state, adjoint_final, send_slot, ext_index, ext_perm):
    n_sub = lax.axis_size("sub")
    slots = send_slot.reshape(-1)

    def evaluate(current):
        outgoing = pack_sends(current, slots, n_sub).astype(jnp.bfloat16)
        arrived = forward_move(outgoing).astype(jnp.float32)
        return (residual(current, arrived, ext_index, ext_perm), arrived)

    def pull_back(current, arrived, cotangent):
        _, pullback = jax.vjp(
            lambda first, second: residual(first, second, ext_index, ext_perm), current, arrived
        )
        grad_state, grad_arrived = pullback(cotangent)
        returned = backward_move(grad_arrived)
        _, pack_pullback = jax.vjp(lambda first: pack_sends(first, slots, n_sub), current)
        return grad_state + pack_pullback(returned)[0]

    rate_first, arrived_first = evaluate(state)
    middle = state + step_size * rate_first
    rate_second, arrived_second = evaluate(middle)
    final = 0.5 * state + 0.5 * (middle + step_size * rate_second)
    back_middle = 0.5 * adjoint_final + 0.5 * step_size * pull_back(
        middle, arrived_second, adjoint_final
    )
    back_start = (
        0.5 * adjoint_final + back_middle + step_size * pull_back(state, arrived_first, back_middle)
    )
    return (final, back_start)


def solution(mesh):
    return jax.shard_map(
        shards,
        mesh=mesh,
        in_specs=(
            P(None, None, ("dom", "sub")),
            P(None, None, ("dom", "sub")),
            P(("dom", "sub"), None),
            P(None, ("dom", "sub")),
            P(None, ("dom", "sub")),
        ),
        out_specs=(P(None, None, ("dom", "sub")), P(None, None, ("dom", "sub"))),
        check_vma=False,
    )
```

profile of v0, /device:TPU:8, one launch (start us, length us, event | category | flops | bytes accessed | tf_op | source)
XLA Modules:
  0.0 273.1 jit_solution(10777783976998210311)
XLA Ops:
  0.6 1.0 copy.1429
  3.3 1.7 gather_fusion
  5.0 1.3 fusion.10
  7.7 12.7 %all-to-all-start = ((bf16[3,8,1280]{2,0,1:T(4,128)(2,1)}), bf16[3,8,1280]{2,0,1:T(4,128)(2,1)S(1)}, u32[]{:S(2)}, u32[]{:S(2)}) async-start(bf16[3,8,1280]{2,0,1:T(4,128)(2,1)} %copy.1383), calls=%async_computation | async-start | bytes 163840 | tf_op jit(solution)/shard_map/all_to_all | solution.py:180
  25.9 1.6 all-to-all-done
  27.6 9.6 %collective-permute-start = (bf16[1,8,1280]{2,1,0:T(8,128)(2,1)S(1)}, bf16[1,8,1280]{2,1,0:T(8,128)(2,1)S(1)}, u32[]{:S(2)}, u32[]{:S(2)}) collective-permute-start(bf16[1,8,1280]{2,1,0:T(8,128)(2,1)S(1)} %copy.1576), channel_id=1, source_target_pairs={{0,760},{8,0},{16,8},{24,16},{32,24},{40,32},{48,40},{56,48},{64,5... | collective-permute-start | bytes 61448 | tf_op jit(solution)/shard_map/ppermute | solution.py:25
  37.3 2.4 collective-permute-start.1
  40.3 0.8 mul.2700
  52.2 1.2 stack.220
  54.7 3.3 %copy.1388 = f32[5,9232]{0,1:T(8,128)} copy(f32[5,9232]{1,0:T(8,128)S(1)} %reshape.2124) | data formatting | bytes 369280 | tf_op jit(solution)/shard_map/reshape | solution.py:155
  58.1 10.5 %gather_fusion.1 = f32[3072,5]{1,0:T(8,128)S(1)} fusion(f32[5,9232]{0,1:T(8,128)} %copy.1388, s32[3072]{0:T(1024)S(1)} %copy-done.25), kind=kCustom, calls=%fused_computation.1.clone | custom fusion | bytes 135168 | tf_op jit(solution)/shard_map/jit(_take)/gather | solution.py:155
  71.3 1.6 scatter-add.90
  73.0 1.6 scatter-add.91
  77.6 0.9 concatenate.75
  78.5 2.0 gather_fusion.2
  80.5 1.3 fusion.11
  83.3 6.6 %all-to-all-start.1 = ((bf16[3,8,1280]{2,0,1:T(4,128)(2,1)}), bf16[3,8,1280]{2,0,1:T(4,128)(2,1)S(1)}, u32[]{:S(2)}, u32[]{:S(2)}) async-start(bf16[3,8,1280]{2,0,1:T(4,128)(2,1)} %copy.1414), calls=%async_computation.1 | async-start | bytes 163840 | tf_op jit(solution)/shard_map/all_to_all | solution.py:180
  89.9 1.5 fusion.53
  95.0 2.0 all-to-all-done.1
  97.1 5.5 %collective-permute-start.2 = (bf16[1,8,1280]{2,1,0:T(8,128)(2,1)S(1)}, bf16[1,8,1280]{2,1,0:T(8,128)(2,1)S(1)}, u32[]{:S(2)}, u32[]{:S(2)}) collective-permute-start(bf16[1,8,1280]{2,1,0:T(8,128)(2,1)S(1)} %copy.1583), channel_id=1, source_target_pairs={{0,760},{8,0},{16,8},{24,16},{32,24},{40,32},{48,40},{56,48},{64,5... | collective-permute-start | bytes 61448 | tf_op jit(solution)/shard_map/ppermute | solution.py:25
  102.7 2.1 collective-permute-start.3
  107.2 0.8 reshape.2137
  109.4 0.8 mul.2789
  110.2 1.6 stack.251
  113.0 3.3 %copy.1419 = f32[5,9232]{0,1:T(8,128)} copy(f32[5,9232]{1,0:T(8,128)S(1)} %reshape.2130) | data formatting | bytes 369280 | tf_op jit(solution)/shard_map/reshape | solution.py:155
  116.4 10.5 %gather_fusion.3 = f32[3072,5]{1,0:T(8,128)S(1)} fusion(f32[5,9232]{0,1:T(8,128)} %copy.1419, s32[3072]{0:T(1024)S(1)} %copy-done.26), kind=kCustom, calls=%fused_computation.4.clone | custom fusion | bytes 135168 | tf_op jit(solution)/shard_map/jit(_take)/gather | solution.py:155
  129.9 19.4 %scatter_custom_fusion = f32[5,9232]{0,1:T(8,128)} fusion(s32[3072]{0:T(1024)} %reshape.2211, f32[3072,5]{1,0:T(8,128)S(1)} %bitcast.261, f32[]{:T(128)} %constant.400.clone.1), kind=kCustom, calls=%fused_computation.12 | custom fusion | flops 15360 | bytes 185152 | tf_op jit(solution)/shard_map/transpose(jvp(jit(_take)))/scatter-add | solution.py:155
  149.3 3.5 %copy.1472 = f32[5,9232]{1,0:T(8,128)S(1)} copy(f32[5,9232]{0,1:T(8,128)} %scatter_custom_fusion) | data formatting | bytes 369280 | tf_op jit(solution)/shard_map/transpose(jvp(jit(_take)))/scatter-add | solution.py:155
  153.9 1.9 collective-permute-start.4
  156.3 7.0 %collective-permute-start.5 = (bf16[1,8,1280]{2,1,0:T(8,128)(2,1)S(1)}, bf16[1,8,1280]{2,1,0:T(8,128)(2,1)S(1)}, u32[]{:S(2)}, u32[]{:S(2)}) collective-permute-start(bf16[1,8,1280]{2,1,0:T(8,128)(2,1)S(1)} %convert_element_type.93), channel_id=1, source_target_pairs={{0,760},{8,0},{16,8},{24,16},{32,24},{40,32},{48,40},{56,48},{64,5... | collective-permute-start | bytes 61448 | tf_op jit(solution)/shard_map/ppermute | solution.py:25
  163.8 0.9 reshape.2131
  166.0 6.4 %all-to-all-start.2 = ((bf16[3,8,1280]{2,0,1:T(4,128)(2,1)}), bf16[3,8,1280]{2,0,1:T(4,128)(2,1)S(1)}, u32[]{:S(2)}, u32[]{:S(2)}) async-start(bf16[3,8,1280]{2,0,1:T(4,128)(2,1)} %copy.1481), calls=%async_computation.2 | async-start | bytes 163840 | tf_op jit(solution)/shard_map/all_to_all | solution.py:184
  173.2 6.2 %all-to-all-done.2 = bf16[3,8,1280]{2,0,1:T(4,128)(2,1)S(1)} async-done(((bf16[3,8,1280]{2,0,1:T(4,128)(2,1)}), bf16[3,8,1280]{2,0,1:T(4,128)(2,1)S(1)}, u32[]{:S(2)}, u32[]{:S(2)}) %all-to-all-start.2) | async-done | bytes 61472 | tf_op jit(solution)/shard_map/all_to_all | solution.py:184
  180.0 14.6 %scatter_fusion = f32[5,16,193]{1,0,2:T(8,128)S(1)} fusion(f32[5,16,193]{1,0,2:T(8,128)S(1)} %broadcast_in_dim.132.clone, s32[384]{0:T(512)S(1)} %copy-done.123, f32[384,5,16]{2,1,0:T(8,128)S(1)} %reshape.2159), kind=kCustom, calls=%fused_computation.7 | custom fusion | flops 30720 | bytes 370176 | tf_op jit(solution)/shard_map/transpose(jvp(jit(_take)))/scatter-add | solution.py:137
  201.1 19.4 %scatter_custom_fusion.2 = f32[5,9232]{0,1:T(8,128)} fusion(s32[3072]{0:T(1024)} %reshape.2211, f32[3072,5]{1,0:T(8,128)S(1)} %bitcast.260, f32[]{:T(128)} %constant.400.clone.1), kind=kCustom, calls=%fused_computation.10 | custom fusion | flops 15360 | bytes 185152 | tf_op jit(solution)/shard_map/transpose(jvp(jit(_take)))/scatter-add | solution.py:155
  220.5 3.5 %copy.1533 = f32[5,9232]{1,0:T(8,128)S(1)} copy(f32[5,9232]{0,1:T(8,128)} %scatter_custom_fusion.2) | data formatting | bytes 369280 | tf_op jit(solution)/shard_map/transpose(jvp(jit(_take)))/scatter-add | solution.py:155
  225.1 0.8 convert_element_type.94
  225.9 1.9 collective-permute-start.6
  228.0 0.8 convert_element_type.95
  228.9 7.0 %collective-permute-start.7 = (bf16[1,8,1280]{2,1,0:T(8,128)(2,1)}, bf16[1,8,1280]{2,1,0:T(8,128)(2,1)}, u32[]{:S(2)}, u32[]{:S(2)}) collective-permute-start(bf16[1,8,1280]{2,1,0:T(8,128)(2,1)} %convert_element_type.95), channel_id=1, source_target_pairs={{0,760},{8,0},{16,8},{24,16},{32,24},{40,32},{48,40},{56,48},{64,5... | collective-permute-start | bytes 61448 | tf_op jit(solution)/shard_map/ppermute | solution.py:25
  236.5 1.6 scatter-add.96
  238.2 1.6 scatter-add.97
  242.6 0.8 pad_maximum_fusion.1
  244.0 4.3 %all-to-all-start.3 = ((bf16[3,8,1280]{2,0,1:T(4,128)(2,1)}), bf16[3,8,1280]{2,0,1:T(4,128)(2,1)S(1)}, u32[]{:S(2)}, u32[]{:S(2)}) async-start(bf16[3,8,1280]{2,0,1:T(4,128)(2,1)} %copy.1542), calls=%async_computation.3 | async-start | bytes 163840 | tf_op jit(solution)/shard_map/all_to_all | solution.py:184
  248.5 0.7 copy.1555
  249.2 6.2 %all-to-all-done.3 = bf16[3,8,1280]{2,0,1:T(4,128)(2,1)S(1)} async-done(((bf16[3,8,1280]{2,0,1:T(4,128)(2,1)}), bf16[3,8,1280]{2,0,1:T(4,128)(2,1)S(1)}, u32[]{:S(2)}, u32[]{:S(2)}) %all-to-all-start.3) | async-done | bytes 61472 | tf_op jit(solution)/shard_map/all_to_all | solution.py:184
  256.0 14.6 %scatter_fusion.1 = f32[5,16,193]{1,0,2:T(8,128)S(1)} fusion(f32[5,16,193]{1,0,2:T(8,128)S(1)} %broadcast_in_dim.132, s32[384]{0:T(512)S(1)} %copy-done.124, f32[384,5,16]{2,1,0:T(8,128)S(1)} %reshape.2160), kind=kCustom, calls=%fused_computation.9 | custom fusion | flops 30720 | bytes 370176 | tf_op jit(solution)/shard_map/transpose(jvp(jit(_take)))/scatter-add | solution.py:137
  272.2 0.7 copy.1556
  (673 shorter events, 56.6 us)
Async XLA Ops:
  5.0 15.5 %copy-start.111 = (f32[5,64,32]{1,2,0:T(8,128)S(1)}, f32[5,64,32]{1,2,0:T(8,128)}, u32[]{:S(2)}) copy-start(f32[5,64,32]{1,2,0:T(8,128)} %param.68) | copy-start | bytes 122884
  6.3 14.4 %copy-start.130 = (s32[6,32]{1,0:T(8,128)S(1)}, s32[6,32]{1,0:T(8,128)}, u32[]{:S(2)}) copy-start(s32[6,32]{1,0:T(8,128)} %param.70) | copy-start | bytes 2308
  6.4 14.5 %copy-start.131 = (s32[6,32]{1,0:T(8,128)S(1)}, s32[6,32]{1,0:T(8,128)}, u32[]{:S(2)}) copy-start(s32[6,32]{1,0:T(8,128)} %param.71) | copy-start | bytes 2308
  6.4 15.1 %copy-start.132 = (s32[8,16]{1,0:T(8,128)S(1)}, s32[8,16]{1,0:T(8,128)}, u32[]{:S(2)}) copy-start(s32[8,16]{1,0:T(8,128)} %constant.431.clone) | copy-start | bytes 1540
  6.4 15.9 %copy-start.24 = (f32[6]{0:T(128)S(1)}, f32[6]{0:T(128)}, u32[]{:S(2)}) copy-start(f32[6]{0:T(128)} %constant.673) | copy-start | bytes 76
  6.4 15.9 %copy-start.94 = (f32[6]{0:T(128)S(1)}, f32[6]{0:T(128)}, u32[]{:S(2)}) copy-start(f32[6]{0:T(128)} %constant.434.clone) | copy-start | bytes 76
  6.4 15.9 %copy-start.99 = (f32[6]{0:T(128)S(1)}, f32[6]{0:T(128)}, u32[]{:S(2)}) copy-start(f32[6]{0:T(128)} %constant.432.clone) | copy-start | bytes 76
  6.4 15.9 %copy-start.105 = (f32[6]{0:T(128)S(1)}, f32[6]{0:T(128)}, u32[]{:S(2)}) copy-start(f32[6]{0:T(128)} %constant.433.clone) | copy-start | bytes 76
  7.7 19.8 %all-to-all-start = ((bf16[3,8,1280]{2,0,1:T(4,128)(2,1)}), bf16[3,8,1280]{2,0,1:T(4,128)(2,1)S(1)}, u32[]{:S(2)}, u32[]{:S(2)}) async-start(bf16[3,8,1280]{2,0,1:T(4,128)(2,1)} %copy.1383), calls=%async_computation | async-start | bytes 163840 | tf_op jit(solution)/shard_map/all_to_all | solution.py:180
  21.6 47.6 %copy-start.116 = (pred[16,192]{1,0:T(8,128)(4,1)}, pred[16,192]{1,0:T(8,128)(4,1)S(1)}, u32[]{:S(2)}) copy-start(pred[16,192]{1,0:T(8,128)(4,1)S(1)} %get-tuple-element.190) | copy-start | bytes 9220
  22.3 46.9 %copy-start.19 = (f32[5,192]{1,0:T(8,128)}, f32[5,192]{1,0:T(8,128)S(1)}, u32[]{:S(2)}) copy-start(f32[5,192]{1,0:T(8,128)S(1)} %fusion.54) | copy-start | bytes 11524
  24.9 14.7 %copy-start.127 = (s32[1,384]{1,0:T(1,128)S(1)}, s32[1,384]{1,0:T(1,128)}, u32[]{:S(2)}) copy-start(s32[1,384]{1,0:T(1,128)} %param.69) | copy-start | bytes 4612
  25.9 27.6 %copy-start.5 = (f32[5,4,4,6,32]{4,3,2,1,0:T(8,128)}, f32[5,4,4,6,32]{4,3,2,1,0:T(8,128)S(1)}, u32[]{:S(2)}) copy-start(f32[5,4,4,6,32]{4,3,2,1,0:T(8,128)S(1)} %constant_dynamic-update-slice_fusion.22) | copy-start | bytes 184324
  27.6 25.8 %collective-permute-start = (bf16[1,8,1280]{2,1,0:T(8,128)(2,1)S(1)}, bf16[1,8,1280]{2,1,0:T(8,128)(2,1)S(1)}, u32[]{:S(2)}, u32[]{:S(2)}) collective-permute-start(bf16[1,8,1280]{2,1,0:T(8,128)(2,1)S(1)} %copy.1576), channel_id=1, source_target_pairs={{0,760},{8,0},{16,8},{24,16},{32,24},{40,32},{48,40},{56,48},{64,5... | collective-permute-start | bytes 61448 | tf_op jit(solution)/shard_map/ppermute | solution.py:25
  37.3 16.2 %collective-permute-start.1 = (bf16[1,8,1280]{2,1,0:T(8,128)(2,1)S(1)}, bf16[1,8,1280]{2,1,0:T(8,128)(2,1)S(1)}, u32[]{:S(2)}, u32[]{:S(2)}) collective-permute-start(bf16[1,8,1280]{2,1,0:T(8,128)(2,1)S(1)} %copy.1578), channel_id=1, source_target_pairs={{0,8},{8,16},{16,24},{24,32},{32,40},{40,48},{48,56},{56,64},{64,7... | collective-permute-start | bytes 61448 | tf_op jit(solution)/shard_map/ppermute | solution.py:25
  77.2 17.5 %copy-start.11 = (f32[1,16,6,32]{3,1,0,2:T(8,128)}, f32[1,16,6,32]{3,1,0,2:T(8,128)S(1)}, u32[]{:S(2)}) copy-start(f32[1,16,6,32]{3,1,0,2:T(8,128)S(1)} %get-tuple-element.205) | copy-start | bytes 36868
  81.9 11.2 %copy-start.85 = (f32[1,64,32]{2,1,0:T(8,128)S(1)}, f32[1,64,32]{2,1,0:T(8,128)}, u32[]{:S(2)}) copy-start(f32[1,64,32]{2,1,0:T(8,128)} %get-tuple-element.333) | copy-start | bytes 24580
  81.9 11.3 %copy-start.84 = (f32[1,64,32]{2,1,0:T(8,128)S(1)}, f32[1,64,32]{2,1,0:T(8,128)}, u32[]{:S(2)}) copy-start(f32[1,64,32]{2,1,0:T(8,128)} %get-tuple-element.334) | copy-start | bytes 24580
  82.0 11.6 %copy-start.51 = (f32[1,64,32]{2,1,0:T(8,128)S(1)}, f32[1,64,32]{2,1,0:T(8,128)}, u32[]{:S(2)}) copy-start(f32[1,64,32]{2,1,0:T(8,128)} %unstack.425) | copy-start | bytes 24580
  82.0 11.6 %copy-start.52 = (f32[1,64,32]{2,1,0:T(8,128)S(1)}, f32[1,64,32]{2,1,0:T(8,128)}, u32[]{:S(2)}) copy-start(f32[1,64,32]{2,1,0:T(8,128)} %unstack.427) | copy-start | bytes 24580
  82.0 11.6 %copy-start.53 = (f32[1,64,32]{2,1,0:T(8,128)S(1)}, f32[1,64,32]{2,1,0:T(8,128)}, u32[]{:S(2)}) copy-start(f32[1,64,32]{2,1,0:T(8,128)} %unstack.429) | copy-start | bytes 24580
  82.0 11.6 %copy-start.54 = (f32[1,64,32]{2,1,0:T(8,128)S(1)}, f32[1,64,32]{2,1,0:T(8,128)}, u32[]{:S(2)}) copy-start(f32[1,64,32]{2,1,0:T(8,128)} %unstack.431) | copy-start | bytes 24580
  82.0 11.6 %copy-start.55 = (f32[1,64,32]{2,1,0:T(8,128)S(1)}, f32[1,64,32]{2,1,0:T(8,128)}, u32[]{:S(2)}) copy-start(f32[1,64,32]{2,1,0:T(8,128)} %unstack.433) | copy-start | bytes 24580
  82.6 11.8 %copy-start.65 = (f32[1,64,32]{2,1,0:T(8,128)S(1)}, f32[1,64,32]{2,1,0:T(8,128)}, u32[]{:S(2)}) copy-start(f32[1,64,32]{2,1,0:T(8,128)} %get-tuple-element.330) | copy-start | bytes 24580
  82.6 11.9 %copy-start.63 = (f32[1,64,32]{2,1,0:T(8,128)S(1)}, f32[1,64,32]{2,1,0:T(8,128)}, u32[]{:S(2)}) copy-start(f32[1,64,32]{2,1,0:T(8,128)} %get-tuple-element.338) | copy-start | bytes 24580
  82.6 11.9 %copy-start.62 = (f32[1,64,32]{2,1,0:T(8,128)S(1)}, f32[1,64,32]{2,1,0:T(8,128)}, u32[]{:S(2)}) copy-start(f32[1,64,32]{2,1,0:T(8,128)} %get-tuple-element.337) | copy-start | bytes 24580
  82.6 12.0 %copy-start.64 = (f32[1,64,32]{2,1,0:T(8,128)S(1)}, f32[1,64,32]{2,1,0:T(8,128)}, u32[]{:S(2)}) copy-start(f32[1,64,32]{2,1,0:T(8,128)} %get-tuple-element.331) | copy-start | bytes 24580
  83.3 11.4 %copy-start.23 = (f32[1,16,6,32]{3,1,0,2:T(8,128)S(1)}, f32[1,16,6,32]{3,1,0,2:T(8,128)}, u32[]{:S(2)}) copy-start(f32[1,16,6,32]{3,1,0,2:T(8,128)} %get-tuple-element.179) | copy-start | bytes 36868
  83.3 11.4 %copy-start.96 = (f32[6]{0:T(128)S(1)}, f32[6]{0:T(128)}, u32[]{:S(2)}) copy-start(f32[6]{0:T(128)} %constant.434.clone) | copy-start | bytes 76
  83.3 11.4 %copy-start.102 = (f32[6]{0:T(128)S(1)}, f32[6]{0:T(128)}, u32[]{:S(2)}) copy-start(f32[6]{0:T(128)} %constant.432.clone) | copy-start | bytes 76
  83.3 11.4 %copy-start.108 = (f32[6]{0:T(128)S(1)}, f32[6]{0:T(128)}, u32[]{:S(2)}) copy-start(f32[6]{0:T(128)} %constant.433.clone) | copy-start | bytes 76
  83.3 13.7 %all-to-all-start.1 = ((bf16[3,8,1280]{2,0,1:T(4,128)(2,1)}), bf16[3,8,1280]{2,0,1:T(4,128)(2,1)S(1)}, u32[]{:S(2)}, u32[]{:S(2)}) async-start(bf16[3,8,1280]{2,0,1:T(4,128)(2,1)} %copy.1414), calls=%async_computation.1 | async-start | bytes 163840 | tf_op jit(solution)/shard_map/all_to_all | solution.py:180
  93.6 11.4 %copy-start.32 = (f32[1,16,192]{2,1,0:T(8,128)S(1)}, f32[1,16,192]{2,1,0:T(8,128)}, u32[]{:S(2)}) copy-start(f32[1,16,192]{2,1,0:T(8,128)} %copy-done.31) | copy-start | bytes 36868
  93.6 12.1 %copy-start.30 = (f32[1,16,192]{2,1,0:T(8,128)S(1)}, f32[1,16,192]{2,1,0:T(8,128)}, u32[]{:S(2)}) copy-start(f32[1,16,192]{2,1,0:T(8,128)} %copy-done.29) | copy-start | bytes 36868
  94.3 12.1 %copy-start.28 = (f32[1,16,192]{2,1,0:T(8,128)S(1)}, f32[1,16,192]{2,1,0:T(8,128)}, u32[]{:S(2)}) copy-start(f32[1,16,192]{2,1,0:T(8,128)} %copy-done.27) | copy-start | bytes 36868
  94.9 13.1 %copy-start.113 = (f32[1,16,192]{2,1,0:T(8,128)S(1)}, f32[1,16,192]{2,1,0:T(8,128)}, u32[]{:S(2)}) copy-start(f32[1,16,192]{2,1,0:T(8,128)} %get-tuple-element.360) | copy-start | bytes 36868
  94.9 13.7 %copy-start.112 = (f32[1,16,192]{2,1,0:T(8,128)S(1)}, f32[1,16,192]{2,1,0:T(8,128)}, u32[]{:S(2)}) copy-start(f32[1,16,192]{2,1,0:T(8,128)} %get-tuple-element.361) | copy-start | bytes 36868
  97.1 14.6 %collective-permute-start.2 = (bf16[1,8,1280]{2,1,0:T(8,128)(2,1)S(1)}, bf16[1,8,1280]{2,1,0:T(8,128)(2,1)S(1)}, u32[]{:S(2)}, u32[]{:S(2)}) collective-permute-start(bf16[1,8,1280]{2,1,0:T(8,128)(2,1)S(1)} %copy.1583), channel_id=1, source_target_pairs={{0,760},{8,0},{16,8},{24,16},{32,24},{40,32},{48,40},{56,48},{64,5... | collective-permute-start | bytes 61448 | tf_op jit(solution)/shard_map/ppermute | solution.py:25
  102.7 9.1 %collective-permute-start.3 = (bf16[1,8,1280]{2,1,0:T(8,128)(2,1)S(1)}, bf16[1,8,1280]{2,1,0:T(8,128)(2,1)S(1)}, u32[]{:S(2)}, u32[]{:S(2)}) collective-permute-start(bf16[1,8,1280]{2,1,0:T(8,128)(2,1)S(1)} %copy.1585), channel_id=1, source_target_pairs={{0,8},{8,16},{16,24},{24,32},{32,40},{40,48},{48,56},{56,64},{64,7... | collective-permute-start | bytes 61448 | tf_op jit(solution)/shard_map/ppermute | solution.py:25
  153.9 11.4 %collective-permute-start.4 = (bf16[1,8,1280]{2,1,0:T(8,128)(2,1)S(1)}, bf16[1,8,1280]{2,1,0:T(8,128)(2,1)S(1)}, u32[]{:S(2)}, u32[]{:S(2)}) collective-permute-start(bf16[1,8,1280]{2,1,0:T(8,128)(2,1)S(1)} %convert_element_type.92), channel_id=1, source_target_pairs={{0,8},{8,16},{16,24},{24,32},{32,40},{40,48},{48,56},{56,64},{64,7... | collective-permute-start | bytes 61448 | tf_op jit(solution)/shard_map/ppermute | solution.py:25
  156.3 9.1 %collective-permute-start.5 = (bf16[1,8,1280]{2,1,0:T(8,128)(2,1)S(1)}, bf16[1,8,1280]{2,1,0:T(8,128)(2,1)S(1)}, u32[]{:S(2)}, u32[]{:S(2)}) collective-permute-start(bf16[1,8,1280]{2,1,0:T(8,128)(2,1)S(1)} %convert_element_type.93), channel_id=1, source_target_pairs={{0,760},{8,0},{16,8},{24,16},{32,24},{40,32},{48,40},{56,48},{64,5... | collective-permute-start | bytes 61448 | tf_op jit(solution)/shard_map/ppermute | solution.py:25
  166.0 13.4 %all-to-all-start.2 = ((bf16[3,8,1280]{2,0,1:T(4,128)(2,1)}), bf16[3,8,1280]{2,0,1:T(4,128)(2,1)S(1)}, u32[]{:S(2)}, u32[]{:S(2)}) async-start(bf16[3,8,1280]{2,0,1:T(4,128)(2,1)} %copy.1481), calls=%async_computation.2 | async-start | bytes 163840 | tf_op jit(solution)/shard_map/all_to_all | solution.py:184
  224.7 11.4 %copy-start = (f32[5,4,4,6,32]{4,3,2,1,0:T(8,128)S(1)}, f32[5,4,4,6,32]{4,3,2,1,0:T(8,128)}, u32[]{:S(2)}) copy-start(f32[5,4,4,6,32]{4,3,2,1,0:T(8,128)} %stack.251) | copy-start | bytes 184324
  224.7 11.4 %copy-start.1 = (f32[5,4,4,6,32]{4,3,2,1,0:T(8,128)S(1)}, f32[5,4,4,6,32]{4,3,2,1,0:T(8,128)}, u32[]{:S(2)}) copy-start(f32[5,4,4,6,32]{4,3,2,1,0:T(8,128)} %reshape.2131) | copy-start | bytes 184324
  224.7 11.4 %copy-start.8 = (f32[5,4,4,6,32]{4,3,2,1,0:T(8,128)S(1)}, f32[5,4,4,6,32]{4,3,2,1,0:T(8,128)}, u32[]{:S(2)}) copy-start(f32[5,4,4,6,32]{4,3,2,1,0:T(8,128)} %copy-done.7) | copy-start | bytes 184324
  225.9 16.6 %collective-permute-start.6 = (bf16[1,8,1280]{2,1,0:T(8,128)(2,1)}, bf16[1,8,1280]{2,1,0:T(8,128)(2,1)}, u32[]{:S(2)}, u32[]{:S(2)}) collective-permute-start(bf16[1,8,1280]{2,1,0:T(8,128)(2,1)} %convert_element_type.94), channel_id=1, source_target_pairs={{0,8},{8,16},{16,24},{24,32},{32,40},{40,48},{48,56},{56,64},{64,7... | collective-permute-start | bytes 61448 | tf_op jit(solution)/shard_map/ppermute | solution.py:25
  228.9 13.7 %collective-permute-start.7 = (bf16[1,8,1280]{2,1,0:T(8,128)(2,1)}, bf16[1,8,1280]{2,1,0:T(8,128)(2,1)}, u32[]{:S(2)}, u32[]{:S(2)}) collective-permute-start(bf16[1,8,1280]{2,1,0:T(8,128)(2,1)} %convert_element_type.95), channel_id=1, source_target_pairs={{0,760},{8,0},{16,8},{24,16},{32,24},{40,32},{48,40},{56,48},{64,5... | collective-permute-start | bytes 61448 | tf_op jit(solution)/shard_map/ppermute | solution.py:25
  244.0 11.4 %all-to-all-start.3 = ((bf16[3,8,1280]{2,0,1:T(4,128)(2,1)}), bf16[3,8,1280]{2,0,1:T(4,128)(2,1)S(1)}, u32[]{:S(2)}, u32[]{:S(2)}) async-start(bf16[3,8,1280]{2,0,1:T(4,128)(2,1)} %copy.1542), calls=%async_computation.3 | async-start | bytes 163840 | tf_op jit(solution)/shard_map/all_to_all | solution.py:184
  (97 other events, 341.2 us)
where the time goes:
time: 278 us; the launch traced here: 273 us
  local copies, waits for them, and re-layouts  96.1 us (35%)
  other arithmetic  87.3 us (31%)
  starting transfers between devices  67.4 us (24%)
  waiting for transfers between devices  16 us (6%)
  between operations  4.45 us (2%)
    scatter-add x2, other arithmetic, residual(): exterior = jnp.take(lookup.reshape(5, -1), gather_index, axis=1)  38.9 us
    ppermute x8, starting transfers between devices, from_behind(): return lax.ppermute(value, axis, pairs)  37.4 us
    scatter-add x2, other arithmetic, pack_sends(): picked = jnp.take(padded, slots, axis=2)  29.2 us
    gather x4, local copies, waits for them, and re-layouts, residual(): exterior = jnp.take(lookup.reshape(5, -1), gather_index, axis=1)  22.2 us
    all_to_all x2, starting transfers between devices, sub_forward(): lax.all_to_all(buffer, 'sub', split_axis=1, concat_axis=1, tiled=True)  19.3 us
    another operation x93, local copies, waits for them, and re-layouts, flux_along(): return jnp.stack(components)  14.7 us
    all_to_all x2, waiting for transfers between devices, sub_backward(): lax.all_to_all(as_sent(buffer), 'sub', split_axis=1, concat_axis=1, tiled...  12.4 us
    all_to_all x2, starting transfers between devices, sub_backward(): lax.all_to_all(as_sent(buffer), 'sub', split_axis=1, concat_axis=1, tiled...  10.7 us
  transfers between devices with their start and end apart: 12, of which 4 were waited for; matrix products, arithmetic and copies ran while one was open for 15% of the time, Pallas kernels for 0%

commit v1 on v0

v1 whole, which is shorter than its diff:
```python
import jax
import jax.numpy as jnp
import numpy as np
import ml_dtypes
from jax import lax
from jax.experimental import pallas as pl
from jax.experimental.pallas import tpu as pltpu
from jax.sharding import PartitionSpec as P

step_size = 0.02
mean_flow = 0.3
lift_factor = 12.0

E = 32
F = 192
S = 384
G = 128
f32 = jnp.float32
bf16 = jnp.bfloat16
i32 = jnp.int32


def derivative_table():
    points = np.array([-1.0, -1.0 / np.sqrt(5.0), 1.0 / np.sqrt(5.0), 1.0])
    products = np.array(
        [np.prod([points[t] - points[s] for s in range(4) if s != t]) for t in range(4)]
    )
    result = np.zeros((4, 4))
    for t in range(4):
        for s in range(4):
            if t != s:
                result[t, s] = products[t] / (products[s] * (points[t] - points[s]))
        result[t, t] = -np.sum(result[t])
    return result.astype(np.float32)


def halves_of(matrix):
    hi = matrix.astype(ml_dtypes.bfloat16)
    lo = (matrix - hi.astype(np.float32)).astype(ml_dtypes.bfloat16)
    return hi, lo


def derivative_operands():
    d = -2.0 * derivative_table()
    eye = np.eye(4, dtype=np.float32)
    along = [
        np.kron(d, np.kron(eye, eye)),
        np.kron(eye, np.kron(d, eye)),
        np.kron(eye, np.kron(eye, d)),
    ]
    two = [np.kron(np.eye(2, dtype=np.float32), a).astype(np.float32) for a in along]
    hi, lo = halves_of(np.concatenate([t.T for t in two], axis=0))
    forward = np.concatenate([hi, lo], axis=1)
    hi, lo = halves_of(np.concatenate(two, axis=1))
    backward = np.concatenate([hi, lo], axis=1)
    return forward, backward


def lanes(rows):
    return lax.broadcasted_iota(i32, (rows, 128), 1)


def take(x, index):
    return jnp.take_along_axis(x, index, axis=1)


def turn(x, shift):
    return pltpu.roll(x, shift, 1)


def halves(x):
    hi = x.astype(bf16)
    lo = (x - hi.astype(f32)).astype(bf16)
    return hi, lo


def dot(a, b):
    return jnp.dot(a, b, preferred_element_type=f32)


def select_rows(onehot, x):
    hi, lo = halves(x)
    r = dot(onehot, jnp.concatenate([hi, lo], axis=1))
    return r[:, :128] + r[:, 128:]


def to_tiles(ref):
    zero = jnp.zeros((64, E), f32)
    tiles = []
    for j in range(3):
        low = ref[2 * j]
        high = ref[2 * j + 1] if j < 2 else zero
        tiles.append(jnp.transpose(jnp.concatenate([low, high], axis=0)))
    return tiles


def from_tiles(tiles, ref):
    for j in range(3):
        t = jnp.transpose(tiles[j])
        ref[2 * j] = t[:64]
        if j < 2:
            ref[2 * j + 1] = t[64:]


def load_tiles(ref):
    return [ref[:, 128 * j : 128 * (j + 1)] for j in range(3)]


def store_tiles(ref, tiles):
    for j in range(3):
        ref[:, 128 * j : 128 * (j + 1)] = tiles[j]


def spread(tiles):
    low = lanes(E) < 64
    back0, back1, back2 = turn(tiles[0], 64), turn(tiles[1], 64), turn(tiles[2], 64)
    ux = jnp.where(low, back0, tiles[0])
    uy = jnp.where(low, tiles[1], back1)
    uz = jnp.where(low, back1, tiles[1])
    p = tiles[2] + back2
    return low, (ux, uy, uz), p


def volume(tiles, table):
    low, speeds, p = spread(tiles)
    fluxes = []
    for a in range(3):
        u = speeds[a]
        c = u + mean_flow if a == 0 else u
        high0 = p if a == 0 else jnp.zeros_like(p)
        parts = [c * tiles[0] + jnp.where(low, u, high0), c * tiles[1], c * tiles[2] + jnp.where(low, u, 0.0)]
        if a == 1:
            parts[1] = parts[1] + jnp.where(low, p, 0.0)
        if a == 2:
            parts[1] = parts[1] + jnp.where(low, 0.0, p)
        fluxes.append(jnp.concatenate(parts, axis=0))
    hi, lo = halves(jnp.concatenate(fluxes, axis=1))
    r = dot(jnp.concatenate([hi, lo], axis=0), table)
    out = r[:96, :128] + (r[:96, 128:] + r[96:, :128])
    return [out[:32], out[32:64], out[64:96]]


def derivative_back(tiles, table):
    hi, lo = halves(jnp.concatenate(tiles, axis=0))
    r = dot(jnp.concatenate([hi, lo], axis=0), table)
    return r[:96, :384] + (r[:96, 384:] + r[96:, :384])


def volume_back(tiles, z):
    low, speeds, _ = spread(tiles)
    one = jnp.where(low, 1.0, 0.0).astype(f32)
    plus = [tiles[0] + one, tiles[1], tiles[2] + one]
    out = [jnp.zeros((E, 128), f32) for _ in range(3)]
    sums = []
    parts = []
    for a in range(3):
        c = speeds[a] + mean_flow if a == 0 else speeds[a]
        za = [z[32 * j : 32 * (j + 1), 128 * a : 128 * (a + 1)] for j in range(3)]
        total = plus[0] * za[0] + plus[1] * za[1] + plus[2] * za[2]
        sums.append(total + turn(total, 64))
        parts.append(za)
        out = [out[j] + c * za[j] for j in range(3)]
    pressure = turn(parts[0][0], 64) + parts[1][1] + turn(parts[2][1], 64)
    out[0] = out[0] + jnp.where(low, 0.0, sums[0])
    out[1] = out[1] + jnp.where(low, sums[1], sums[2])
    out[2] = out[2] + jnp.where(low, pressure, 0.0)
    return out


def traces(tiles):
    lane = lanes(E)
    m = lane & 15
    r, s = m >> 2, m & 3
    base = ((lane >> 4) & 1) * 64
    rows = []
    for f in range(6):
        b = f % 2
        node = (48 * b + m, 16 * r + 12 * b + s, 4 * m + 3 * b)[f // 2]
        index = base + node
        t = jnp.where(
            lane < 32,
            take(tiles[0], index),
            jnp.where(lane < 64, take(tiles[1], index), take(tiles[2], index)),
        )
        rows.append(jnp.where(lane < 80, t, 0.0))
    return jnp.concatenate(rows, axis=0)


def lifted(x):
    lane = lanes(E)
    n = lane & 63
    i, j, k = n >> 4, (n >> 2) & 3, n & 3
    grid = ((i, 4 * j + k), (j, 4 * i + k), (k, 4 * i + j))
    tiles = []
    for tile in range(3):
        v = 2 * tile + (lane >> 6)
        total = jnp.zeros((E, 128), f32)
        for a in range(3):
            layer, m = grid[a]
            index = v * 16 + m
            first = take(x[64 * a : 64 * a + 32], index)
            last = take(x[64 * a + 32 : 64 * a + 64], index)
            total = total + jnp.where(layer == 0, first, jnp.where(layer == 3, last, 0.0))
        tiles.append(total)
    return tiles


class Faces:
    def __init__(self):
        row = lax.broadcasted_iota(i32, (F, 128), 0)
        lane = lanes(F)
        self.v = lane >> 4
        m = lane & 15
        axis = row >> 6
        self.sign = jnp.where((row >> 5) & 1 == 1, 1.0, -1.0).astype(f32)
        self.drift = jnp.where(axis == 0, mean_flow, 0.0).astype(f32)
        self.normal = self.v == axis + 1
        self.normal_index = (axis + 1) * 16 + m
        self.pressure_index = 64 + m
        self.m = m
        self.ends = (self.v == 0) | (self.v == 4)
        self.ones = jnp.where(self.ends, 1.0, 0.0).astype(f32)
        self.axis = axis

    def flux(self, x):
        u = take(x, self.normal_index)
        p = take(x, self.pressure_index)
        return self.sign * (
            (self.drift + u) * x + jnp.where(self.ends, u, 0.0) + jnp.where(self.normal, p, 0.0)
        )

    def flux_back(self, x, w):
        u = take(x, self.normal_index)
        n = take(w, self.normal_index)
        h = over_fields((x + self.ones) * w)
        return self.sign * (
            (self.drift + u) * w + jnp.where(self.v == 4, n, 0.0) + jnp.where(self.normal, h, 0.0)
        )

    def flux_back_along(self, a, x, w):
        index = (a + 1) * 16 + self.m
        u = take(x, index)
        n = take(w, index)
        h = over_fields((x + self.ones) * w)
        c = u + mean_flow if a == 0 else u
        return c * w + jnp.where(self.v == 4, n, 0.0) + jnp.where(self.v == a + 1, h, 0.0)

    def mirror(self, x):
        return jnp.where(self.normal, -x, x)


def over_fields(h):
    h = h + turn(h, 16)
    h = h + turn(h, 32)
    return h + turn(h, 64)


def column_of(table_ref):
    x = table_ref[...].astype(f32)
    x = jnp.concatenate([x, jnp.zeros((2, E), f32)], axis=0)
    t = jnp.transpose(x)
    return jnp.concatenate([t[:, f : f + 1] for f in range(6)], axis=0).astype(i32)


def row_of(table_ref):
    return jnp.concatenate([table_ref[f : f + 1, :] for f in range(6)], axis=1)


def slot_column(send_ref):
    x = jnp.broadcast_to(send_ref[...].astype(f32), (8, S))
    return jnp.transpose(x)[:, :1].astype(i32)


def onehot(rows, columns, first, second):
    return jnp.where(first == second, 1.0, 0.0).astype(bf16)


def faces_from_columns(ext_col):
    return onehot(F, F, ext_col, lax.broadcasted_iota(i32, (F, F), 1))


def columns_from_faces(ext_row):
    return onehot(F, F, ext_row, lax.broadcasted_iota(i32, (F, F), 0))


def faces_from_slots(ext_col):
    return onehot(F, S, ext_col - F, lax.broadcasted_iota(i32, (F, S), 1))


def slots_from_faces(ext_row):
    return onehot(S, F, ext_row - F, lax.broadcasted_iota(i32, (S, F), 0))


def slots_from_columns(send_col):
    return onehot(S, F, send_col, lax.broadcasted_iota(i32, (S, F), 1))


def columns_from_slots(send_row):
    return onehot(F, S, send_row, lax.broadcasted_iota(i32, (F, S), 0))


def orientation(perm_col):
    lane = lanes(F)
    m = lane & 15
    r, s = m >> 2, m & 3
    k = jnp.broadcast_to(perm_col, (F, 128))
    flip_r = (k & 1) == 1
    flip_s = (k & 2) == 2
    swap = (k & 4) == 4
    r1 = jnp.where(flip_r, 3 - r, r)
    s1 = jnp.where(flip_s, 3 - s, s)
    base = lane - m
    index = base + jnp.where(swap, 4 * s1 + r1, 4 * r1 + s1)
    r2 = jnp.where(swap, s, r)
    s2 = jnp.where(swap, r, s)
    r2 = jnp.where(flip_r, 3 - r2, r2)
    s2 = jnp.where(flip_s, 3 - s2, s2)
    inverse = base + 4 * r2 + s2
    return index, inverse


def packed(x):
    tail = lanes(F) >= 80
    first = jnp.where(tail, turn(x, 80), 0.0)
    second = jnp.where(tail, turn(x, 32), 0.0)
    return jnp.concatenate([first, second], axis=1).astype(bf16)


def unpacked(g):
    lane = lanes(F)
    first = jnp.where(lane < 48, turn(g[:, :128], 48), 0.0)
    second = jnp.where((lane >= 48) & (lane < 80), turn(g[:, 128:256], 96), 0.0)
    return first + second


def write_buffers(forward, back, refs):
    for o, ref in enumerate(refs):
        fw = forward[G * o : G * (o + 1)]
        bk = back[G * (2 - o) : G * (3 - o)]
        wide = bk.shape[1]
        ref[:, :256] = (fw + bk[:, :256]).astype(bf16) if wide > 128 else (fw + jnp.concatenate([bk, jnp.zeros_like(bk)], axis=1)).astype(bf16)
        if wide > 256:
            ref[:, 256:] = bk[:, 256:].astype(bf16)


def exterior(faces, wall, index, onehot_local, t):
    return jnp.where(wall, faces.mirror(t), take(select_rows(onehot_local, t), index))


def arrivals(z_ref):
    width = z_ref.shape[3]
    return [z_ref[:, o].reshape(G, width) for o in range(3)]


def pack_kernel(state_ref, final_ref, send_ref, ext_ref, perm_ref,
                minus_ref, own_ref, plus_ref, q_ref, w_ref, t_ref, lam_ref):
    faces = Faces()
    q = to_tiles(state_ref)
    w = to_tiles(final_ref)
    store_tiles(q_ref, q)
    store_tiles(w_ref, w)
    t = traces(q)
    lam = lift_factor * traces(w)
    t_ref[...] = t
    lam_ref[...] = lam
    _, inverse = orientation(column_of(perm_ref))
    y = take(lam, inverse)
    signed = faces.sign * y
    stack = [y] + [jnp.where(faces.axis == a, signed, 0.0) for a in range(3)]
    stack = jnp.concatenate([x.astype(bf16) for x in stack], axis=1)
    back = dot(slots_from_faces(row_of(ext_ref)), stack)
    forward = dot(slots_from_columns(slot_column(send_ref)), packed(t))
    write_buffers(forward, back, (minus_ref, own_ref, plus_ref))


def first_local_kernel(q_ref, w_ref, t_ref, ext_ref, perm_ref, forward_ref, backward_ref, base_ref, z_ref):
    faces = Faces()
    ext_col = column_of(ext_ref)
    index, _ = orientation(column_of(perm_ref))
    wall = jnp.broadcast_to(ext_col, (F, 128)) == F + S
    q = load_tiles(q_ref)
    t = t_ref[...]
    x = exterior(faces, wall, index, faces_from_columns(ext_col), t)
    jump = 0.5 * (faces.flux(t) - faces.flux(x)) + (x - t)
    faced = lifted(lift_factor * jump)
    inner = volume(q, forward_ref[...])
    store_tiles(base_ref, [q[j] + step_size * (inner[j] + faced[j]) for j in range(3)])
    z_ref[...] = derivative_back(load_tiles(w_ref), backward_ref[...])


def middle_kernel(base_ref, w_ref, t_lam_ref, z_ref, arrived_ref, send_ref, ext_ref, perm_ref,
                  minus_ref, own_ref, plus_ref, q1_ref, w1_ref, t1_ref, x1_ref, lam1_ref):
    faces = Faces()
    ext_col = column_of(ext_ref)
    ext_row = row_of(ext_ref)
    index, inverse = orientation(column_of(perm_ref))
    ext_wide = jnp.broadcast_to(ext_col, (F, 128))
    wall = ext_wide == F + S
    remote = (ext_wide >= F) & (ext_wide < F + S)
    from_plus, from_own, from_minus = arrivals(arrived_ref)
    incoming = jnp.concatenate([from_plus[:, :256], from_own[:, :256], from_minus[:, :256]], axis=0)
    xr = take(unpacked(dot(faces_from_slots(ext_col), incoming)), index)
    faced = lifted((lift_factor * step_size) * (xr - 0.5 * faces.flux(xr)))
    base = load_tiles(base_ref)
    q1 = [base[j] + faced[j] for j in range(3)]
    store_tiles(q1_ref, q1)
    t1 = traces(q1)
    t1_ref[...] = t1
    send_row = send_ref[...]
    forward = dot(slots_from_columns(slot_column(send_ref)), packed(t1))
    lam = t_lam_ref[...]
    x1 = exterior(faces, wall, index, faces_from_columns(ext_col), t1)
    x1_ref[...] = x1
    bar = jnp.where(remote, 0.0, lam - 0.5 * faces.flux_back(x1, lam))
    total = 0.5 * faces.flux_back(t1, lam) - lam + jnp.where(wall, faces.mirror(bar), 0.0)
    total = total + select_rows(columns_from_faces(ext_row), take(bar, inverse))
    returned = jnp.concatenate([from_minus, from_own, from_plus], axis=0)
    sums = dot(columns_from_slots(send_row), returned)
    valid = lanes(F) < 80
    sums = [jnp.where(valid, sums[:, 128 * a : 128 * (a + 1)], 0.0) for a in range(4)]
    t1_sent = t1.astype(bf16).astype(f32)
    through = [faces.flux_back_along(a, t1_sent, sums[a + 1]) for a in range(3)]
    total = total + sums[0] - 0.5 * (through[0] + through[1] + through[2])
    inner = volume_back(q1, z_ref[...])
    faced = lifted(total)
    w = load_tiles(w_ref)
    w1 = [0.5 * w[j] + (0.5 * step_size) * (inner[j] + faced[j]) for j in range(3)]
    store_tiles(w1_ref, w1)
    lam1 = lift_factor * traces(w1)
    lam1_ref[...] = lam1
    y = take(lam1 - 0.5 * faces.flux_back(xr, lam1), inverse)
    back = dot(slots_from_faces(ext_row), y.astype(bf16))
    write_buffers(forward, back, (minus_ref, own_ref, plus_ref))


def second_local_kernel(q_ref, w_ref, t_ref, q1_ref, w1_ref, t1_ref, x1_ref, lam1_ref, ext_ref, perm_ref,
                        forward_ref, backward_ref, end_ref, start_ref):
    faces = Faces()
    ext_col = column_of(ext_ref)
    index, inverse = orientation(column_of(perm_ref))
    ext_wide = jnp.broadcast_to(ext_col, (F, 128))
    wall = ext_wide == F + S
    remote = (ext_wide >= F) & (ext_wide < F + S)
    q = load_tiles(q_ref)
    q1 = load_tiles(q1_ref)
    t1 = t1_ref[...]
    x1 = x1_ref[...]
    jump = 0.5 * (faces.flux(t1) - faces.flux(x1)) + (x1 - t1)
    faced = lifted(lift_factor * jump)
    inner = volume(q1, forward_ref[...])
    store_tiles(end_ref, [0.5 * q[j] + 0.5 * (q1[j] + step_size * (inner[j] + faced[j])) for j in range(3)])
    t = t_ref[...]
    lam1 = lam1_ref[...]
    x = exterior(faces, wall, index, faces_from_columns(ext_col), t)
    bar = jnp.where(remote, 0.0, lam1 - 0.5 * faces.flux_back(x, lam1))
    total = 0.5 * faces.flux_back(t, lam1) - lam1 + jnp.where(wall, faces.mirror(bar), 0.0)
    total = total + select_rows(columns_from_faces(row_of(ext_ref)), take(bar, inverse))
    w = load_tiles(w_ref)
    w1 = load_tiles(w1_ref)
    inner = volume_back(q, derivative_back(w1, backward_ref[...]))
    faced = lifted(total)
    store_tiles(start_ref, [0.5 * w[j] + w1[j] + step_size * (inner[j] + faced[j]) for j in range(3)])


def last_kernel(end_base_ref, start_base_ref, arrived_ref, send_ref, ext_ref, perm_ref, end_ref, start_ref):
    faces = Faces()
    index, _ = orientation(column_of(perm_ref))
    from_plus, from_own, from_minus = arrivals(arrived_ref)
    incoming = jnp.concatenate([from_plus, from_own, from_minus], axis=0)
    returned = jnp.concatenate([from_minus[:, :128], from_own[:, :128], from_plus[:, :128]], axis=0)
    xr = take(unpacked(dot(faces_from_slots(column_of(ext_ref)), incoming)), index)
    faced = lifted((0.5 * step_size * lift_factor) * (xr - 0.5 * faces.flux(xr)))
    base = load_tiles(end_base_ref)
    from_tiles([base[j] + faced[j] for j in range(3)], end_ref)
    bar = dot(columns_from_slots(send_ref[...]), returned)
    bar = jnp.where(lanes(F) < 80, bar, 0.0)
    faced = lifted(step_size * bar)
    base = load_tiles(start_base_ref)
    from_tiles([base[j] + faced[j] for j in range(3)], start_ref)


def shape(*dims, dtype=f32):
    return jax.ShapeDtypeStruct(dims, dtype)


def call(kernel, outs, *args):
    return pl.pallas_call(
        kernel,
        out_shape=outs,
        cost_estimate=pl.CostEstimate(flops=200_000_000, bytes_accessed=1_000_000, transcendentals=0),
        compiler_params=pltpu.CompilerParams(vmem_limit_bytes=32 * 1024 * 1024),
    )(*args)


def exchange(to_minus, to_own, to_plus):
    count = lax.axis_size("dom")
    width = to_own.shape[1]

    def moved(value, steps):
        pairs = [(source, (source + steps) % count) for source in range(count)]
        return lax.ppermute(value, "dom", pairs)

    pieces = [moved(to_minus, -1), to_own, moved(to_plus, 1)]
    whole = jnp.stack([x.reshape(8, 16, width) for x in pieces], axis=1)
    return lax.all_to_all(whole, "sub", split_axis=0, concat_axis=0, tiled=True)


def shards(state, adjoint_final, send_slot, ext_index, ext_perm):
    forward, backward = derivative_operands()
    forward, backward = jnp.asarray(forward), jnp.asarray(backward)
    node = shape(E, 384)
    face = shape(F, 128)
    wide = shape(G, 512, dtype=bf16)
    slim = shape(G, 256, dtype=bf16)

    *buffers, q, w, t, lam = call(
        pack_kernel, (wide, wide, wide, node, node, face, face),
        state, adjoint_final, send_slot, ext_index, ext_perm)
    arrived = exchange(*buffers)
    base, z = call(first_local_kernel, (node, shape(96, 384)), q, w, t, ext_index, ext_perm, forward, backward)
    *buffers, q1, w1, t1, x1, lam1 = call(
        middle_kernel, (slim, slim, slim, node, node, face, face, face),
        base, w, lam, z, arrived, send_slot, ext_index, ext_perm)
    arrived = exchange(*buffers)
    end_base, start_base = call(
        second_local_kernel, (node, node),
        q, w, t, q1, w1, t1, x1, lam1, ext_index, ext_perm, forward, backward)
    out = shape(5, 64, E)
    return tuple(call(
        last_kernel, (out, out), end_base, start_base, arrived, send_slot, ext_index, ext_perm))


def solution(mesh):
    return jax.shard_map(
        shards,
        mesh=mesh,
        in_specs=(
            P(None, None, ("dom", "sub")),
            P(None, None, ("dom", "sub")),
            P(("dom", "sub"), None),
            P(None, ("dom", "sub")),
            P(None, ("dom", "sub")),
        ),
        out_specs=(P(None, None, ("dom", "sub")), P(None, None, ("dom", "sub"))),
        check_vma=False,
    )
```

time: 278 us -> 80.4 us (0.29); the launches traced: 273 us -> 79.9 us
  local copies, waits for them, and re-layouts: 96.1 us -> 3.22 us
  other arithmetic: 87.3 us -> 1.51 us
  starting transfers between devices: 67.4 us -> 35.3 us
  waiting for transfers between devices: 16 us -> 30.8 us
  Pallas kernels: 0 us -> 8.36 us
  between operations: 4.45 us -> 0.75 us
    scatter-add x8 -> x0, other arithmetic: 68.2 us -> none  [the longest x2 38.9 us: residual(): exterior = jnp.take(lookup.reshape(5, -1), gather_index, axis=1)]
    gather x12 -> x0, local copies, waits for them, and re-layouts: 26.1 us -> none  [the longest x4 22.2 us: residual(): exterior = jnp.take(lookup.reshape(5, -1), gather_index, axis=1)]
    another operation x122 -> x0, local copies, waits for them, and re-layouts: 19.4 us -> none  [the longest x93 14.7 us: flux_along(): return jnp.stack(components)]
    all_to_all x4 -> x2, starting transfers between devices: 30 us -> 12.4 us  [exchange(): return lax.all_to_all(whole, 'sub', split_axis=0, concat_axis=0, tiled=True)]
    ppermute x8 -> x4, waiting for transfers between devices: 0.02 us -> 14.6 us  [moved(): return lax.ppermute(value, 'dom', pairs)]
    ppermute x8 -> x4, starting transfers between devices: 37.4 us -> 22.9 us  [moved(): return lax.ppermute(value, 'dom', pairs)]
    scatter-add x10 -> x0, local copies, waits for them, and re-layouts: 13.5 us -> none  [the longest x2 7.05 us: residual(): exterior = jnp.take(lookup.reshape(5, -1), gather_index, axis=1)]
    reshape x21 -> x0, local copies, waits for them, and re-layouts: 11 us -> none  [the longest x6 7.37 us: residual(): exterior = jnp.take(lookup.reshape(5, -1), gather_index, axis=1)]
  transfers between devices with their start and end apart: 12 -> 6, of which waited for: 4 -> 5; matrix products, arithmetic and copies ran while one was open for 15% -> 0% of each run, Pallas kernels for 0% -> 3%
where the time goes in v1:
time: 80.4 us; the launch traced here: 79.9 us
  starting transfers between devices  35.3 us (44%)
  waiting for transfers between devices  30.8 us (38%)
  Pallas kernels  8.36 us (10%)
  local copies, waits for them, and re-layouts  3.22 us (4%)
  other arithmetic  1.51 us (2%)
    ppermute x4, starting transfers between devices, moved(): return lax.ppermute(value, 'dom', pairs)  22.9 us
    all_to_all x2, waiting for transfers between devices, exchange(): return lax.all_to_all(whole, 'sub', split_axis=0, concat_axis=0, tiled=True)  16.2 us
    ppermute x4, waiting for transfers between devices, moved(): return lax.ppermute(value, 'dom', pairs)  14.6 us
    all_to_all x2, starting transfers between devices, exchange(): return lax.all_to_all(whole, 'sub', split_axis=0, concat_axis=0, tiled=True)  12.4 us
    pallas_call x5, Pallas kernels, call(): pl.pallas_call(kernel, out_shape=outs, cost_estimate=pl.CostEstimate(flop...  8.36 us
    unnamed x14, local copies, waits for them, and re-layouts  1.73 us
  transfers between devices with their start and end apart: 6, of which 5 were waited for; matrix products, arithmetic and copies ran while one was open for 0% of the time, Pallas kernels for 3%

profile of v1, /device:TPU:8, one launch (start us, length us, event | category | flops | bytes accessed | tf_op | source)
XLA Modules:
  0.0 79.9 jit_solution(14088129438717592336)
XLA Ops:
  0.6 0.0 copy-start.5
  0.6 1.0 %copy.9.state_ref = f32[5,64,32]{2,1,0:T(8,128)S(1)} copy(f32[5,64,32]{1,2,0:T(8,128)} %param.7) | data formatting | bytes 81920 | tf_op args[0]
  1.7 0.0 copy-done.5
  1.7 0.0 copy-start.2
  1.7 0.0 copy-start.3
  1.7 0.0 copy-start.4
  1.7 0.1 copy.10.final_ref
  1.8 0.5 copy-done.2
  2.4 0.0 copy-done.3
  2.4 0.0 copy-done.4
  2.4 1.0 %shard_map.86 = (bf16[128,512]{1,0:T(8,128)(2,1)S(1)}, bf16[128,512]{1,0:T(8,128)(2,1)S(1)}, bf16[128,512]{1,0:T(8,128)(2,1)S(1)}, f32[32,384]{1,0:T(8,128)S(1)}...) custom-call(f32[5,64,32]{2,1,0:T(8,128)S(1)} %copy.9.state_ref, ...), custom_call_target="tpu_custom_call" | custom-call | flops 200000000 | bytes 1000000 | tf_op jit(solution)/shard_map/pallas_call | solution.py:487
  3.4 16.2 %collective-permute-start = (bf16[128,512]{1,0:T(8,128)(2,1)S(1)}, bf16[128,512]{1,0:T(8,128)(2,1)S(1)}, u32[]{:S(2)}, u32[]{:S(2)}) collective-permute-start(bf16[128,512]{1,0:T(8,128)(2,1)S(1)} %get-tuple-element.27), channel_id=1, source_target_pairs={{0,760},{8,0},{16,8},{24,16},{32,24},{40,32},{48,40},{56,48},{64,5... | collective-permute-start | bytes 393224 | tf_op jit(solution)/shard_map/ppermute | solution.py:501
  19.6 1.9 %collective-permute-start.1 = (bf16[128,512]{1,0:T(8,128)(2,1)S(1)}, bf16[128,512]{1,0:T(8,128)(2,1)S(1)}, u32[]{:S(2)}, u32[]{:S(2)}) collective-permute-start(bf16[128,512]{1,0:T(8,128)(2,1)S(1)} %get-tuple-element.29), channel_id=1, source_target_pairs={{0,8},{8,16},{16,24},{24,32},{32,40},{40,48},{48,56},{56,64},{64,7... | collective-permute-start | bytes 393224 | tf_op jit(solution)/shard_map/ppermute | solution.py:501
  21.5 0.6 collective-permute-done
  22.1 7.1 %collective-permute-done.1 = bf16[128,512]{1,0:T(8,128)(2,1)S(1)} collective-permute-done((bf16[128,512]{1,0:T(8,128)(2,1)S(1)}, bf16[128,512]{1,0:T(8,128)(2,1)S(1)}, u32[]{:S(2)}, u32[]{:S(2)}) %collective-permute-start.1) | collective-permute-done | bytes 131104 | tf_op jit(solution)/shard_map/ppermute | solution.py:501
  29.2 0.8 pad_maximum_fusion
  30.0 0.0 copy-start
  30.0 0.0 copy-start.1
  30.0 7.7 %all-to-all-start = ((bf16[8,3,16,512]{3,2,1,0:T(8,128)(2,1)}), bf16[8,3,16,512]{3,2,1,0:T(8,128)(2,1)S(1)}, u32[]{:S(2)}, u32[]{:S(2)}) async-start(bf16[8,3,16,512]{3,2,1,0:T(8,128)(2,1)} %pad_maximum_fusion), calls=%async_computation | async-start | bytes 786432 | tf_op jit(solution)/shard_map/all_to_all | solution.py:505
  37.7 0.0 copy-done
  37.7 0.0 copy-done.1
  37.7 0.8 %shard_map.87 = (f32[32,384]{1,0:T(8,128)S(1)}, f32[96,384]{1,0:T(8,128)S(1)}) custom-call(f32[32,384]{1,0:T(8,128)S(1)} %get-tuple-element.21.q_ref, f32[32,384]{1,0:T(8,128)S(1)} %get-tuple-element.22.w_ref, f32[192,128]{1,0:T(8,128)S(1)} %get-tuple-element.23.t_ref, s32[6,32]{1,0:T(8,128)S(1)} %copy-done.2, s32[6,32]{1,0:T(8,128)S(1)} %copy-done.3, ...), custom_call_target="tpu_custom_call" | custom-call | flops 200000000 | bytes 1000000 | tf_op jit(solution)/shard_map/pallas_call | solution.py:487
  38.5 9.6 %all-to-all-done.arrived_ref = bf16[8,3,16,512]{3,2,1,0:T(8,128)(2,1)S(1)} async-done(((bf16[8,3,16,512]{3,2,1,0:T(8,128)(2,1)}), bf16[8,3,16,512]{3,2,1,0:T(8,128)(2,1)S(1)}, u32[]{:S(2)}, u32[]{:S(2)}) %all-to-all-start) | async-done | bytes 393248 | tf_op jit(solution)/shard_map/all_to_all | solution.py:505
  48.1 3.6 %shard_map.88 = (bf16[128,256]{1,0:T(8,128)(2,1)S(1)}, bf16[128,256]{1,0:T(8,128)(2,1)S(1)}, bf16[128,256]{1,0:T(8,128)(2,1)S(1)}, f32[32,384]{1,0:T(8,128)S(1)}...) custom-call(f32[32,384]{1,0:T(8,128)S(1)} %get-tuple-element.24.base_ref, ...), custom_call_target="tpu_custom_call" | custom-call | flops 200000000 | bytes 1000000 | tf_op jit(solution)/shard_map/pallas_call | solution.py:487
  51.7 2.8 %collective-permute-start.2 = (bf16[128,256]{1,0:T(8,128)(2,1)S(1)}, bf16[128,256]{1,0:T(8,128)(2,1)S(1)}, u32[]{:S(2)}, u32[]{:S(2)}) collective-permute-start(bf16[128,256]{1,0:T(8,128)(2,1)S(1)} %get-tuple-element.37), channel_id=1, source_target_pairs={{0,760},{8,0},{16,8},{24,16},{32,24},{40,32},{48,40},{56,48},{64,5... | collective-permute-start | bytes 196616 | tf_op jit(solution)/shard_map/ppermute | solution.py:501
  54.5 1.9 %collective-permute-start.3 = (bf16[128,256]{1,0:T(8,128)(2,1)S(1)}, bf16[128,256]{1,0:T(8,128)(2,1)S(1)}, u32[]{:S(2)}, u32[]{:S(2)}) collective-permute-start(bf16[128,256]{1,0:T(8,128)(2,1)S(1)} %get-tuple-element.39), channel_id=1, source_target_pairs={{0,8},{8,16},{16,24},{24,32},{32,40},{40,48},{48,56},{56,64},{64,7... | collective-permute-start | bytes 196616 | tf_op jit(solution)/shard_map/ppermute | solution.py:501
  56.4 0.0 collective-permute-done.2
  56.4 7.0 %collective-permute-done.3 = bf16[128,256]{1,0:T(8,128)(2,1)S(1)} collective-permute-done((bf16[128,256]{1,0:T(8,128)(2,1)S(1)}, bf16[128,256]{1,0:T(8,128)(2,1)S(1)}, u32[]{:S(2)}, u32[]{:S(2)}) %collective-permute-start.3) | collective-permute-done | bytes 65568 | tf_op jit(solution)/shard_map/ppermute | solution.py:501
  63.4 0.7 pad_maximum_fusion.1
  64.1 4.8 %all-to-all-start.1 = ((bf16[8,3,16,256]{3,2,1,0:T(8,128)(2,1)}), bf16[8,3,16,256]{3,2,1,0:T(8,128)(2,1)S(1)}, u32[]{:S(2)}, u32[]{:S(2)}) async-start(bf16[8,3,16,256]{3,2,1,0:T(8,128)(2,1)} %pad_maximum_fusion.1), calls=%async_computation.1 | async-start | bytes 393216 | tf_op jit(solution)/shard_map/all_to_all | solution.py:505
  68.9 1.8 %shard_map.89 = (f32[32,384]{1,0:T(8,128)S(1)}, f32[32,384]{1,0:T(8,128)S(1)}) custom-call(f32[32,384]{1,0:T(8,128)S(1)} %get-tuple-element.21.q_ref, f32[32,384]{1,0:T(8,128)S(1)} %get-tuple-element.22.w_ref, f32[192,128]{1,0:T(8,128)S(1)} %get-tuple-element.23.t_ref, f32[32,384]{1,0:T(8,128)S(1)} %get-tuple-element.30.q1_ref, ...), custom_call_target="tpu_custom_call" | custom-call | flops 200000000 | bytes 1000000 | tf_op jit(solution)/shard_map/pallas_call | solution.py:487
  70.6 6.6 %all-to-all-done.1.arrived_ref = bf16[8,3,16,256]{3,2,1,0:T(8,128)(2,1)S(1)} async-done(((bf16[8,3,16,256]{3,2,1,0:T(8,128)(2,1)}), bf16[8,3,16,256]{3,2,1,0:T(8,128)(2,1)S(1)}, u32[]{:S(2)}, u32[]{:S(2)}) %all-to-all-start.1) | async-done | bytes 196640 | tf_op jit(solution)/shard_map/all_to_all | solution.py:505
  77.2 1.2 %shard_map.90 = (f32[5,64,32]{2,1,0:T(8,128)S(1)}, f32[5,64,32]{2,1,0:T(8,128)S(1)}) custom-call(f32[32,384]{1,0:T(8,128)S(1)} %get-tuple-element.35.end_base_ref, f32[32,384]{1,0:T(8,128)S(1)} %get-tuple-element.36.start_base_ref, bf16[8,3,16,256]{3,2,1,0:T(8,128)(2,1)S(1)} %all-to-all-done.1.arrived_ref, s32[1,384]{1,0:T(1,128)S(1)} %copy-done.4, ...), custom_call_target="tpu_custom_call" | custom-call | flops 200000000 | bytes 1000000 | tf_op jit(solution)/shard_map/pallas_call | solution.py:487
  78.5 0.7 copy.11
  79.2 0.7 copy.12
Async XLA Ops:
  0.6 1.0 %copy-start.5 = (f32[5,64,32]{1,2,0:T(8,128)S(1)}, f32[5,64,32]{1,2,0:T(8,128)}, u32[]{:S(2)}) copy-start(f32[5,64,32]{1,2,0:T(8,128)} %param.8) | copy-start | bytes 122884
  1.7 0.7 copy-start.2
  1.7 0.7 copy-start.3
  1.7 0.7 copy-start.4
  3.4 18.7 %collective-permute-start = (bf16[128,512]{1,0:T(8,128)(2,1)S(1)}, bf16[128,512]{1,0:T(8,128)(2,1)S(1)}, u32[]{:S(2)}, u32[]{:S(2)}) collective-permute-start(bf16[128,512]{1,0:T(8,128)(2,1)S(1)} %get-tuple-element.27), channel_id=1, source_target_pairs={{0,760},{8,0},{16,8},{24,16},{32,24},{40,32},{48,40},{56,48},{64,5... | collective-permute-start | bytes 393224 | tf_op jit(solution)/shard_map/ppermute | solution.py:501
  19.6 9.6 %collective-permute-start.1 = (bf16[128,512]{1,0:T(8,128)(2,1)S(1)}, bf16[128,512]{1,0:T(8,128)(2,1)S(1)}, u32[]{:S(2)}, u32[]{:S(2)}) collective-permute-start(bf16[128,512]{1,0:T(8,128)(2,1)S(1)} %get-tuple-element.29), channel_id=1, source_target_pairs={{0,8},{8,16},{16,24},{24,32},{32,40},{40,48},{48,56},{56,64},{64,7... | collective-permute-start | bytes 393224 | tf_op jit(solution)/shard_map/ppermute | solution.py:501
  30.0 7.7 %copy-start = (bf16[128,768]{1,0:T(8,128)(2,1)S(1)}, bf16[128,768]{1,0:T(8,128)(2,1)}, u32[]{:S(2)}) copy-start(bf16[128,768]{1,0:T(8,128)(2,1)} %constant.5.clone.backward_ref) | copy-start | bytes 589828
  30.0 7.7 %copy-start.1 = (bf16[384,256]{1,0:T(8,128)(2,1)S(1)}, bf16[384,256]{1,0:T(8,128)(2,1)}, u32[]{:S(2)}) copy-start(bf16[384,256]{1,0:T(8,128)(2,1)} %constant.4.clone.forward_ref) | copy-start | bytes 589828
  30.0 18.1 %all-to-all-start = ((bf16[8,3,16,512]{3,2,1,0:T(8,128)(2,1)}), bf16[8,3,16,512]{3,2,1,0:T(8,128)(2,1)S(1)}, u32[]{:S(2)}, u32[]{:S(2)}) async-start(bf16[8,3,16,512]{3,2,1,0:T(8,128)(2,1)} %pad_maximum_fusion), calls=%async_computation | async-start | bytes 786432 | tf_op jit(solution)/shard_map/all_to_all | solution.py:505
  51.7 4.7 %collective-permute-start.2 = (bf16[128,256]{1,0:T(8,128)(2,1)S(1)}, bf16[128,256]{1,0:T(8,128)(2,1)S(1)}, u32[]{:S(2)}, u32[]{:S(2)}) collective-permute-start(bf16[128,256]{1,0:T(8,128)(2,1)S(1)} %get-tuple-element.37), channel_id=1, source_target_pairs={{0,760},{8,0},{16,8},{24,16},{32,24},{40,32},{48,40},{56,48},{64,5... | collective-permute-start | bytes 196616 | tf_op jit(solution)/shard_map/ppermute | solution.py:501
  54.5 8.9 %collective-permute-start.3 = (bf16[128,256]{1,0:T(8,128)(2,1)S(1)}, bf16[128,256]{1,0:T(8,128)(2,1)S(1)}, u32[]{:S(2)}, u32[]{:S(2)}) collective-permute-start(bf16[128,256]{1,0:T(8,128)(2,1)S(1)} %get-tuple-element.39), channel_id=1, source_target_pairs={{0,8},{8,16},{16,24},{24,32},{32,40},{40,48},{48,56},{56,64},{64,7... | collective-permute-start | bytes 196616 | tf_op jit(solution)/shard_map/ppermute | solution.py:501
  64.1 13.1 %all-to-all-start.1 = ((bf16[8,3,16,256]{3,2,1,0:T(8,128)(2,1)}), bf16[8,3,16,256]{3,2,1,0:T(8,128)(2,1)S(1)}, u32[]{:S(2)}, u32[]{:S(2)}) async-start(bf16[8,3,16,256]{3,2,1,0:T(8,128)(2,1)} %pad_maximum_fusion.1), calls=%async_computation.1 | async-start | bytes 393216 | tf_op jit(solution)/shard_map/all_to_all | solution.py:505

commit v2 on v1

--- a/solution.py
+++ b/solution.py
@@ -85,21 +85,19 @@
 
 
 def to_tiles(ref):
-    zero = jnp.zeros((64, E), f32)
+    zero = jnp.zeros((E, 64), f32)
     tiles = []
     for j in range(3):
-        low = ref[2 * j]
         high = ref[2 * j + 1] if j < 2 else zero
-        tiles.append(jnp.transpose(jnp.concatenate([low, high], axis=0)))
+        tiles.append(jnp.concatenate([ref[2 * j], high], axis=1))
     return tiles
 
 
 def from_tiles(tiles, ref):
     for j in range(3):
-        t = jnp.transpose(tiles[j])
-        ref[2 * j] = t[:64]
+        ref[2 * j] = tiles[j][:, :64]
         if j < 2:
-            ref[2 * j + 1] = t[64:]
+            ref[2 * j + 1] = tiles[j][:, 64:]
 
 
 def load_tiles(ref):
@@ -237,13 +235,18 @@
             (self.drift + u) * w + jnp.where(self.v == 4, n, 0.0) + jnp.where(self.normal, h, 0.0)
         )
 
-    def flux_back_along(self, a, x, w):
-        index = (a + 1) * 16 + self.m
-        u = take(x, index)
-        n = take(w, index)
-        h = over_fields((x + self.ones) * w)
-        c = u + mean_flow if a == 0 else u
-        return c * w + jnp.where(self.v == 4, n, 0.0) + jnp.where(self.v == a + 1, h, 0.0)
+    def shifted(self, d):
+        target = self.v + d
+        target = jnp.where(target >= 5, target - 5, target)
+        return target, jnp.where(self.v < 5, target * 16 + self.m, 16 * self.v + self.m)
+
+    def hessian(self, d, y):
+        target, index = self.shifted(d)
+        other = take(y, index)
+        inside = self.v < 5
+        half = jnp.where(self.normal, other, 0.0)
+        half = half + jnp.where(inside & (target == self.axis + 1), y, 0.0)
+        return -0.5 * self.sign * half
 
     def mirror(self, x):
         return jnp.where(self.normal, -x, x)
@@ -266,8 +269,8 @@
     return jnp.concatenate([table_ref[f : f + 1, :] for f in range(6)], axis=1)
 
 
-def slot_column(send_ref):
-    x = jnp.broadcast_to(send_ref[...].astype(f32), (8, S))
+def slot_column(send):
+    x = jnp.broadcast_to(send.astype(f32), (8, S))
     return jnp.transpose(x)[:, :1].astype(i32)
 
 
@@ -319,6 +322,21 @@
     return index, inverse
 
 
+def peer_tables(send_ref, ext_ref):
+    odd = (lax.axis_index("dom") & 1) == 1
+    send = send_ref[...]
+    swapped = jnp.concatenate([send[:, 2 * G :], send[:, G : 2 * G], send[:, :G]], axis=1)
+    send = jnp.where(odd, send, swapped)
+
+    def reordered(table):
+        slot = table - F
+        turned = jnp.where(slot < G, slot + 2 * G, jnp.where(slot >= 2 * G, slot - 2 * G, slot))
+        turned = jnp.where((slot >= 0) & (slot < S), turned + F, table)
+        return jnp.where(odd, turned, table)
+
+    return send, reordered(column_of(ext_ref)), reordered(row_of(ext_ref))
+
+
 def packed(x):
     tail = lanes(F) >= 80
     first = jnp.where(tail, turn(x, 80), 0.0)
@@ -333,27 +351,12 @@
     return first + second
 
 
-def write_buffers(forward, back, refs):
-    for o, ref in enumerate(refs):
-        fw = forward[G * o : G * (o + 1)]
-        bk = back[G * (2 - o) : G * (3 - o)]
-        wide = bk.shape[1]
-        ref[:, :256] = (fw + bk[:, :256]).astype(bf16) if wide > 128 else (fw + jnp.concatenate([bk, jnp.zeros_like(bk)], axis=1)).astype(bf16)
-        if wide > 256:
-            ref[:, 256:] = bk[:, 256:].astype(bf16)
-
-
 def exterior(faces, wall, index, onehot_local, t):
     return jnp.where(wall, faces.mirror(t), take(select_rows(onehot_local, t), index))
 
 
-def arrivals(z_ref):
-    width = z_ref.shape[3]
-    return [z_ref[:, o].reshape(G, width) for o in range(3)]
-
-
 def pack_kernel(state_ref, final_ref, send_ref, ext_ref, perm_ref,
-                minus_ref, own_ref, plus_ref, q_ref, w_ref, t_ref, lam_ref):
+                out_ref, q_ref, w_ref, t_ref, lam_ref, send_slots_ref, back_slots_ref, inverse_ref):
     faces = Faces()
     q = to_tiles(state_ref)
     w = to_tiles(final_ref)
@@ -363,24 +366,43 @@
     lam = lift_factor * traces(w)
     t_ref[...] = t
     lam_ref[...] = lam
+    send, _, ext_row = peer_tables(send_ref, ext_ref)
+    send_slots = slots_from_columns(slot_column(send))
+    back_slots = slots_from_faces(ext_row)
+    send_slots_ref[...] = send_slots
+    back_slots_ref[...] = back_slots
     _, inverse = orientation(column_of(perm_ref))
+    inverse_ref[...] = inverse
     y = take(lam, inverse)
-    signed = faces.sign * y
-    stack = [y] + [jnp.where(faces.axis == a, signed, 0.0) for a in range(3)]
-    stack = jnp.concatenate([x.astype(bf16) for x in stack], axis=1)
-    back = dot(slots_from_faces(row_of(ext_ref)), stack)
-    forward = dot(slots_from_columns(slot_column(send_ref)), packed(t))
-    write_buffers(forward, back, (minus_ref, own_ref, plus_ref))
-
-
-def first_local_kernel(q_ref, w_ref, t_ref, ext_ref, perm_ref, forward_ref, backward_ref, base_ref, z_ref):
+    diagonal = jnp.where(faces.normal, -faces.sign * y, 0.0)
+    first = y - 0.5 * faces.flux_back(jnp.zeros_like(y), y) + turn(diagonal, 64)
+    stack = jnp.concatenate([x.astype(bf16) for x in (first, faces.hessian(1, y), faces.hessian(2, y))], axis=1)
+    back = dot(back_slots, stack)
+    forward = dot(send_slots, packed(t))
+    whole = jnp.concatenate([back[:, :128], back[:, 128:] + forward], axis=1).astype(bf16)
+    for o in range(3):
+        for peer in range(8):
+            at = G * o + 16 * peer
+            out_ref[peer, o] = whole[at : at + 16]
+
+
+def first_local_kernel(q_ref, w_ref, t_ref, send_ref, ext_ref, perm_ref, forward_ref, backward_ref,
+                       base_ref, z_ref, from_slots_ref, to_columns_ref, local_ref, local_back_ref, index_ref, kind_ref):
     faces = Faces()
-    ext_col = column_of(ext_ref)
+    send, ext_col, ext_row = peer_tables(send_ref, ext_ref)
     index, _ = orientation(column_of(perm_ref))
-    wall = jnp.broadcast_to(ext_col, (F, 128)) == F + S
+    index_ref[...] = index
+    ext_wide = jnp.broadcast_to(ext_col, (F, 128))
+    wall = ext_wide == F + S
+    kind_ref[...] = jnp.where(wall, 2, jnp.where(ext_wide >= F, 1, 0))
+    from_slots_ref[...] = faces_from_slots(ext_col)
+    to_columns_ref[...] = columns_from_slots(send)
+    local = faces_from_columns(ext_col)
+    local_ref[...] = local
+    local_back_ref[...] = columns_from_faces(ext_row)
     q = load_tiles(q_ref)
     t = t_ref[...]
-    x = exterior(faces, wall, index, faces_from_columns(ext_col), t)
+    x = exterior(faces, wall, index, local, t)
     jump = 0.5 * (faces.flux(t) - faces.flux(x)) + (x - t)
     faced = lifted(lift_factor * jump)
     inner = volume(q, forward_ref[...])
@@ -388,39 +410,43 @@
     z_ref[...] = derivative_back(load_tiles(w_ref), backward_ref[...])
 
 
-def middle_kernel(base_ref, w_ref, t_lam_ref, z_ref, arrived_ref, send_ref, ext_ref, perm_ref,
-                  minus_ref, own_ref, plus_ref, q1_ref, w1_ref, t1_ref, x1_ref, lam1_ref):
+def middle_kernel(base_ref, w_ref, lam_ref, z_ref, chip_ref, own_ref, next_ref,
+                  from_slots_ref, to_columns_ref, local_ref, local_back_ref, send_slots_ref, back_slots_ref,
+                  index_ref, inverse_ref, kind_ref,
+                  out_ref, q1_ref, w1_ref, t1_ref, x1_ref, lam1_ref):
     faces = Faces()
-    ext_col = column_of(ext_ref)
-    ext_row = row_of(ext_ref)
-    index, inverse = orientation(column_of(perm_ref))
-    ext_wide = jnp.broadcast_to(ext_col, (F, 128))
-    wall = ext_wide == F + S
-    remote = (ext_wide >= F) & (ext_wide < F + S)
-    from_plus, from_own, from_minus = arrivals(arrived_ref)
-    incoming = jnp.concatenate([from_plus[:, :256], from_own[:, :256], from_minus[:, :256]], axis=0)
-    xr = take(unpacked(dot(faces_from_slots(ext_col), incoming)), index)
+    index = index_ref[...]
+    inverse = inverse_ref[...]
+    kind = kind_ref[...]
+    wall = kind == 2
+    arrived = jnp.concatenate(
+        [chip_ref[...].reshape(G, 384), own_ref[:, 1].reshape(G, 384), next_ref[...].reshape(G, 384)], axis=0)
+    xr = take(unpacked(dot(from_slots_ref[...], arrived[:, 128:])), index)
+    sums = dot(to_columns_ref[...], arrived)
     faced = lifted((lift_factor * step_size) * (xr - 0.5 * faces.flux(xr)))
     base = load_tiles(base_ref)
     q1 = [base[j] + faced[j] for j in range(3)]
     store_tiles(q1_ref, q1)
     t1 = traces(q1)
     t1_ref[...] = t1
-    send_row = send_ref[...]
-    forward = dot(slots_from_columns(slot_column(send_ref)), packed(t1))
-    lam = t_lam_ref[...]
-    x1 = exterior(faces, wall, index, faces_from_columns(ext_col), t1)
+    forward = dot(send_slots_ref[...], packed(t1))
+    lam = lam_ref[...]
+    x1 = exterior(faces, wall, index, local_ref[...], t1)
     x1_ref[...] = x1
-    bar = jnp.where(remote, 0.0, lam - 0.5 * faces.flux_back(x1, lam))
+    bar = jnp.where(kind == 1, 0.0, lam - 0.5 * faces.flux_back(x1, lam))
     total = 0.5 * faces.flux_back(t1, lam) - lam + jnp.where(wall, faces.mirror(bar), 0.0)
-    total = total + select_rows(columns_from_faces(ext_row), take(bar, inverse))
-    returned = jnp.concatenate([from_minus, from_own, from_plus], axis=0)
-    sums = dot(columns_from_slots(send_row), returned)
-    valid = lanes(F) < 80
-    sums = [jnp.where(valid, sums[:, 128 * a : 128 * (a + 1)], 0.0) for a in range(4)]
-    t1_sent = t1.astype(bf16).astype(f32)
-    through = [faces.flux_back_along(a, t1_sent, sums[a + 1]) for a in range(3)]
-    total = total + sums[0] - 0.5 * (through[0] + through[1] + through[2])
+    total = total + select_rows(local_back_ref[...], take(bar, inverse))
+    lane = lanes(F)
+    sent = t1.astype(bf16).astype(f32)
+    h1, h2 = sums[:, 128:256], sums[:, 256:]
+    _, index1 = faces.shifted(1)
+    _, index2 = faces.shifted(2)
+    _, index3 = faces.shifted(3)
+    _, index4 = faces.shifted(4)
+    through = sums[:, :128] + h1 * take(sent, index1) + h2 * take(sent, index2)
+    through = through + take(h1, index4) * take(sent, index4) + take(h2, index3) * take(sent, index3)
+    through = through + jnp.where((lane >= 16) & (lane < 64), turn(sums[:, :128], 64) * sent, 0.0)
+    total = total + jnp.where(lane < 80, through, 0.0)
     inner = volume_back(q1, z_ref[...])
     faced = lifted(total)
     w = load_tiles(w_ref)
@@ -429,18 +455,26 @@
     lam1 = lift_factor * traces(w1)
     lam1_ref[...] = lam1
     y = take(lam1 - 0.5 * faces.flux_back(xr, lam1), inverse)
-    back = dot(slots_from_faces(ext_row), y.astype(bf16))
-    write_buffers(forward, back, (minus_ref, own_ref, plus_ref))
-
-
-def second_local_kernel(q_ref, w_ref, t_ref, q1_ref, w1_ref, t1_ref, x1_ref, lam1_ref, ext_ref, perm_ref,
+    back = dot(back_slots_ref[...], y.astype(bf16))
+    main = (back + forward[:, :128]).astype(bf16)
+    tail = [turn(forward[G * o : G * (o + 1), 128:], 48 + 32 * o) for o in range(3)]
+    shared = (tail[0] + tail[1] + tail[2]).astype(bf16)
+    for peer in range(8):
+        at = 16 * peer
+        out_ref[peer, 0] = main[at : at + 16]
+        out_ref[peer, 1] = shared[at : at + 16]
+        out_ref[peer, 2] = main[2 * G + at : 2 * G + at + 16]
+        out_ref[peer, 3] = main[G + at : G + at + 16]
+
+
+def second_local_kernel(q_ref, w_ref, t_ref, q1_ref, w1_ref, t1_ref, x1_ref, lam1_ref,
+                        local_ref, local_back_ref, index_ref, inverse_ref, kind_ref,
                         forward_ref, backward_ref, end_ref, start_ref):
     faces = Faces()
-    ext_col = column_of(ext_ref)
-    index, inverse = orientation(column_of(perm_ref))
-    ext_wide = jnp.broadcast_to(ext_col, (F, 128))
-    wall = ext_wide == F + S
-    remote = (ext_wide >= F) & (ext_wide < F + S)
+    index = index_ref[...]
+    inverse = inverse_ref[...]
+    kind = kind_ref[...]
+    wall = kind == 2
     q = load_tiles(q_ref)
     q1 = load_tiles(q1_ref)
     t1 = t1_ref[...]
@@ -451,10 +485,10 @@
     store_tiles(end_ref, [0.5 * q[j] + 0.5 * (q1[j] + step_size * (inner[j] + faced[j])) for j in range(3)])
     t = t_ref[...]
     lam1 = lam1_ref[...]
-    x = exterior(faces, wall, index, faces_from_columns(ext_col), t)
-    bar = jnp.where(remote, 0.0, lam1 - 0.5 * faces.flux_back(x, lam1))
+    x = exterior(faces, wall, index, local_ref[...], t)
+    bar = jnp.where(kind == 1, 0.0, lam1 - 0.5 * faces.flux_back(x, lam1))
     total = 0.5 * faces.flux_back(t, lam1) - lam1 + jnp.where(wall, faces.mirror(bar), 0.0)
-    total = total + select_rows(columns_from_faces(row_of(ext_ref)), take(bar, inverse))
+    total = total + select_rows(local_back_ref[...], take(bar, inverse))
     w = load_tiles(w_ref)
     w1 = load_tiles(w1_ref)
     inner = volume_back(q, derivative_back(w1, backward_ref[...]))
@@ -462,18 +496,29 @@
     store_tiles(start_ref, [0.5 * w[j] + w1[j] + step_size * (inner[j] + faced[j]) for j in range(3)])
 
 
-def last_kernel(end_base_ref, start_base_ref, arrived_ref, send_ref, ext_ref, perm_ref, end_ref, start_ref):
+def last_kernel(end_base_ref, start_base_ref, chip_ref, own_ref, next_ref, from_slots_ref, to_columns_ref, index_ref,
+                end_ref, start_ref):
     faces = Faces()
-    index, _ = orientation(column_of(perm_ref))
-    from_plus, from_own, from_minus = arrivals(arrived_ref)
-    incoming = jnp.concatenate([from_plus, from_own, from_minus], axis=0)
-    returned = jnp.concatenate([from_minus[:, :128], from_own[:, :128], from_plus[:, :128]], axis=0)
-    xr = take(unpacked(dot(faces_from_slots(column_of(ext_ref)), incoming)), index)
+    main = jnp.concatenate(
+        [chip_ref[:, 0].reshape(G, 128), own_ref[:, 3].reshape(G, 128), next_ref[:, 1].reshape(G, 128)], axis=0)
+    lane = lanes(G)
+    zero = jnp.zeros((G, 128), bf16)
+    shared = jnp.concatenate([
+        jnp.where(lane < 32, chip_ref[:, 1].reshape(G, 128), zero),
+        jnp.where((lane >= 32) & (lane < 64), own_ref[:, 1].reshape(G, 128), zero),
+        jnp.where((lane >= 64) & (lane < 96), next_ref[:, 0].reshape(G, 128), zero)], axis=0)
+    g = dot(from_slots_ref[...], jnp.concatenate([main, shared], axis=1))
+    lane = lanes(F)
+    x = jnp.where(lane < 48, turn(g[:, :128], 48), 0.0)
+    high = g[:, 128:]
+    high = turn(high, 48) + turn(high, 16) + turn(high, 112)
+    x = x + jnp.where((lane >= 48) & (lane < 80), high, 0.0)
+    xr = take(x, index_ref[...])
     faced = lifted((0.5 * step_size * lift_factor) * (xr - 0.5 * faces.flux(xr)))
     base = load_tiles(end_base_ref)
     from_tiles([base[j] + faced[j] for j in range(3)], end_ref)
-    bar = dot(columns_from_slots(send_ref[...]), returned)
-    bar = jnp.where(lanes(F) < 80, bar, 0.0)
+    bar = dot(to_columns_ref[...], main)
+    bar = jnp.where(lane < 80, bar, 0.0)
     faced = lifted(step_size * bar)
     base = load_tiles(start_base_ref)
     from_tiles([base[j] + faced[j] for j in range(3)], start_ref)
@@ -492,42 +537,56 @@
     )(*args)
 
 
-def exchange(to_minus, to_own, to_plus):
+def all_peers(whole):
+    return lax.all_to_all(whole, "sub", split_axis=0, concat_axis=0, tiled=True)
+
+
+def next_partner(value):
     count = lax.axis_size("dom")
-    width = to_own.shape[1]
-
-    def moved(value, steps):
-        pairs = [(source, (source + steps) % count) for source in range(count)]
-        return lax.ppermute(value, "dom", pairs)
-
-    pieces = [moved(to_minus, -1), to_own, moved(to_plus, 1)]
-    whole = jnp.stack([x.reshape(8, 16, width) for x in pieces], axis=1)
-    return lax.all_to_all(whole, "sub", split_axis=0, concat_axis=0, tiled=True)
+    pairs = [(d, (d + 1) % count if d % 2 else (d - 1) % count) for d in range(count)]
+    return lax.ppermute(value, "dom", pairs)
+
+
+def chip_partner(value):
+    return lax.ppermute(value, "dom", [(d, d ^ 1) for d in range(lax.axis_size("dom"))])
 
 
 def shards(state, adjoint_final, send_slot, ext_index, ext_perm):
     forward, backward = derivative_operands()
     forward, backward = jnp.asarray(forward), jnp.asarray(backward)
+    state, adjoint_final = jnp.swapaxes(state, 1, 2), jnp.swapaxes(adjoint_final, 1, 2)
     node = shape(E, 384)
     face = shape(F, 128)
-    wide = shape(G, 512, dtype=bf16)
-    slim = shape(G, 256, dtype=bf16)
-
-    *buffers, q, w, t, lam = call(
-        pack_kernel, (wide, wide, wide, node, node, face, face),
+    index_face = shape(F, 128, dtype=i32)
+
+    out, q, w, t, lam, send_slots, back_slots, inverse = call(
+        pack_kernel,
+        (shape(8, 3, 16, 384, dtype=bf16), node, node, face, face,
+         shape(S, F, dtype=bf16), shape(S, F, dtype=bf16), index_face),
         state, adjoint_final, send_slot, ext_index, ext_perm)
-    arrived = exchange(*buffers)
-    base, z = call(first_local_kernel, (node, shape(96, 384)), q, w, t, ext_index, ext_perm, forward, backward)
-    *buffers, q1, w1, t1, x1, lam1 = call(
-        middle_kernel, (slim, slim, slim, node, node, face, face, face),
-        base, w, lam, z, arrived, send_slot, ext_index, ext_perm)
-    arrived = exchange(*buffers)
+    arrived = all_peers(out)
+    base, z, from_slots, to_columns, local, local_back, index, kind = call(
+        first_local_kernel,
+        (node, shape(96, 384), shape(F, S, dtype=bf16), shape(F, S, dtype=bf16),
+         shape(F, F, dtype=bf16), shape(F, F, dtype=bf16), index_face, index_face),
+        q, w, t, send_slot, ext_index, ext_perm, forward, backward)
+    from_next = next_partner(arrived[:, 2])
+    from_chip = chip_partner(arrived[:, 0])
+    out, q1, w1, t1, x1, lam1 = call(
+        middle_kernel, (shape(8, 4, 16, 128, dtype=bf16), node, node, face, face, face),
+        base, w, lam, z, from_chip, arrived, from_next,
+        from_slots, to_columns, local, local_back, send_slots, back_slots, index, inverse, kind)
+    arrived = all_peers(out)
     end_base, start_base = call(
         second_local_kernel, (node, node),
-        q, w, t, q1, w1, t1, x1, lam1, ext_index, ext_perm, forward, backward)
-    out = shape(5, 64, E)
-    return tuple(call(
-        last_kernel, (out, out), end_base, start_base, arrived, send_slot, ext_index, ext_perm))
+        q, w, t, q1, w1, t1, x1, lam1, local, local_back, index, inverse, kind, forward, backward)
+    from_next = next_partner(arrived[:, 1:3])
+    from_chip = chip_partner(arrived[:, 0:2])
+    out = shape(5, E, 64)
+    end, start = call(
+        last_kernel, (out, out),
+        end_base, start_base, from_chip, arrived, from_next, from_slots, to_columns, index)
+    return jnp.swapaxes(end, 1, 2), jnp.swapaxes(start, 1, 2)
 
 
 def solution(mesh):

time: 80.4 us -> 70.2 us (0.87)
  the two profiles are of different devices: /device:TPU:8 before, /device:TPU:1 now
where the time goes in v2:
time: 70.2 us; the launch traced here: 69.7 us
  starting transfers between devices  29 us (41%)
  blocking collectives  28.1 us (40%)
  Pallas kernels  8.01 us (11%)
  local copies, waits for them, and re-layouts  3.86 us (5%)
  between operations  0.76 us (1%)
    all_to_all x2, blocking collectives, all_peers(): return lax.all_to_all(whole, 'sub', split_axis=0, concat_axis=0, tiled=True)  28.1 us
    ppermute x2, starting transfers between devices, chip_partner(): lax.ppermute(value, 'dom', [(d, d ^ 1) for d in range(lax.axis_size('dom'...  19.2 us
    ppermute x2, starting transfers between devices, next_partner(): return lax.ppermute(value, 'dom', pairs)  9.79 us
    pallas_call x5, Pallas kernels, call(): pl.pallas_call(kernel, out_shape=outs, cost_estimate=pl.CostEstimate(flop...  8.01 us
    unnamed x14, local copies, waits for them, and re-layouts  3.83 us
  transfers between devices with their start and end apart: 4, of which 0 were waited for; matrix products, arithmetic and copies ran while one was open for 0% of the time, Pallas kernels for 3%

profile of v2, /device:TPU:1, one launch (start us, length us, event | category | flops | bytes accessed | tf_op | source)
XLA Modules:
  0.0 69.7 jit_solution(7650996322255356028)
XLA Ops:
  0.6 0.0 copy-start.6
  0.6 0.7 copy-done.6
  1.3 0.0 copy-start.2
  1.3 0.9 %copy-done.2 = f32[5,64,32]{1,2,0:T(8,128)S(1)} copy-done((f32[5,64,32]{1,2,0:T(8,128)S(1)}, f32[5,64,32]{1,2,0:T(8,128)}, u32[]{:S(2)}) %copy-start.2) | copy-done | bytes 40984
  2.2 0.0 copy-start.3
  2.2 0.9 %copy-done.3 = f32[5,64,32]{1,2,0:T(8,128)S(1)} copy-done((f32[5,64,32]{1,2,0:T(8,128)S(1)}, f32[5,64,32]{1,2,0:T(8,128)}, u32[]{:S(2)}) %copy-start.3) | copy-done | bytes 40984
  3.1 0.0 copy-start.4
  3.1 0.7 copy-done.4
  3.8 0.0 copy-start.5
  3.8 0.7 copy-done.5
  4.5 1.3 %shard_map.86 = (bf16[8,3,16,384]{3,2,1,0:T(8,128)(2,1)S(1)}, f32[32,384]{1,0:T(8,128)S(1)}, f32[32,384]{1,0:T(8,128)S(1)}, f32[192,128]{1,0:T(8,128)S(1)}, f32[...) custom-call(f32[5,32,64]{2,1,0:T(8,128)S(1)} %bitcast.12, ...), custom_call_target="tpu_custom_call" | custom-call | flops 200000000 | bytes 1000000 | tf_op jit(solution)/shard_map/pallas_call | solution.py:532
  5.8 17.1 %all_to_all.10.own_ref = bf16[8,3,16,384]{3,2,1,0:T(8,128)(2,1)S(1)} all-to-all(bf16[8,3,16,384]{3,2,1,0:T(8,128)(2,1)S(1)} %get-tuple-element.34), channel_id=1, replica_groups=mesh['dom'=96,'sub'=8] {'sub'}, dimensions={0} | all-to-all | bytes 589824 | tf_op jit(solution)/shard_map/all_to_all | solution.py:541
  22.9 0.0 copy-start
  22.9 0.0 copy-start.1
  23.0 7.9 %collective-permute-start.1 = (bf16[8,16,384]{2,1,0:T(8,128)(2,1)S(1)}, bf16[8,16,384]{2,1,0:T(8,128)(2,1)S(1)}, u32[]{:S(2)}, u32[]{:S(2)}) collective-permute-start(bf16[8,16,384]{2,1,0:T(8,128)(2,1)S(1)} %get-tuple-element.54), channel_id=1, source_target_pairs={{0,760},{8,16},{16,8},{24,32},{32,24},{40,48},{48,40},{56,64},{64,... | collective-permute-start | bytes 294920 | tf_op jit(solution)/shard_map/ppermute | solution.py:547
  30.8 12.2 %collective-permute-start = (bf16[8,16,384]{2,1,0:T(8,128)(2,1)S(1)}, bf16[8,16,384]{2,1,0:T(8,128)(2,1)S(1)}, u32[]{:S(2)}, u32[]{:S(2)}) collective-permute-start(bf16[8,16,384]{2,1,0:T(8,128)(2,1)S(1)} %get-tuple-element.55), channel_id=1, source_target_pairs={{0,8},{8,0},{16,24},{24,16},{32,40},{40,32},{48,56},{56,48},{64,72... | collective-permute-start | bytes 294920 | tf_op jit(solution)/shard_map/ppermute | solution.py:551
  43.1 0.0 copy-done
  43.1 0.0 copy-done.1
  43.1 0.9 %shard_map.87 = (f32[32,384]{1,0:T(8,128)S(1)}, f32[96,384]{1,0:T(8,128)S(1)}, bf16[192,384]{1,0:T(8,128)(2,1)S(1)}, bf16[192,384]{1,0:T(8,128)(2,1)S(1)}, bf16[...) custom-call(f32[32,384]{1,0:T(8,128)S(1)} %get-tuple-element.28.q_ref, ...), custom_call_target="tpu_custom_call" | custom-call | flops 200000000 | bytes 1000000 | tf_op jit(solution)/shard_map/pallas_call | solution.py:532
  44.0 0.0 collective-permute-done.1.next_ref
  44.0 0.0 collective-permute-done.chip_ref
  44.0 2.8 %shard_map.88 = (bf16[8,4,16,128]{3,2,1,0:T(8,128)(2,1)S(1)}, f32[32,384]{1,0:T(8,128)S(1)}, f32[32,384]{1,0:T(8,128)S(1)}, f32[192,128]{1,0:T(8,128)S(1)}, f32[...) custom-call(f32[32,384]{1,0:T(8,128)S(1)} %get-tuple-element.31.base_ref, f32[32,384]{1,0:T(8,128)S(1)} %get-tuple-element.29.w_ref, ...), custom_call_target="tpu_custom_call" | custom-call | flops 200000000 | bytes 1000000 | tf_op jit(solution)/shard_map/pallas_call | solution.py:532
  46.8 11.0 %all_to_all.11.own_ref = bf16[8,4,16,128]{3,2,1,0:T(8,128)(2,1)S(1)} all-to-all(bf16[8,4,16,128]{3,2,1,0:T(8,128)(2,1)S(1)} %get-tuple-element.51), channel_id=1, replica_groups=mesh['dom'=96,'sub'=8] {'sub'}, dimensions={0} | all-to-all | bytes 262144 | tf_op jit(solution)/shard_map/all_to_all | solution.py:541
  57.8 1.9 %collective-permute-start.3 = (bf16[8,2,16,128]{3,2,1,0:T(8,128)(2,1)S(1)}, bf16[8,2,16,128]{3,2,1,0:T(8,128)(2,1)S(1)}, u32[]{:S(2)}, u32[]{:S(2)}) collective-permute-start(bf16[8,2,16,128]{3,2,1,0:T(8,128)(2,1)S(1)} %get-tuple-element.56), channel_id=1, source_target_pairs={{0,760},{8,16},{16,8},{24,32},{32,24},{40,48},{48,40},{56,64},{64,... | collective-permute-start | bytes 196616 | tf_op jit(solution)/shard_map/ppermute | solution.py:547
  59.7 7.0 %collective-permute-start.2 = (bf16[8,2,16,128]{3,2,1,0:T(8,128)(2,1)S(1)}, bf16[8,2,16,128]{3,2,1,0:T(8,128)(2,1)S(1)}, u32[]{:S(2)}, u32[]{:S(2)}) collective-permute-start(bf16[8,2,16,128]{3,2,1,0:T(8,128)(2,1)S(1)} %get-tuple-element.57), channel_id=1, source_target_pairs={{0,8},{8,0},{16,24},{24,16},{32,40},{40,32},{48,56},{56,48},{64,72... | collective-permute-start | bytes 196616 | tf_op jit(solution)/shard_map/ppermute | solution.py:551
  66.7 1.4 %shard_map.89 = (f32[32,384]{1,0:T(8,128)S(1)}, f32[32,384]{1,0:T(8,128)S(1)}) custom-call(f32[32,384]{1,0:T(8,128)S(1)} %get-tuple-element.28.q_ref, f32[32,384]{1,0:T(8,128)S(1)} %get-tuple-element.29.w_ref, f32[192,128]{1,0:T(8,128)S(1)} %get-tuple-element.30.t_ref, f32[32,384]{1,0:T(8,128)S(1)} %get-tuple-element.44.q1_ref, ...), custom_call_target="tpu_custom_call" | custom-call | flops 200000000 | bytes 1000000 | tf_op jit(solution)/shard_map/pallas_call | solution.py:532
  68.1 0.0 collective-permute-done.3.next_ref
  68.1 0.0 collective-permute-done.2.chip_ref
  68.1 1.6 %shard_map.90 = (f32[5,32,64]{2,1,0:T(8,128)}, f32[5,32,64]{2,1,0:T(8,128)}) custom-call(f32[32,384]{1,0:T(8,128)S(1)} %get-tuple-element.49.end_base_ref, f32[32,384]{1,0:T(8,128)S(1)} %get-tuple-element.50.start_base_ref, bf16[8,2,16,128]{3,2,1,0:T(8,128)(2,1)S(1)} %collective-permute-done.2.chip_ref, bf16[8,4,16,128]{3,2,1,0:T(8,128)(2,1)S(1)} %all_to_all.11.own_ref, ...), custom_call_target="tpu_custom_call" | custom-call | flops 200000000 | bytes 1000000 | tf_op jit(solution)/shard_map/pallas_call | solution.py:532
  (2 shorter events, 0.0 us)
Async XLA Ops:
  0.6 0.7 copy-start.6
  1.3 0.9 %copy-start.2 = (f32[5,64,32]{1,2,0:T(8,128)S(1)}, f32[5,64,32]{1,2,0:T(8,128)}, u32[]{:S(2)}) copy-start(f32[5,64,32]{1,2,0:T(8,128)} %param.7) | copy-start | bytes 122884
  2.2 0.9 %copy-start.3 = (f32[5,64,32]{1,2,0:T(8,128)S(1)}, f32[5,64,32]{1,2,0:T(8,128)}, u32[]{:S(2)}) copy-start(f32[5,64,32]{1,2,0:T(8,128)} %param.8) | copy-start | bytes 122884
  3.1 0.7 copy-start.4
  3.8 0.7 copy-start.5
  22.9 20.1 %copy-start = (bf16[128,768]{1,0:T(8,128)(2,1)S(1)}, bf16[128,768]{1,0:T(8,128)(2,1)}, u32[]{:S(2)}) copy-start(bf16[128,768]{1,0:T(8,128)(2,1)} %constant.5.clone.backward_ref) | copy-start | bytes 589828
  22.9 20.1 %copy-start.1 = (bf16[384,256]{1,0:T(8,128)(2,1)S(1)}, bf16[384,256]{1,0:T(8,128)(2,1)}, u32[]{:S(2)}) copy-start(bf16[384,256]{1,0:T(8,128)(2,1)} %constant.4.clone.forward_ref) | copy-start | bytes 589828
  23.0 21.0 %collective-permute-start.1 = (bf16[8,16,384]{2,1,0:T(8,128)(2,1)S(1)}, bf16[8,16,384]{2,1,0:T(8,128)(2,1)S(1)}, u32[]{:S(2)}, u32[]{:S(2)}) collective-permute-start(bf16[8,16,384]{2,1,0:T(8,128)(2,1)S(1)} %get-tuple-element.54), channel_id=1, source_target_pairs={{0,760},{8,16},{16,8},{24,32},{32,24},{40,48},{48,40},{56,64},{64,... | collective-permute-start | bytes 294920 | tf_op jit(solution)/shard_map/ppermute | solution.py:547
  30.8 13.2 %collective-permute-start = (bf16[8,16,384]{2,1,0:T(8,128)(2,1)S(1)}, bf16[8,16,384]{2,1,0:T(8,128)(2,1)S(1)}, u32[]{:S(2)}, u32[]{:S(2)}) collective-permute-start(bf16[8,16,384]{2,1,0:T(8,128)(2,1)S(1)} %get-tuple-element.55), channel_id=1, source_target_pairs={{0,8},{8,0},{16,24},{24,16},{32,40},{40,32},{48,56},{56,48},{64,72... | collective-permute-start | bytes 294920 | tf_op jit(solution)/shard_map/ppermute | solution.py:551
  57.8 10.3 %collective-permute-start.3 = (bf16[8,2,16,128]{3,2,1,0:T(8,128)(2,1)S(1)}, bf16[8,2,16,128]{3,2,1,0:T(8,128)(2,1)S(1)}, u32[]{:S(2)}, u32[]{:S(2)}) collective-permute-start(bf16[8,2,16,128]{3,2,1,0:T(8,128)(2,1)S(1)} %get-tuple-element.56), channel_id=1, source_target_pairs={{0,760},{8,16},{16,8},{24,32},{32,24},{40,48},{48,40},{56,64},{64,... | collective-permute-start | bytes 196616 | tf_op jit(solution)/shard_map/ppermute | solution.py:547
  59.7 8.4 %collective-permute-start.2 = (bf16[8,2,16,128]{3,2,1,0:T(8,128)(2,1)S(1)}, bf16[8,2,16,128]{3,2,1,0:T(8,128)(2,1)S(1)}, u32[]{:S(2)}, u32[]{:S(2)}) collective-permute-start(bf16[8,2,16,128]{3,2,1,0:T(8,128)(2,1)S(1)} %get-tuple-element.57), channel_id=1, source_target_pairs={{0,8},{8,0},{16,24},{24,16},{32,40},{40,32},{48,56},{56,48},{64,72... | collective-permute-start | bytes 196616 | tf_op jit(solution)/shard_map/ppermute | solution.py:551

commit v3 on v2

--- a/solution.py
+++ b/solution.py
@@ -56,12 +56,16 @@
     return forward, backward
 
 
-def lanes(rows):
+def lanes(rows=1):
     return lax.broadcasted_iota(i32, (rows, 128), 1)
 
 
 def take(x, index):
-    return jnp.take_along_axis(x, index, axis=1)
+    return jnp.take_along_axis(x, jnp.broadcast_to(index, x.shape), axis=1)
+
+
+def mask(condition):
+    return jnp.where(condition, 1.0, 0.0).astype(f32)
 
 
 def turn(x, shift):
@@ -166,74 +170,93 @@
 
 
 def traces(tiles):
-    lane = lanes(E)
+    lane = lanes()
+    wide = lanes(E)
     m = lane & 15
     r, s = m >> 2, m & 3
     base = ((lane >> 4) & 1) * 64
     rows = []
     for f in range(6):
         b = f % 2
-        node = (48 * b + m, 16 * r + 12 * b + s, 4 * m + 3 * b)[f // 2]
-        index = base + node
+        index = base + (48 * b + m, 16 * r + 12 * b + s, 4 * m + 3 * b)[f // 2]
+        index = jnp.where(lane < 80, index, 64)
         t = jnp.where(
-            lane < 32,
+            wide < 32,
             take(tiles[0], index),
-            jnp.where(lane < 64, take(tiles[1], index), take(tiles[2], index)),
+            jnp.where(wide < 64, take(tiles[1], index), take(tiles[2], index)),
         )
-        rows.append(jnp.where(lane < 80, t, 0.0))
+        rows.append(t)
     return jnp.concatenate(rows, axis=0)
 
 
 def lifted(x):
-    lane = lanes(E)
+    lane = lanes()
+    wide = lanes(E)
     n = lane & 63
     i, j, k = n >> 4, (n >> 2) & 3, n & 3
-    grid = ((i, 4 * j + k), (j, 4 * i + k), (k, 4 * i + j))
+    places = (4 * j + k, 4 * i + k, 4 * i + j)
+    layers = ((wide >> 4) & 3, (wide >> 2) & 3, wide & 3)
     tiles = []
     for tile in range(3):
         v = 2 * tile + (lane >> 6)
-        total = jnp.zeros((E, 128), f32)
+        total = None
         for a in range(3):
-            layer, m = grid[a]
-            index = v * 16 + m
+            index = v * 16 + places[a]
             first = take(x[64 * a : 64 * a + 32], index)
             last = take(x[64 * a + 32 : 64 * a + 64], index)
-            total = total + jnp.where(layer == 0, first, jnp.where(layer == 3, last, 0.0))
+            part = jnp.where(layers[a] == 0, first, jnp.where(layers[a] == 3, last, 0.0))
+            total = part if total is None else total + part
         tiles.append(total)
     return tiles
 
 
+def by_axis(function, *arrays):
+    return jnp.concatenate(
+        [function(a, *[x[64 * a : 64 * (a + 1)] for x in arrays]) for a in range(3)], axis=0)
+
+
+def signed(x):
+    return jnp.concatenate([-x[:32], x[32:]], axis=0)
+
+
 class Faces:
     def __init__(self):
-        row = lax.broadcasted_iota(i32, (F, 128), 0)
-        lane = lanes(F)
+        lane = lanes()
         self.v = lane >> 4
-        m = lane & 15
-        axis = row >> 6
-        self.sign = jnp.where((row >> 5) & 1 == 1, 1.0, -1.0).astype(f32)
-        self.drift = jnp.where(axis == 0, mean_flow, 0.0).astype(f32)
-        self.normal = self.v == axis + 1
-        self.normal_index = (axis + 1) * 16 + m
-        self.pressure_index = 64 + m
-        self.m = m
-        self.ends = (self.v == 0) | (self.v == 4)
-        self.ones = jnp.where(self.ends, 1.0, 0.0).astype(f32)
-        self.axis = axis
+        self.m = lane & 15
+        self.ends = mask((self.v == 0) | (self.v == 4))
+        self.last = mask(self.v == 4)
+        self.normal = [mask(self.v == a + 1) for a in range(3)]
+        self.normal_index = [(a + 1) * 16 + self.m for a in range(3)]
+        self.pressure_index = 64 + self.m
 
     def flux(self, x):
-        u = take(x, self.normal_index)
-        p = take(x, self.pressure_index)
-        return self.sign * (
-            (self.drift + u) * x + jnp.where(self.ends, u, 0.0) + jnp.where(self.normal, p, 0.0)
-        )
+        def along(a, x):
+            u = take(x, self.normal_index[a])
+            p = take(x, self.pressure_index)
+            c = u + mean_flow if a == 0 else u
+            return signed(c * x + self.ends * u + self.normal[a] * p)
+
+        return by_axis(along, x)
 
     def flux_back(self, x, w):
-        u = take(x, self.normal_index)
-        n = take(w, self.normal_index)
-        h = over_fields((x + self.ones) * w)
-        return self.sign * (
-            (self.drift + u) * w + jnp.where(self.v == 4, n, 0.0) + jnp.where(self.normal, h, 0.0)
-        )
+        def along(a, x, w):
+            u = take(x, self.normal_index[a])
+            n = take(w, self.normal_index[a])
+            c = u + mean_flow if a == 0 else u
+            h = over_fields((x + self.ends) * w)
+            return signed(c * w + self.last * n + self.normal[a] * h)
+
+        return by_axis(along, x, w)
+
+    def rest_back(self, w):
+        def along(a, w):
+            n = take(w, self.normal_index[a])
+            h = over_fields(self.ends * w)
+            part = self.last * n + self.normal[a] * h
+            return signed(mean_flow * w + part if a == 0 else part)
+
+        return by_axis(along, w)
 
     def shifted(self, d):
         target = self.v + d
@@ -242,14 +265,15 @@
 
     def hessian(self, d, y):
         target, index = self.shifted(d)
-        other = take(y, index)
-        inside = self.v < 5
-        half = jnp.where(self.normal, other, 0.0)
-        half = half + jnp.where(inside & (target == self.axis + 1), y, 0.0)
-        return -0.5 * self.sign * half
+
+        def along(a, y):
+            back = mask((self.v < 5) & (target == a + 1))
+            return signed(-0.5 * (self.normal[a] * take(y, index) + back * y))
+
+        return by_axis(along, y)
 
     def mirror(self, x):
-        return jnp.where(self.normal, -x, x)
+        return by_axis(lambda a, x: x * (1.0 - 2.0 * self.normal[a]), x)
 
 
 def over_fields(h):
@@ -305,21 +329,13 @@
 def orientation(perm_col):
     lane = lanes(F)
     m = lane & 15
-    r, s = m >> 2, m & 3
+    crossed = lane - m + ((m & 3) * 4 + (m >> 2))
     k = jnp.broadcast_to(perm_col, (F, 128))
-    flip_r = (k & 1) == 1
-    flip_s = (k & 2) == 2
+    flips = (k & 1) * 12 + ((k & 2) >> 1) * 3
+    crossed_flips = (k & 1) * 3 + ((k & 2) >> 1) * 12
     swap = (k & 4) == 4
-    r1 = jnp.where(flip_r, 3 - r, r)
-    s1 = jnp.where(flip_s, 3 - s, s)
-    base = lane - m
-    index = base + jnp.where(swap, 4 * s1 + r1, 4 * r1 + s1)
-    r2 = jnp.where(swap, s, r)
-    s2 = jnp.where(swap, r, s)
-    r2 = jnp.where(flip_r, 3 - r2, r2)
-    s2 = jnp.where(flip_s, 3 - s2, s2)
-    inverse = base + 4 * r2 + s2
-    return index, inverse
+    place = jnp.where(swap, crossed, lane)
+    return place ^ jnp.where(swap, crossed_flips, flips), place ^ flips
 
 
 def peer_tables(send_ref, ext_ref):
@@ -355,9 +371,25 @@
     return jnp.where(wall, faces.mirror(t), take(select_rows(onehot_local, t), index))
 
 
-def pack_kernel(state_ref, final_ref, send_ref, ext_ref, perm_ref,
-                out_ref, q_ref, w_ref, t_ref, lam_ref, send_slots_ref, back_slots_ref, inverse_ref):
+def pack_kernel(state_hbm, final_hbm, send_hbm, ext_hbm, perm_hbm,
+                out_ref, q_ref, w_ref, t_ref, lam_ref, send_slots_ref, back_slots_ref, inverse_ref,
+                send_ref, ext_ref, perm_ref, state_ref, final_ref, sems):
+    pairs = ((send_hbm, send_ref), (ext_hbm, ext_ref), (perm_hbm, perm_ref), (final_hbm, final_ref), (state_hbm, state_ref))
+    copies = [pltpu.make_async_copy(a, b, sems.at[i]) for i, (a, b) in enumerate(pairs)]
+    for copy in copies:
+        copy.start()
     faces = Faces()
+    for copy in copies[:3]:
+        copy.wait()
+    send, _, ext_row = peer_tables(send_ref, ext_ref)
+    send_slots = slots_from_columns(slot_column(send))
+    back_slots = slots_from_faces(ext_row)
+    send_slots_ref[...] = send_slots
+    back_slots_ref[...] = back_slots
+    _, inverse = orientation(column_of(perm_ref))
+    inverse_ref[...] = inverse
+    for copy in copies[3:]:
+        copy.wait()
     q = to_tiles(state_ref)
     w = to_tiles(final_ref)
     store_tiles(q_ref, q)
@@ -366,16 +398,9 @@
     lam = lift_factor * traces(w)
     t_ref[...] = t
     lam_ref[...] = lam
-    send, _, ext_row = peer_tables(send_ref, ext_ref)
-    send_slots = slots_from_columns(slot_column(send))
-    back_slots = slots_from_faces(ext_row)
-    send_slots_ref[...] = send_slots
-    back_slots_ref[...] = back_slots
-    _, inverse = orientation(column_of(perm_ref))
-    inverse_ref[...] = inverse
     y = take(lam, inverse)
-    diagonal = jnp.where(faces.normal, -faces.sign * y, 0.0)
-    first = y - 0.5 * faces.flux_back(jnp.zeros_like(y), y) + turn(diagonal, 64)
+    diagonal = by_axis(lambda a, y: signed(-faces.normal[a] * y), y)
+    first = y - 0.5 * faces.rest_back(y) + turn(diagonal, 64)
     stack = jnp.concatenate([x.astype(bf16) for x in (first, faces.hessian(1, y), faces.hessian(2, y))], axis=1)
     back = dot(back_slots, stack)
     forward = dot(send_slots, packed(t))
@@ -436,7 +461,7 @@
     bar = jnp.where(kind == 1, 0.0, lam - 0.5 * faces.flux_back(x1, lam))
     total = 0.5 * faces.flux_back(t1, lam) - lam + jnp.where(wall, faces.mirror(bar), 0.0)
     total = total + select_rows(local_back_ref[...], take(bar, inverse))
-    lane = lanes(F)
+    lane = lanes()
     sent = t1.astype(bf16).astype(f32)
     h1, h2 = sums[:, 128:256], sums[:, 256:]
     _, index1 = faces.shifted(1)
@@ -445,8 +470,8 @@
     _, index4 = faces.shifted(4)
     through = sums[:, :128] + h1 * take(sent, index1) + h2 * take(sent, index2)
     through = through + take(h1, index4) * take(sent, index4) + take(h2, index3) * take(sent, index3)
-    through = through + jnp.where((lane >= 16) & (lane < 64), turn(sums[:, :128], 64) * sent, 0.0)
-    total = total + jnp.where(lane < 80, through, 0.0)
+    through = through + mask((lane >= 16) & (lane < 64)) * turn(sums[:, :128], 64) * sent
+    total = total + mask(lane < 80) * through
     inner = volume_back(q1, z_ref[...])
     faced = lifted(total)
     w = load_tiles(w_ref)
@@ -528,10 +553,12 @@
     return jax.ShapeDtypeStruct(dims, dtype)
 
 
-def call(kernel, outs, *args):
+def call(kernel, outs, *args, scratch=(), in_hbm=False):
     return pl.pallas_call(
         kernel,
         out_shape=outs,
+        in_specs=[pl.BlockSpec(memory_space=pl.ANY if in_hbm else pltpu.VMEM)] * len(args),
+        scratch_shapes=scratch,
         cost_estimate=pl.CostEstimate(flops=200_000_000, bytes_accessed=1_000_000, transcendentals=0),
         compiler_params=pltpu.CompilerParams(vmem_limit_bytes=32 * 1024 * 1024),
     )(*args)
@@ -559,11 +586,13 @@
     face = shape(F, 128)
     index_face = shape(F, 128, dtype=i32)
 
-    out, q, w, t, lam, send_slots, back_slots, inverse = call(
+    out, q, w, t, lam, send_slots, back_slots, inverse, send_slot, ext_index, ext_perm = call(
         pack_kernel,
         (shape(8, 3, 16, 384, dtype=bf16), node, node, face, face,
-         shape(S, F, dtype=bf16), shape(S, F, dtype=bf16), index_face),
-        state, adjoint_final, send_slot, ext_index, ext_perm)
+         shape(S, F, dtype=bf16), shape(S, F, dtype=bf16), index_face,
+         shape(1, S, dtype=i32), shape(6, E, dtype=i32), shape(6, E, dtype=i32)),
+        *[pltpu.with_memory_space_constraint(x, pltpu.HBM) for x in (state, adjoint_final, send_slot, ext_index, ext_perm)], in_hbm=True,
+        scratch=[pltpu.VMEM((5, E, 64), f32), pltpu.VMEM((5, E, 64), f32), pltpu.SemaphoreType.DMA((5,))])
     arrived = all_peers(out)
     base, z, from_slots, to_columns, local, local_back, index, kind = call(
         first_local_kernel,

time: 70.2 us -> 67 us (0.954)
  local copies, waits for them, and re-layouts: 3.86 us -> 0.04 us
  Pallas kernels: 8.01 us -> 8.77 us
    unnamed x14 -> x4, local copies, waits for them, and re-layouts: 3.83 us -> 0.01 us
    pallas_call x5, Pallas kernels: 8.01 us -> 8.77 us  [call(): pl.pallas_call(kernel, out_shape=outs, in_specs=[pl.BlockSpec(memory_spac...]
  transfers between devices with their start and end apart: 4 -> 4, of which waited for: 0 -> 0; matrix products, arithmetic and copies ran while one was open for 0% -> 0% of each run, Pallas kernels for 3% -> 4%
where the time goes in v3:
time: 67 us; the launch traced here: 66.7 us
  starting transfers between devices  29.1 us (43%)
  blocking collectives  28 us (42%)
  Pallas kernels  8.77 us (13%)
  between operations  0.73 us (1%)
    all_to_all x2, blocking collectives, all_peers(): return lax.all_to_all(whole, 'sub', split_axis=0, concat_axis=0, tiled=True)  28 us
    ppermute x2, starting transfers between devices, chip_partner(): lax.ppermute(value, 'dom', [(d, d ^ 1) for d in range(lax.axis_size('dom'...  19.3 us
    ppermute x2, starting transfers between devices, next_partner(): return lax.ppermute(value, 'dom', pairs)  9.78 us
    pallas_call x5, Pallas kernels, call(): pl.pallas_call(kernel, out_shape=outs, in_specs=[pl.BlockSpec(memory_spac...  8.77 us
  transfers between devices with their start and end apart: 4, of which 0 were waited for; matrix products, arithmetic and copies ran while one was open for 0% of the time, Pallas kernels for 4%

profile of v3, /device:TPU:1, one launch (start us, length us, event | category | flops | bytes accessed | tf_op | source)
XLA Modules:
  0.0 66.7 jit_solution(16772454278566520183)
XLA Ops:
  0.6 2.1 %shard_map.86 = (bf16[8,3,16,384]{3,2,1,0:T(8,128)(2,1)S(1)}, f32[32,384]{1,0:T(8,128)S(1)}, f32[32,384]{1,0:T(8,128)S(1)}, f32[192,128]{1,0:T(8,128)S(1)}, f32[...) custom-call(f32[5,32,64]{2,1,0:T(8,128)} %bitcast.12, ...), custom_call_target="tpu_custom_call" | custom-call | flops 200000000 | bytes 1000000 | tf_op jit(solution)/shard_map/pallas_call | solution.py:557
  2.7 17.1 %all_to_all.10.own_ref = bf16[8,3,16,384]{3,2,1,0:T(8,128)(2,1)S(1)} all-to-all(bf16[8,3,16,384]{3,2,1,0:T(8,128)(2,1)S(1)} %get-tuple-element.40), channel_id=1, replica_groups=mesh['dom'=96,'sub'=8] {'sub'}, dimensions={0} | all-to-all | bytes 589824 | tf_op jit(solution)/shard_map/all_to_all | solution.py:568
  19.9 0.0 copy-start
  19.9 0.0 copy-start.1
  19.9 7.9 %collective-permute-start.1 = (bf16[8,16,384]{2,1,0:T(8,128)(2,1)S(1)}, bf16[8,16,384]{2,1,0:T(8,128)(2,1)S(1)}, u32[]{:S(2)}, u32[]{:S(2)}) collective-permute-start(bf16[8,16,384]{2,1,0:T(8,128)(2,1)S(1)} %get-tuple-element.60), channel_id=1, source_target_pairs={{0,760},{8,16},{16,8},{24,32},{32,24},{40,48},{48,40},{56,64},{64,... | collective-permute-start | bytes 294920 | tf_op jit(solution)/shard_map/ppermute | solution.py:574
  27.8 12.2 %collective-permute-start = (bf16[8,16,384]{2,1,0:T(8,128)(2,1)S(1)}, bf16[8,16,384]{2,1,0:T(8,128)(2,1)S(1)}, u32[]{:S(2)}, u32[]{:S(2)}) collective-permute-start(bf16[8,16,384]{2,1,0:T(8,128)(2,1)S(1)} %get-tuple-element.61), channel_id=1, source_target_pairs={{0,8},{8,0},{16,24},{24,16},{32,40},{40,32},{48,56},{56,48},{64,72... | collective-permute-start | bytes 294920 | tf_op jit(solution)/shard_map/ppermute | solution.py:578
  40.0 0.0 copy-done
  40.0 0.0 copy-done.1
  40.0 0.9 %shard_map.87 = (f32[32,384]{1,0:T(8,128)S(1)}, f32[96,384]{1,0:T(8,128)S(1)}, bf16[192,384]{1,0:T(8,128)(2,1)S(1)}, bf16[192,384]{1,0:T(8,128)(2,1)S(1)}, bf16[...) custom-call(f32[32,384]{1,0:T(8,128)S(1)} %get-tuple-element.31.q_ref, ...), custom_call_target="tpu_custom_call" | custom-call | flops 200000000 | bytes 1000000 | tf_op jit(solution)/shard_map/pallas_call | solution.py:557
  40.9 0.0 collective-permute-done.1.next_ref
  40.9 0.0 collective-permute-done.chip_ref
  41.0 2.7 %shard_map.88 = (bf16[8,4,16,128]{3,2,1,0:T(8,128)(2,1)S(1)}, f32[32,384]{1,0:T(8,128)S(1)}, f32[32,384]{1,0:T(8,128)S(1)}, f32[192,128]{1,0:T(8,128)S(1)}, f32[...) custom-call(f32[32,384]{1,0:T(8,128)S(1)} %get-tuple-element.37.base_ref, f32[32,384]{1,0:T(8,128)S(1)} %get-tuple-element.32.w_ref, ...), custom_call_target="tpu_custom_call" | custom-call | flops 200000000 | bytes 1000000 | tf_op jit(solution)/shard_map/pallas_call | solution.py:557
  43.6 10.9 %all_to_all.11.own_ref = bf16[8,4,16,128]{3,2,1,0:T(8,128)(2,1)S(1)} all-to-all(bf16[8,4,16,128]{3,2,1,0:T(8,128)(2,1)S(1)} %get-tuple-element.57), channel_id=1, replica_groups=mesh['dom'=96,'sub'=8] {'sub'}, dimensions={0} | all-to-all | bytes 262144 | tf_op jit(solution)/shard_map/all_to_all | solution.py:568
  54.5 1.9 %collective-permute-start.3 = (bf16[8,2,16,128]{3,2,1,0:T(8,128)(2,1)S(1)}, bf16[8,2,16,128]{3,2,1,0:T(8,128)(2,1)S(1)}, u32[]{:S(2)}, u32[]{:S(2)}) collective-permute-start(bf16[8,2,16,128]{3,2,1,0:T(8,128)(2,1)S(1)} %get-tuple-element.62), channel_id=1, source_target_pairs={{0,760},{8,16},{16,8},{24,32},{32,24},{40,48},{48,40},{56,64},{64,... | collective-permute-start | bytes 196616 | tf_op jit(solution)/shard_map/ppermute | solution.py:574
  56.4 7.1 %collective-permute-start.2 = (bf16[8,2,16,128]{3,2,1,0:T(8,128)(2,1)S(1)}, bf16[8,2,16,128]{3,2,1,0:T(8,128)(2,1)S(1)}, u32[]{:S(2)}, u32[]{:S(2)}) collective-permute-start(bf16[8,2,16,128]{3,2,1,0:T(8,128)(2,1)S(1)} %get-tuple-element.63), channel_id=1, source_target_pairs={{0,8},{8,0},{16,24},{24,16},{32,40},{40,32},{48,56},{56,48},{64,72... | collective-permute-start | bytes 196616 | tf_op jit(solution)/shard_map/ppermute | solution.py:578
  63.5 1.6 %shard_map.89 = (f32[32,384]{1,0:T(8,128)S(1)}, f32[32,384]{1,0:T(8,128)S(1)}) custom-call(f32[32,384]{1,0:T(8,128)S(1)} %get-tuple-element.31.q_ref, f32[32,384]{1,0:T(8,128)S(1)} %get-tuple-element.32.w_ref, f32[192,128]{1,0:T(8,128)S(1)} %get-tuple-element.33.t_ref, f32[32,384]{1,0:T(8,128)S(1)} %get-tuple-element.50.q1_ref, ...), custom_call_target="tpu_custom_call" | custom-call | flops 200000000 | bytes 1000000 | tf_op jit(solution)/shard_map/pallas_call | solution.py:557
  65.1 0.0 collective-permute-done.3.next_ref
  65.1 0.0 collective-permute-done.2.chip_ref
  65.1 1.5 %shard_map.90 = (f32[5,32,64]{2,1,0:T(8,128)}, f32[5,32,64]{2,1,0:T(8,128)}) custom-call(f32[32,384]{1,0:T(8,128)S(1)} %get-tuple-element.55.end_base_ref, f32[32,384]{1,0:T(8,128)S(1)} %get-tuple-element.56.start_base_ref, bf16[8,2,16,128]{3,2,1,0:T(8,128)(2,1)S(1)} %collective-permute-done.2.chip_ref, bf16[8,4,16,128]{3,2,1,0:T(8,128)(2,1)S(1)} %all_to_all.11.own_ref, ...), custom_call_target="tpu_custom_call" | custom-call | flops 200000000 | bytes 1000000 | tf_op jit(solution)/shard_map/pallas_call | solution.py:557
  (2 shorter events, 0.0 us)
Async XLA Ops:
  19.9 20.1 %copy-start = (bf16[128,768]{1,0:T(8,128)(2,1)S(1)}, bf16[128,768]{1,0:T(8,128)(2,1)}, u32[]{:S(2)}) copy-start(bf16[128,768]{1,0:T(8,128)(2,1)} %constant.5.clone.backward_ref) | copy-start | bytes 589828
  19.9 20.2 %copy-start.1 = (bf16[384,256]{1,0:T(8,128)(2,1)S(1)}, bf16[384,256]{1,0:T(8,128)(2,1)}, u32[]{:S(2)}) copy-start(bf16[384,256]{1,0:T(8,128)(2,1)} %constant.4.clone.forward_ref) | copy-start | bytes 589828
  19.9 21.0 %collective-permute-start.1 = (bf16[8,16,384]{2,1,0:T(8,128)(2,1)S(1)}, bf16[8,16,384]{2,1,0:T(8,128)(2,1)S(1)}, u32[]{:S(2)}, u32[]{:S(2)}) collective-permute-start(bf16[8,16,384]{2,1,0:T(8,128)(2,1)S(1)} %get-tuple-element.60), channel_id=1, source_target_pairs={{0,760},{8,16},{16,8},{24,32},{32,24},{40,48},{48,40},{56,64},{64,... | collective-permute-start | bytes 294920 | tf_op jit(solution)/shard_map/ppermute | solution.py:574
  27.8 13.2 %collective-permute-start = (bf16[8,16,384]{2,1,0:T(8,128)(2,1)S(1)}, bf16[8,16,384]{2,1,0:T(8,128)(2,1)S(1)}, u32[]{:S(2)}, u32[]{:S(2)}) collective-permute-start(bf16[8,16,384]{2,1,0:T(8,128)(2,1)S(1)} %get-tuple-element.61), channel_id=1, source_target_pairs={{0,8},{8,0},{16,24},{24,16},{32,40},{40,32},{48,56},{56,48},{64,72... | collective-permute-start | bytes 294920 | tf_op jit(solution)/shard_map/ppermute | solution.py:578
  54.5 10.6 %collective-permute-start.3 = (bf16[8,2,16,128]{3,2,1,0:T(8,128)(2,1)S(1)}, bf16[8,2,16,128]{3,2,1,0:T(8,128)(2,1)S(1)}, u32[]{:S(2)}, u32[]{:S(2)}) collective-permute-start(bf16[8,2,16,128]{3,2,1,0:T(8,128)(2,1)S(1)} %get-tuple-element.62), channel_id=1, source_target_pairs={{0,760},{8,16},{16,8},{24,32},{32,24},{40,48},{48,40},{56,64},{64,... | collective-permute-start | bytes 196616 | tf_op jit(solution)/shard_map/ppermute | solution.py:574
  56.4 8.7 %collective-permute-start.2 = (bf16[8,2,16,128]{3,2,1,0:T(8,128)(2,1)S(1)}, bf16[8,2,16,128]{3,2,1,0:T(8,128)(2,1)S(1)}, u32[]{:S(2)}, u32[]{:S(2)}) collective-permute-start(bf16[8,2,16,128]{3,2,1,0:T(8,128)(2,1)S(1)} %get-tuple-element.63), channel_id=1, source_target_pairs={{0,8},{8,0},{16,24},{24,16},{32,40},{40,32},{48,56},{56,48},{64,72... | collective-permute-start | bytes 196616 | tf_op jit(solution)/shard_map/ppermute | solution.py:578

commit v4 on v3

--- a/solution.py
+++ b/solution.py
@@ -195,18 +195,24 @@
     n = lane & 63
     i, j, k = n >> 4, (n >> 2) & 3, n & 3
     places = (4 * j + k, 4 * i + k, 4 * i + j)
-    layers = ((wide >> 4) & 3, (wide >> 2) & 3, wide & 3)
-    tiles = []
-    for tile in range(3):
-        v = 2 * tile + (lane >> 6)
-        total = None
-        for a in range(3):
+    layers = (i, j, k)
+    wide_layers = ((wide >> 4) & 3, (wide >> 2) & 3, wide & 3)
+    tiles = [None] * 3
+    for a in range(3):
+        first, last = x[64 * a : 64 * a + 32], turn(x[64 * a + 32 : 64 * a + 64], 64)
+        pair = jnp.where(wide < 64, first, last)
+        tail = jnp.where(wide < 16, last, first)
+        ends = (wide_layers[a] == 0) | (wide_layers[a] == 3)
+        for tile in range(3):
+            v = 2 * tile + (lane >> 6)
             index = v * 16 + places[a]
-            first = take(x[64 * a : 64 * a + 32], index)
-            last = take(x[64 * a + 32 : 64 * a + 64], index)
-            part = jnp.where(layers[a] == 0, first, jnp.where(layers[a] == 3, last, 0.0))
-            total = part if total is None else total + part
-        tiles.append(total)
+            at_last = jnp.where(layers[a] == 3, 64, 0)
+            if tile < 2:
+                part = take(pair, index + at_last)
+            else:
+                part = take(tail, jnp.where(lane < 64, index - at_last, 80))
+            part = jnp.where(ends, part, 0.0)
+            tiles[tile] = part if tiles[tile] is None else tiles[tile] + part
     return tiles
 
 
@@ -230,24 +236,30 @@
         self.normal_index = [(a + 1) * 16 + self.m for a in range(3)]
         self.pressure_index = 64 + self.m
 
-    def flux(self, x):
-        def along(a, x):
-            u = take(x, self.normal_index[a])
-            p = take(x, self.pressure_index)
+    def normal_of(self, x):
+        return by_axis(lambda a, x: take(x, self.normal_index[a]), x)
+
+    def pressure_of(self, x):
+        return take(x, self.pressure_index)
+
+    def flux(self, x, u=None, p=None):
+        u = self.normal_of(x) if u is None else u
+        p = self.pressure_of(x) if p is None else p
+
+        def along(a, x, u, p):
             c = u + mean_flow if a == 0 else u
             return signed(c * x + self.ends * u + self.normal[a] * p)
 
-        return by_axis(along, x)
-
-    def flux_back(self, x, w):
-        def along(a, x, w):
-            u = take(x, self.normal_index[a])
+        return by_axis(along, x, u, p)
+
+    def flux_back(self, x, u, w):
+        def along(a, x, u, w):
             n = take(w, self.normal_index[a])
             c = u + mean_flow if a == 0 else u
             h = over_fields((x + self.ends) * w)
             return signed(c * w + self.last * n + self.normal[a] * h)
 
-        return by_axis(along, x, w)
+        return by_axis(along, x, u, w)
 
     def rest_back(self, w):
         def along(a, w):
@@ -258,6 +270,12 @@
 
         return by_axis(along, w)
 
+    def state_back(self, x, u, w):
+        def along(a, x, u, w):
+            return signed(u * w + self.normal[a] * over_fields(x * w))
+
+        return by_axis(along, x, u, w)
+
     def shifted(self, d):
         target = self.v + d
         target = jnp.where(target >= 5, target - 5, target)
@@ -277,9 +295,10 @@
 
 
 def over_fields(h):
-    h = h + turn(h, 16)
-    h = h + turn(h, 32)
-    return h + turn(h, 64)
+    table = ((lax.broadcasted_iota(i32, (128, 128), 0) ^ lax.broadcasted_iota(i32, (128, 128), 1)) & 15) == 0
+    table = mask(table).astype(bf16)
+    hi, lo = halves(h)
+    return dot(jnp.concatenate([hi, lo], axis=1), jnp.concatenate([table, table], axis=0))
 
 
 def column_of(table_ref):
@@ -360,15 +379,16 @@
     return jnp.concatenate([first, second], axis=1).astype(bf16)
 
 
-def unpacked(g):
-    lane = lanes(F)
-    first = jnp.where(lane < 48, turn(g[:, :128], 48), 0.0)
-    second = jnp.where((lane >= 48) & (lane < 80), turn(g[:, 128:256], 96), 0.0)
-    return first + second
-
-
-def exterior(faces, wall, index, onehot_local, t):
-    return jnp.where(wall, faces.mirror(t), take(select_rows(onehot_local, t), index))
+def exterior(faces, wall, index, onehot_local, t, u):
+    g = select_rows(onehot_local, t)
+    node = index & 15
+    x = jnp.where(wall, faces.mirror(t), take(g, index))
+    v = by_axis(lambda a, g, node: take(g, (a + 1) * 16 + node), g, node)
+    return x, jnp.where(wall, -u, v)
+
+
+def block_of(ref, row):
+    return ref[:, row : row + 16].reshape(G, 128)
 
 
 def pack_kernel(state_hbm, final_hbm, send_hbm, ext_hbm, perm_hbm,
@@ -408,11 +428,14 @@
     for o in range(3):
         for peer in range(8):
             at = G * o + 16 * peer
-            out_ref[peer, o] = whole[at : at + 16]
-
-
-def first_local_kernel(q_ref, w_ref, t_ref, send_ref, ext_ref, perm_ref, forward_ref, backward_ref,
-                       base_ref, z_ref, from_slots_ref, to_columns_ref, local_ref, local_back_ref, index_ref, kind_ref):
+            for j in range(3):
+                row = 48 * o + 16 * j
+                out_ref[peer, row : row + 16] = whole[at : at + 16, 128 * j : 128 * (j + 1)]
+
+
+def first_local_kernel(q_ref, w_ref, t_ref, lam_ref, send_ref, ext_ref, perm_ref, forward_ref, backward_ref,
+                       base_ref, z_ref, rest_ref, from_slots_ref, to_columns_ref, local_ref, local_back_ref,
+                       index_ref, kind_ref):
     faces = Faces()
     send, ext_col, ext_row = peer_tables(send_ref, ext_ref)
     index, _ = orientation(column_of(perm_ref))
@@ -427,50 +450,64 @@
     local_back_ref[...] = columns_from_faces(ext_row)
     q = load_tiles(q_ref)
     t = t_ref[...]
-    x = exterior(faces, wall, index, local, t)
-    jump = 0.5 * (faces.flux(t) - faces.flux(x)) + (x - t)
+    lam = lam_ref[...]
+    rest_ref[...] = lam - 0.5 * faces.rest_back(lam)
+    u = faces.normal_of(t)
+    x, v = exterior(faces, wall, index, local, t, u)
+    jump = 0.5 * (faces.flux(t, u) - faces.flux(x, v)) + (x - t)
     faced = lifted(lift_factor * jump)
     inner = volume(q, forward_ref[...])
     store_tiles(base_ref, [q[j] + step_size * (inner[j] + faced[j]) for j in range(3)])
     z_ref[...] = derivative_back(load_tiles(w_ref), backward_ref[...])
 
 
-def middle_kernel(base_ref, w_ref, lam_ref, z_ref, chip_ref, own_ref, next_ref,
+def middle_kernel(base_ref, w_ref, lam_ref, rest_ref, z_ref, chip_ref, own_ref, next_ref,
                   from_slots_ref, to_columns_ref, local_ref, local_back_ref, send_slots_ref, back_slots_ref,
                   index_ref, inverse_ref, kind_ref,
-                  out_ref, q1_ref, w1_ref, t1_ref, x1_ref, lam1_ref):
+                  out_ref, q1_ref, w1_ref, t1_ref, u1_ref, x1_ref, v1_ref, lam1_ref):
     faces = Faces()
     index = index_ref[...]
     inverse = inverse_ref[...]
     kind = kind_ref[...]
     wall = kind == 2
+    wide = lanes(F)
+    lane = lanes()
+    node = index & 15
     arrived = jnp.concatenate(
-        [chip_ref[...].reshape(G, 384), own_ref[:, 1].reshape(G, 384), next_ref[...].reshape(G, 384)], axis=0)
-    xr = take(unpacked(dot(from_slots_ref[...], arrived[:, 128:])), index)
+        [jnp.concatenate([block_of(ref, at + 16 * j) for j in range(3)], axis=1)
+         for ref, at in ((chip_ref, 0), (own_ref, 48), (next_ref, 0))], axis=0)
+    g = dot(from_slots_ref[...], arrived[:, 128:])
     sums = dot(to_columns_ref[...], arrived)
-    faced = lifted((lift_factor * step_size) * (xr - 0.5 * faces.flux(xr)))
+    g0, g1 = g[:, :128], g[:, 128:]
+    place = jnp.where(wide < 48, index + 80, jnp.where(wide < 80, index + 32, 112 + node))
+    xr = jnp.where(wide < 48, take(g0, place), take(g1, place))
+    ur = jnp.concatenate(
+        [take(g0[:64], 96 + node[:64]), take(g0[64:128], 112 + node[64:128]), take(g1[128:], 80 + node[128:])], axis=0)
+    pr = take(g1, 96 + node)
+    faced = lifted((lift_factor * step_size) * (xr - 0.5 * faces.flux(xr, ur, pr)))
     base = load_tiles(base_ref)
     q1 = [base[j] + faced[j] for j in range(3)]
     store_tiles(q1_ref, q1)
     t1 = traces(q1)
     t1_ref[...] = t1
-    forward = dot(send_slots_ref[...], packed(t1))
+    t1_sent = t1.astype(bf16)
+    forward = dot(send_slots_ref[...], t1_sent)
     lam = lam_ref[...]
-    x1 = exterior(faces, wall, index, local_ref[...], t1)
+    rest = rest_ref[...]
+    u1 = faces.normal_of(t1)
+    u1_ref[...] = u1
+    x1, v1 = exterior(faces, wall, index, local_ref[...], t1, u1)
     x1_ref[...] = x1
-    bar = jnp.where(kind == 1, 0.0, lam - 0.5 * faces.flux_back(x1, lam))
-    total = 0.5 * faces.flux_back(t1, lam) - lam + jnp.where(wall, faces.mirror(bar), 0.0)
+    v1_ref[...] = v1
+    bar = jnp.where(kind == 1, 0.0, rest - 0.5 * faces.state_back(x1, v1, lam))
+    total = 0.5 * faces.state_back(t1, u1, lam) - rest + jnp.where(wall, faces.mirror(bar), 0.0)
     total = total + select_rows(local_back_ref[...], take(bar, inverse))
-    lane = lanes()
-    sent = t1.astype(bf16).astype(f32)
-    h1, h2 = sums[:, 128:256], sums[:, 256:]
-    _, index1 = faces.shifted(1)
-    _, index2 = faces.shifted(2)
-    _, index3 = faces.shifted(3)
-    _, index4 = faces.shifted(4)
-    through = sums[:, :128] + h1 * take(sent, index1) + h2 * take(sent, index2)
-    through = through + take(h1, index4) * take(sent, index4) + take(h2, index3) * take(sent, index3)
-    through = through + mask((lane >= 16) & (lane < 64)) * turn(sums[:, :128], 64) * sent
+    sent = t1_sent.astype(f32)
+    h0, h1, h2 = sums[:, :128], sums[:, 128:256], sums[:, 256:]
+    ahead1, ahead2, behind2, behind1 = [faces.shifted(d)[1] for d in (1, 2, 3, 4)]
+    through = h0 + h1 * take(sent, ahead1) + h2 * take(sent, ahead2)
+    through = through + take(h1 * sent, behind1) + take(h2 * sent, behind2)
+    through = through + mask((lane >= 16) & (lane < 64)) * turn(h0, 64) * sent
     total = total + mask(lane < 80) * through
     inner = volume_back(q1, z_ref[...])
     faced = lifted(total)
@@ -479,20 +516,22 @@
     store_tiles(w1_ref, w1)
     lam1 = lift_factor * traces(w1)
     lam1_ref[...] = lam1
-    y = take(lam1 - 0.5 * faces.flux_back(xr, lam1), inverse)
-    back = dot(back_slots_ref[...], y.astype(bf16))
-    main = (back + forward[:, :128]).astype(bf16)
-    tail = [turn(forward[G * o : G * (o + 1), 128:], 48 + 32 * o) for o in range(3)]
-    shared = (tail[0] + tail[1] + tail[2]).astype(bf16)
+    bar = lam1 - 0.5 * faces.flux_back(xr, ur, lam1)
+    first = take(bar, jnp.where(wide >= 80, inverse - 80, 80))
+    second = take(bar, jnp.where(wide < 32, inverse + 48, 80))
+    back = dot(back_slots_ref[...], jnp.concatenate([first, second], axis=1).astype(bf16))
+    main = (back[:, :128] + forward).astype(bf16)
+    tail = [back[G * o : G * (o + 1), 128:] for o in range(3)]
+    shared = (tail[0] + turn(tail[1], 32) + turn(tail[2], 64)).astype(bf16)
     for peer in range(8):
         at = 16 * peer
-        out_ref[peer, 0] = main[at : at + 16]
-        out_ref[peer, 1] = shared[at : at + 16]
-        out_ref[peer, 2] = main[2 * G + at : 2 * G + at + 16]
-        out_ref[peer, 3] = main[G + at : G + at + 16]
-
-
-def second_local_kernel(q_ref, w_ref, t_ref, q1_ref, w1_ref, t1_ref, x1_ref, lam1_ref,
+        out_ref[peer, :16] = main[at : at + 16]
+        out_ref[peer, 16:32] = shared[at : at + 16]
+        out_ref[peer, 32:48] = main[2 * G + at : 2 * G + at + 16]
+        out_ref[peer, 48:] = main[G + at : G + at + 16]
+
+
+def second_local_kernel(q_ref, w_ref, t_ref, q1_ref, w1_ref, t1_ref, u1_ref, x1_ref, v1_ref, lam1_ref,
                         local_ref, local_back_ref, index_ref, inverse_ref, kind_ref,
                         forward_ref, backward_ref, end_ref, start_ref):
     faces = Faces()
@@ -504,15 +543,17 @@
     q1 = load_tiles(q1_ref)
     t1 = t1_ref[...]
     x1 = x1_ref[...]
-    jump = 0.5 * (faces.flux(t1) - faces.flux(x1)) + (x1 - t1)
+    jump = 0.5 * (faces.flux(t1, u1_ref[...]) - faces.flux(x1, v1_ref[...])) + (x1 - t1)
     faced = lifted(lift_factor * jump)
     inner = volume(q1, forward_ref[...])
     store_tiles(end_ref, [0.5 * q[j] + 0.5 * (q1[j] + step_size * (inner[j] + faced[j])) for j in range(3)])
     t = t_ref[...]
     lam1 = lam1_ref[...]
-    x = exterior(faces, wall, index, local_ref[...], t)
-    bar = jnp.where(kind == 1, 0.0, lam1 - 0.5 * faces.flux_back(x, lam1))
-    total = 0.5 * faces.flux_back(t, lam1) - lam1 + jnp.where(wall, faces.mirror(bar), 0.0)
+    u = faces.normal_of(t)
+    x, v = exterior(faces, wall, index, local_ref[...], t, u)
+    rest = lam1 - 0.5 * faces.rest_back(lam1)
+    bar = jnp.where(kind == 1, 0.0, rest - 0.5 * faces.state_back(x, v, lam1))
+    total = 0.5 * faces.state_back(t, u, lam1) - rest + jnp.where(wall, faces.mirror(bar), 0.0)
     total = total + select_rows(local_back_ref[...], take(bar, inverse))
     w = load_tiles(w_ref)
     w1 = load_tiles(w1_ref)
@@ -524,26 +565,26 @@
 def last_kernel(end_base_ref, start_base_ref, chip_ref, own_ref, next_ref, from_slots_ref, to_columns_ref, index_ref,
                 end_ref, start_ref):
     faces = Faces()
-    main = jnp.concatenate(
-        [chip_ref[:, 0].reshape(G, 128), own_ref[:, 3].reshape(G, 128), next_ref[:, 1].reshape(G, 128)], axis=0)
+    main = jnp.concatenate([block_of(chip_ref, 0), block_of(own_ref, 48), block_of(next_ref, 16)], axis=0)
     lane = lanes(G)
     zero = jnp.zeros((G, 128), bf16)
     shared = jnp.concatenate([
-        jnp.where(lane < 32, chip_ref[:, 1].reshape(G, 128), zero),
-        jnp.where((lane >= 32) & (lane < 64), own_ref[:, 1].reshape(G, 128), zero),
-        jnp.where((lane >= 64) & (lane < 96), next_ref[:, 0].reshape(G, 128), zero)], axis=0)
-    g = dot(from_slots_ref[...], jnp.concatenate([main, shared], axis=1))
-    lane = lanes(F)
-    x = jnp.where(lane < 48, turn(g[:, :128], 48), 0.0)
-    high = g[:, 128:]
-    high = turn(high, 48) + turn(high, 16) + turn(high, 112)
-    x = x + jnp.where((lane >= 48) & (lane < 80), high, 0.0)
-    xr = take(x, index_ref[...])
-    faced = lifted((0.5 * step_size * lift_factor) * (xr - 0.5 * faces.flux(xr)))
+        jnp.where(lane < 32, block_of(chip_ref, 16), zero),
+        jnp.where((lane >= 32) & (lane < 64), block_of(own_ref, 16), zero),
+        jnp.where((lane >= 64) & (lane < 96), block_of(next_ref, 0), zero)], axis=0)
+    node = index_ref[...] & 15
+    g = dot(from_slots_ref[...], main)
+    b = dot(to_columns_ref[...], jnp.concatenate([main, shared], axis=1))
+    lane = lanes()
+    valid = mask(lane < 80)
+    xr = valid * take(g, index_ref[...])
+    ur = by_axis(lambda a, g, node: take(g, (a + 1) * 16 + node), g, node)
+    pr = take(g, 64 + node)
+    faced = lifted((0.5 * step_size * lift_factor) * (xr - 0.5 * faces.flux(xr, ur, pr)))
     base = load_tiles(end_base_ref)
     from_tiles([base[j] + faced[j] for j in range(3)], end_ref)
-    bar = dot(to_columns_ref[...], main)
-    bar = jnp.where(lane < 80, bar, 0.0)
+    high = turn(b[:, 128:], 48) + turn(b[:, 128:], 16) + turn(b[:, 128:], 112)
+    bar = mask(lane < 48) * turn(b[:, :128], 48) + mask((lane >= 48) & (lane < 80)) * high
     faced = lifted(step_size * bar)
     base = load_tiles(start_base_ref)
     from_tiles([base[j] + faced[j] for j in range(3)], start_ref)
@@ -588,29 +629,29 @@
 
     out, q, w, t, lam, send_slots, back_slots, inverse, send_slot, ext_index, ext_perm = call(
         pack_kernel,
-        (shape(8, 3, 16, 384, dtype=bf16), node, node, face, face,
+        (shape(8, 144, 128, dtype=bf16), node, node, face, face,
          shape(S, F, dtype=bf16), shape(S, F, dtype=bf16), index_face,
          shape(1, S, dtype=i32), shape(6, E, dtype=i32), shape(6, E, dtype=i32)),
         *[pltpu.with_memory_space_constraint(x, pltpu.HBM) for x in (state, adjoint_final, send_slot, ext_index, ext_perm)], in_hbm=True,
         scratch=[pltpu.VMEM((5, E, 64), f32), pltpu.VMEM((5, E, 64), f32), pltpu.SemaphoreType.DMA((5,))])
     arrived = all_peers(out)
-    base, z, from_slots, to_columns, local, local_back, index, kind = call(
+    base, z, rest, from_slots, to_columns, local, local_back, index, kind = call(
         first_local_kernel,
-        (node, shape(96, 384), shape(F, S, dtype=bf16), shape(F, S, dtype=bf16),
+        (node, shape(96, 384), face, shape(F, S, dtype=bf16), shape(F, S, dtype=bf16),
          shape(F, F, dtype=bf16), shape(F, F, dtype=bf16), index_face, index_face),
-        q, w, t, send_slot, ext_index, ext_perm, forward, backward)
-    from_next = next_partner(arrived[:, 2])
-    from_chip = chip_partner(arrived[:, 0])
-    out, q1, w1, t1, x1, lam1 = call(
-        middle_kernel, (shape(8, 4, 16, 128, dtype=bf16), node, node, face, face, face),
-        base, w, lam, z, from_chip, arrived, from_next,
+        q, w, t, lam, send_slot, ext_index, ext_perm, forward, backward)
+    from_next = next_partner(arrived[:, 96:])
+    from_chip = chip_partner(arrived[:, :48])
+    out, q1, w1, t1, u1, x1, v1, lam1 = call(
+        middle_kernel, (shape(8, 64, 128, dtype=bf16), node, node, face, face, face, face, face),
+        base, w, lam, rest, z, from_chip, arrived, from_next,
         from_slots, to_columns, local, local_back, send_slots, back_slots, index, inverse, kind)
     arrived = all_peers(out)
     end_base, start_base = call(
         second_local_kernel, (node, node),
-        q, w, t, q1, w1, t1, x1, lam1, local, local_back, index, inverse, kind, forward, backward)
-    from_next = next_partner(arrived[:, 1:3])
-    from_chip = chip_partner(arrived[:, 0:2])
+        q, w, t, q1, w1, t1, u1, x1, v1, lam1, local, local_back, index, inverse, kind, forward, backward)
+    from_next = next_partner(arrived[:, 16:48])
+    from_chip = chip_partner(arrived[:, :32])
     out = shape(5, E, 64)
     end, start = call(
         last_kernel, (out, out),

time: 67 us -> 66.1 us (0.987)
  Pallas kernels: 8.77 us -> 7.97 us
    pallas_call x5, Pallas kernels: 8.77 us -> 7.97 us  [call(): pl.pallas_call(kernel, out_shape=outs, in_specs=[pl.BlockSpec(memory_spac...]
  transfers between devices with their start and end apart: 4 -> 4, of which waited for: 0 -> 0; matrix products, arithmetic and copies ran while one was open for 0% -> 0% of each run, Pallas kernels for 4% -> 3%
where the time goes in v4:
time: 66.1 us; the launch traced here: 65.8 us
  starting transfers between devices  29 us (44%)
  blocking collectives  28.1 us (43%)
  Pallas kernels  7.97 us (12%)
  between operations  0.74 us (1%)
    all_to_all x2, blocking collectives, all_peers(): return lax.all_to_all(whole, 'sub', split_axis=0, concat_axis=0, tiled=True)  28.1 us
    ppermute x2, starting transfers between devices, chip_partner(): lax.ppermute(value, 'dom', [(d, d ^ 1) for d in range(lax.axis_size('dom'...  19.2 us
    ppermute x2, starting transfers between devices, next_partner(): return lax.ppermute(value, 'dom', pairs)  9.78 us
    pallas_call x5, Pallas kernels, call(): pl.pallas_call(kernel, out_shape=outs, in_specs=[pl.BlockSpec(memory_spac...  7.97 us
  transfers between devices with their start and end apart: 4, of which 0 were waited for; matrix products, arithmetic and copies ran while one was open for 0% of the time, Pallas kernels for 3%

profile of v4, /device:TPU:1, one launch (start us, length us, event | category | flops | bytes accessed | tf_op | source)
XLA Modules:
  0.0 65.8 jit_solution(4042902056991968025)
XLA Ops:
  0.6 2.0 %shard_map.86 = (bf16[8,144,128]{2,1,0:T(8,128)(2,1)S(1)}, f32[32,384]{1,0:T(8,128)S(1)}, f32[32,384]{1,0:T(8,128)S(1)}, f32[192,128]{1,0:T(8,128)S(1)}, f32[192...) custom-call(f32[5,32,64]{2,1,0:T(8,128)} %bitcast.4, ...), custom_call_target="tpu_custom_call" | custom-call | flops 200000000 | bytes 1000000 | tf_op jit(solution)/shard_map/pallas_call | solution.py:598
  2.7 17.1 %all_to_all.10.own_ref = bf16[8,144,128]{2,1,0:T(8,128)(2,1)S(1)} all-to-all(bf16[8,144,128]{2,1,0:T(8,128)(2,1)S(1)} %get-tuple-element.44), channel_id=1, replica_groups=mesh['dom'=96,'sub'=8] {'sub'}, dimensions={0} | all-to-all | bytes 589824 | tf_op jit(solution)/shard_map/all_to_all | solution.py:609
  19.8 0.0 copy-start
  19.8 0.0 copy-start.1
  19.8 7.9 %collective-permute-start.1 = (bf16[8,48,128]{2,1,0:T(8,128)(2,1)S(1)}, bf16[8,48,128]{2,1,0:T(8,128)(2,1)S(1)}, u32[]{:S(2)}, u32[]{:S(2)}) collective-permute-start(bf16[8,48,128]{2,1,0:T(8,128)(2,1)S(1)} %get-tuple-element.66), channel_id=1, source_target_pairs={{0,760},{8,16},{16,8},{24,32},{32,24},{40,48},{48,40},{56,64},{64,... | collective-permute-start | bytes 294920 | tf_op jit(solution)/shard_map/ppermute | solution.py:615
  27.7 12.2 %collective-permute-start = (bf16[8,48,128]{2,1,0:T(8,128)(2,1)S(1)}, bf16[8,48,128]{2,1,0:T(8,128)(2,1)S(1)}, u32[]{:S(2)}, u32[]{:S(2)}) collective-permute-start(bf16[8,48,128]{2,1,0:T(8,128)(2,1)S(1)} %get-tuple-element.67), channel_id=1, source_target_pairs={{0,8},{8,0},{16,24},{24,16},{32,40},{40,32},{48,56},{56,48},{64,72... | collective-permute-start | bytes 294920 | tf_op jit(solution)/shard_map/ppermute | solution.py:619
  39.9 0.0 copy-done
  40.0 0.0 copy-done.1
  40.0 0.9 %shard_map.87 = (f32[32,384]{1,0:T(8,128)S(1)}, f32[96,384]{1,0:T(8,128)S(1)}, f32[192,128]{1,0:T(8,128)S(1)}, bf16[192,384]{1,0:T(8,128)(2,1)S(1)}, bf16[192,38...) custom-call(f32[32,384]{1,0:T(8,128)S(1)} %get-tuple-element.34.q_re, ...), custom_call_target="tpu_custom_call" | custom-call | flops 200000000 | bytes 1000000 | tf_op jit(solution)/shard_map/pallas_call | solution.py:598
  40.9 0.0 collective-permute-done.1.next_ref
  40.9 0.0 collective-permute-done.chip_ref
  40.9 2.4 %shard_map.88 = (bf16[8,64,128]{2,1,0:T(8,128)(2,1)S(1)}, f32[32,384]{1,0:T(8,128)S(1)}, f32[32,384]{1,0:T(8,128)S(1)}, f32[192,128]{1,0:T(8,128)S(1)}, f32[192,...) custom-call(f32[32,384]{1,0:T(8,128)S(1)} %get-tuple-element.41.base_ref, ...), custom_call_target="tpu_custom_call" | custom-call | flops 200000000 | bytes 1000000 | tf_op jit(solution)/shard_map/pallas_call | solution.py:598
  43.3 10.9 %all_to_all.11.own_ref = bf16[8,64,128]{2,1,0:T(8,128)(2,1)S(1)} all-to-all(bf16[8,64,128]{2,1,0:T(8,128)(2,1)S(1)} %get-tuple-element.63), channel_id=1, replica_groups=mesh['dom'=96,'sub'=8] {'sub'}, dimensions={0} | all-to-all | bytes 262144 | tf_op jit(solution)/shard_map/all_to_all | solution.py:609
  54.3 1.9 %collective-permute-start.3 = (bf16[8,32,128]{2,1,0:T(8,128)(2,1)S(1)}, bf16[8,32,128]{2,1,0:T(8,128)(2,1)S(1)}, u32[]{:S(2)}, u32[]{:S(2)}) collective-permute-start(bf16[8,32,128]{2,1,0:T(8,128)(2,1)S(1)} %get-tuple-element.68), channel_id=1, source_target_pairs={{0,760},{8,16},{16,8},{24,32},{32,24},{40,48},{48,40},{56,64},{64,... | collective-permute-start | bytes 196616 | tf_op jit(solution)/shard_map/ppermute | solution.py:615
  56.2 7.0 %collective-permute-start.2 = (bf16[8,32,128]{2,1,0:T(8,128)(2,1)S(1)}, bf16[8,32,128]{2,1,0:T(8,128)(2,1)S(1)}, u32[]{:S(2)}, u32[]{:S(2)}) collective-permute-start(bf16[8,32,128]{2,1,0:T(8,128)(2,1)S(1)} %get-tuple-element.69), channel_id=1, source_target_pairs={{0,8},{8,0},{16,24},{24,16},{32,40},{40,32},{48,56},{56,48},{64,72... | collective-permute-start | bytes 196616 | tf_op jit(solution)/shard_map/ppermute | solution.py:619
  63.2 1.2 %shard_map.89 = (f32[32,384]{1,0:T(8,128)S(1)}, f32[32,384]{1,0:T(8,128)S(1)}) custom-call(f32[32,384]{1,0:T(8,128)S(1)} %get-tuple-element.34.q_ref, f32[32,384]{1,0:T(8,128)S(1)} %get-tuple-element.35.w_ref, f32[192,128]{1,0:T(8,128)S(1)} %get-tuple-element.36.t_ref, f32[32,384]{1,0:T(8,128)S(1)} %get-tuple-element.54.q1_ref, ...), custom_call_target="tpu_custom_call" | custom-call | flops 200000000 | bytes 1000000 | tf_op jit(solution)/shard_map/pallas_call | solution.py:598
  64.4 0.0 collective-permute-done.3.next_ref
  64.4 0.0 collective-permute-done.2.chip_ref
  64.4 1.4 %shard_map.90 = (f32[5,32,64]{2,1,0:T(8,128)}, f32[5,32,64]{2,1,0:T(8,128)}) custom-call(f32[32,384]{1,0:T(8,128)S(1)} %get-tuple-element.61.end_base_ref, f32[32,384]{1,0:T(8,128)S(1)} %get-tuple-element.62.start_base_ref, bf16[8,32,128]{2,1,0:T(8,128)(2,1)S(1)} %collective-permute-done.2.chip_ref, bf16[8,64,128]{2,1,0:T(8,128)(2,1)S(1)} %all_to_all.11.own_ref, ...), custom_call_target="tpu_custom_call" | custom-call | flops 200000000 | bytes 1000000 | tf_op jit(solution)/shard_map/pallas_call | solution.py:598
  (2 shorter events, 0.0 us)
Async XLA Ops:
  19.8 20.1 %copy-start = (bf16[128,768]{1,0:T(8,128)(2,1)S(1)}, bf16[128,768]{1,0:T(8,128)(2,1)}, u32[]{:S(2)}) copy-start(bf16[128,768]{1,0:T(8,128)(2,1)} %constant.5.clone.backward_ref) | copy-start | bytes 589828
  19.8 20.2 %copy-start.1 = (bf16[384,256]{1,0:T(8,128)(2,1)S(1)}, bf16[384,256]{1,0:T(8,128)(2,1)}, u32[]{:S(2)}) copy-start(bf16[384,256]{1,0:T(8,128)(2,1)} %constant.4.clone.forward_ref) | copy-start | bytes 589828
  19.8 21.0 %collective-permute-start.1 = (bf16[8,48,128]{2,1,0:T(8,128)(2,1)S(1)}, bf16[8,48,128]{2,1,0:T(8,128)(2,1)S(1)}, u32[]{:S(2)}, u32[]{:S(2)}) collective-permute-start(bf16[8,48,128]{2,1,0:T(8,128)(2,1)S(1)} %get-tuple-element.66), channel_id=1, source_target_pairs={{0,760},{8,16},{16,8},{24,32},{32,24},{40,48},{48,40},{56,64},{64,... | collective-permute-start | bytes 294920 | tf_op jit(solution)/shard_map/ppermute | solution.py:615
  27.7 13.2 %collective-permute-start = (bf16[8,48,128]{2,1,0:T(8,128)(2,1)S(1)}, bf16[8,48,128]{2,1,0:T(8,128)(2,1)S(1)}, u32[]{:S(2)}, u32[]{:S(2)}) collective-permute-start(bf16[8,48,128]{2,1,0:T(8,128)(2,1)S(1)} %get-tuple-element.67), channel_id=1, source_target_pairs={{0,8},{8,0},{16,24},{24,16},{32,40},{40,32},{48,56},{56,48},{64,72... | collective-permute-start | bytes 294920 | tf_op jit(solution)/shard_map/ppermute | solution.py:619
  54.3 10.1 %collective-permute-start.3 = (bf16[8,32,128]{2,1,0:T(8,128)(2,1)S(1)}, bf16[8,32,128]{2,1,0:T(8,128)(2,1)S(1)}, u32[]{:S(2)}, u32[]{:S(2)}) collective-permute-start(bf16[8,32,128]{2,1,0:T(8,128)(2,1)S(1)} %get-tuple-element.68), channel_id=1, source_target_pairs={{0,760},{8,16},{16,8},{24,32},{32,24},{40,48},{48,40},{56,64},{64,... | collective-permute-start | bytes 196616 | tf_op jit(solution)/shard_map/ppermute | solution.py:615
  56.2 8.2 %collective-permute-start.2 = (bf16[8,32,128]{2,1,0:T(8,128)(2,1)S(1)}, bf16[8,32,128]{2,1,0:T(8,128)(2,1)S(1)}, u32[]{:S(2)}, u32[]{:S(2)}) collective-permute-start(bf16[8,32,128]{2,1,0:T(8,128)(2,1)S(1)} %get-tuple-element.69), channel_id=1, source_target_pairs={{0,8},{8,0},{16,24},{24,16},{32,40},{40,32},{48,56},{56,48},{64,72... | collective-permute-start | bytes 196616 | tf_op jit(solution)/shard_map/ppermute | solution.py:619

commit v5 on v4

--- a/solution.py
+++ b/solution.py
@@ -387,8 +387,13 @@
     return x, jnp.where(wall, -u, v)
 
 
-def block_of(ref, row):
-    return ref[:, row : row + 16].reshape(G, 128)
+def places():
+    own = jnp.where((lax.axis_index("dom") & 1) == 1, 0, 8)
+    return own, 8 - own
+
+
+def block_of(ref, row, start=0):
+    return ref[pl.ds(start, 8), row : row + 16].reshape(G, 128)
 
 
 def pack_kernel(state_hbm, final_hbm, send_hbm, ext_hbm, perm_hbm,
@@ -425,12 +430,14 @@
     back = dot(back_slots, stack)
     forward = dot(send_slots, packed(t))
     whole = jnp.concatenate([back[:, :128], back[:, 128:] + forward], axis=1).astype(bf16)
-    for o in range(3):
-        for peer in range(8):
+    own, other = places()
+    for peer in range(8):
+        for o, place, start in ((0, own, 48), (1, own, 0), (2, other, 0)):
             at = G * o + 16 * peer
             for j in range(3):
-                row = 48 * o + 16 * j
-                out_ref[peer, row : row + 16] = whole[at : at + 16, 128 * j : 128 * (j + 1)]
+                row = start + 16 * j
+                out_ref[place + peer, row : row + 16] = whole[at : at + 16, 128 * j : 128 * (j + 1)]
+        out_ref[other + peer, 48:] = jnp.zeros((48, 128), bf16)
 
 
 def first_local_kernel(q_ref, w_ref, t_ref, lam_ref, send_ref, ext_ref, perm_ref, forward_ref, backward_ref,
@@ -461,7 +468,7 @@
     z_ref[...] = derivative_back(load_tiles(w_ref), backward_ref[...])
 
 
-def middle_kernel(base_ref, w_ref, lam_ref, rest_ref, z_ref, chip_ref, own_ref, next_ref,
+def middle_kernel(base_ref, w_ref, lam_ref, rest_ref, z_ref, chip_ref, arrived_ref,
                   from_slots_ref, to_columns_ref, local_ref, local_back_ref, send_slots_ref, back_slots_ref,
                   index_ref, inverse_ref, kind_ref,
                   out_ref, q1_ref, w1_ref, t1_ref, u1_ref, x1_ref, v1_ref, lam1_ref):
@@ -473,9 +480,10 @@
     wide = lanes(F)
     lane = lanes()
     node = index & 15
+    own, other = places()
     arrived = jnp.concatenate(
-        [jnp.concatenate([block_of(ref, at + 16 * j) for j in range(3)], axis=1)
-         for ref, at in ((chip_ref, 0), (own_ref, 48), (next_ref, 0))], axis=0)
+        [jnp.concatenate([block_of(ref, 16 * j, start) for j in range(3)], axis=1)
+         for ref, start in ((chip_ref, 0), (arrived_ref, own), (arrived_ref, other))], axis=0)
     g = dot(from_slots_ref[...], arrived[:, 128:])
     sums = dot(to_columns_ref[...], arrived)
     g0, g1 = g[:, :128], g[:, 128:]
@@ -522,13 +530,16 @@
     back = dot(back_slots_ref[...], jnp.concatenate([first, second], axis=1).astype(bf16))
     main = (back[:, :128] + forward).astype(bf16)
     tail = [back[G * o : G * (o + 1), 128:] for o in range(3)]
-    shared = (tail[0] + turn(tail[1], 32) + turn(tail[2], 64)).astype(bf16)
+    shared = (tail[0] + turn(tail[1], 32)).astype(bf16)
+    last = turn(tail[2], 64).astype(bf16)
     for peer in range(8):
         at = 16 * peer
-        out_ref[peer, :16] = main[at : at + 16]
-        out_ref[peer, 16:32] = shared[at : at + 16]
-        out_ref[peer, 32:48] = main[2 * G + at : 2 * G + at + 16]
-        out_ref[peer, 48:] = main[G + at : G + at + 16]
+        out_ref[own + peer, :16] = main[G + at : G + at + 16]
+        out_ref[own + peer, 16:32] = main[at : at + 16]
+        out_ref[own + peer, 32:] = shared[at : at + 16]
+        out_ref[other + peer, :16] = main[2 * G + at : 2 * G + at + 16]
+        out_ref[other + peer, 16:32] = last[at : at + 16]
+        out_ref[other + peer, 32:] = jnp.zeros((16, 128), bf16)
 
 
 def second_local_kernel(q_ref, w_ref, t_ref, q1_ref, w1_ref, t1_ref, u1_ref, x1_ref, v1_ref, lam1_ref,
@@ -562,16 +573,17 @@
     store_tiles(start_ref, [0.5 * w[j] + w1[j] + step_size * (inner[j] + faced[j]) for j in range(3)])
 
 
-def last_kernel(end_base_ref, start_base_ref, chip_ref, own_ref, next_ref, from_slots_ref, to_columns_ref, index_ref,
+def last_kernel(end_base_ref, start_base_ref, chip_ref, arrived_ref, from_slots_ref, to_columns_ref, index_ref,
                 end_ref, start_ref):
     faces = Faces()
-    main = jnp.concatenate([block_of(chip_ref, 0), block_of(own_ref, 48), block_of(next_ref, 16)], axis=0)
+    own, other = places()
+    main = jnp.concatenate([block_of(chip_ref, 0), block_of(arrived_ref, 0, own), block_of(arrived_ref, 0, other)], axis=0)
     lane = lanes(G)
     zero = jnp.zeros((G, 128), bf16)
     shared = jnp.concatenate([
         jnp.where(lane < 32, block_of(chip_ref, 16), zero),
-        jnp.where((lane >= 32) & (lane < 64), block_of(own_ref, 16), zero),
-        jnp.where((lane >= 64) & (lane < 96), block_of(next_ref, 0), zero)], axis=0)
+        jnp.where((lane >= 32) & (lane < 64), block_of(arrived_ref, 32, own), zero),
+        jnp.where((lane >= 64) & (lane < 96), block_of(arrived_ref, 16, other), zero)], axis=0)
     node = index_ref[...] & 15
     g = dot(from_slots_ref[...], main)
     b = dot(to_columns_ref[...], jnp.concatenate([main, shared], axis=1))
@@ -609,6 +621,18 @@
     return lax.all_to_all(whole, "sub", split_axis=0, concat_axis=0, tiled=True)
 
 
+def pair_peers(whole):
+    count, peers = lax.axis_size("dom"), lax.axis_size("sub")
+    groups = [[d % count * peers + peer for d in (first, first + 1) for peer in range(peers)]
+              for first in range(1, count, 2)]
+    return lax.all_to_all(
+        whole, ("dom", "sub"), split_axis=0, concat_axis=0, tiled=True, axis_index_groups=groups)
+
+
+def own_part(arrived):
+    return jnp.where((lax.axis_index("dom") & 1) == 1, arrived[:8], arrived[8:])
+
+
 def next_partner(value):
     count = lax.axis_size("dom")
     pairs = [(d, (d + 1) % count if d % 2 else (d - 1) % count) for d in range(count)]
@@ -629,33 +653,31 @@
 
     out, q, w, t, lam, send_slots, back_slots, inverse, send_slot, ext_index, ext_perm = call(
         pack_kernel,
-        (shape(8, 144, 128, dtype=bf16), node, node, face, face,
+        (shape(16, 96, 128, dtype=bf16), node, node, face, face,
          shape(S, F, dtype=bf16), shape(S, F, dtype=bf16), index_face,
          shape(1, S, dtype=i32), shape(6, E, dtype=i32), shape(6, E, dtype=i32)),
         *[pltpu.with_memory_space_constraint(x, pltpu.HBM) for x in (state, adjoint_final, send_slot, ext_index, ext_perm)], in_hbm=True,
         scratch=[pltpu.VMEM((5, E, 64), f32), pltpu.VMEM((5, E, 64), f32), pltpu.SemaphoreType.DMA((5,))])
-    arrived = all_peers(out)
+    arrived = pair_peers(out)
     base, z, rest, from_slots, to_columns, local, local_back, index, kind = call(
         first_local_kernel,
         (node, shape(96, 384), face, shape(F, S, dtype=bf16), shape(F, S, dtype=bf16),
          shape(F, F, dtype=bf16), shape(F, F, dtype=bf16), index_face, index_face),
         q, w, t, lam, send_slot, ext_index, ext_perm, forward, backward)
-    from_next = next_partner(arrived[:, 96:])
-    from_chip = chip_partner(arrived[:, :48])
+    from_chip = chip_partner(own_part(arrived[:, 48:]))
     out, q1, w1, t1, u1, x1, v1, lam1 = call(
-        middle_kernel, (shape(8, 64, 128, dtype=bf16), node, node, face, face, face, face, face),
-        base, w, lam, rest, z, from_chip, arrived, from_next,
+        middle_kernel, (shape(16, 48, 128, dtype=bf16), node, node, face, face, face, face, face),
+        base, w, lam, rest, z, from_chip, arrived,
         from_slots, to_columns, local, local_back, send_slots, back_slots, index, inverse, kind)
-    arrived = all_peers(out)
+    arrived = pair_peers(out)
     end_base, start_base = call(
         second_local_kernel, (node, node),
         q, w, t, q1, w1, t1, u1, x1, v1, lam1, local, local_back, index, inverse, kind, forward, backward)
-    from_next = next_partner(arrived[:, 16:48])
-    from_chip = chip_partner(arrived[:, :32])
+    from_chip = chip_partner(own_part(arrived[:, 16:]))
     out = shape(5, E, 64)
     end, start = call(
         last_kernel, (out, out),
-        end_base, start_base, from_chip, arrived, from_next, from_slots, to_columns, index)
+        end_base, start_base, from_chip, arrived, from_slots, to_columns, index)
     return jnp.swapaxes(end, 1, 2), jnp.swapaxes(start, 1, 2)
 
 

time: 66.1 us -> 60.7 us (0.918)
  blocking collectives: 28.1 us -> 11.5 us
  waiting for transfers between devices: 0.01 us -> 9.04 us
  starting transfers between devices: 29 us -> 30.4 us
  Pallas kernels: 7.97 us -> 8.72 us
    all_to_all x2 -> x1, blocking collectives: 28.1 us -> 11.5 us  [pair_peers(): lax.all_to_all(whole, ('dom', 'sub'), split_axis=0, concat_axis=0, tiled=...]
    all_to_all x0 -> x1, starting transfers between devices: none -> 10.3 us  [pair_peers(): lax.all_to_all(whole, ('dom', 'sub'), split_axis=0, concat_axis=0, tiled=...]
    ppermute x2 -> x0, starting transfers between devices: 9.78 us -> none  [next_partner(): return lax.ppermute(value, 'dom', pairs)]
    all_to_all x0 -> x1, waiting for transfers between devices: none -> 9.03 us  [pair_peers(): lax.all_to_all(whole, ('dom', 'sub'), split_axis=0, concat_axis=0, tiled=...]
    ppermute x2, starting transfers between devices: 19.2 us -> 20.1 us  [chip_partner(): lax.ppermute(value, 'dom', [(d, d ^ 1) for d in range(lax.axis_size('dom'...]
    pallas_call x5, Pallas kernels: 7.97 us -> 8.72 us  [call(): pl.pallas_call(kernel, out_shape=outs, in_specs=[pl.BlockSpec(memory_spac...]
  transfers between devices with their start and end apart: 4 -> 3, of which waited for: 0 -> 1; matrix products, arithmetic and copies ran while one was open for 0% -> 0% of each run, Pallas kernels for 3% -> 3%
where the time goes in v5:
time: 60.7 us; the launch traced here: 60.4 us
  starting transfers between devices  30.4 us (50%)
  blocking collectives  11.5 us (19%)
  waiting for transfers between devices  9.04 us (15%)
  Pallas kernels  8.72 us (14%)
  between operations  0.74 us (1%)
    ppermute x2, starting transfers between devices, chip_partner(): lax.ppermute(value, 'dom', [(d, d ^ 1) for d in range(lax.axis_size('dom'...  20.1 us
    all_to_all x1, blocking collectives, pair_peers(): lax.all_to_all(whole, ('dom', 'sub'), split_axis=0, concat_axis=0, tiled=...  11.5 us
    all_to_all x1, starting transfers between devices, pair_peers(): lax.all_to_all(whole, ('dom', 'sub'), split_axis=0, concat_axis=0, tiled=...  10.3 us
    all_to_all x1, waiting for transfers between devices, pair_peers(): lax.all_to_all(whole, ('dom', 'sub'), split_axis=0, concat_axis=0, tiled=...  9.03 us
    pallas_call x5, Pallas kernels, call(): pl.pallas_call(kernel, out_shape=outs, in_specs=[pl.BlockSpec(memory_spac...  8.72 us
  transfers between devices with their start and end apart: 3, of which 1 were waited for; matrix products, arithmetic and copies ran while one was open for 0% of the time, Pallas kernels for 3%

profile of v5, /device:TPU:1, one launch (start us, length us, event | category | flops | bytes accessed | tf_op | source)
XLA Modules:
  0.0 60.4 jit_solution(5251021654577780977)
XLA Ops:
  0.6 2.8 %shard_map.86 = (bf16[16,96,128]{2,1,0:T(8,128)(2,1)}, f32[32,384]{1,0:T(8,128)S(1)}, f32[32,384]{1,0:T(8,128)S(1)}, f32[192,128]{1,0:T(8,128)S(1)}, f32[192,128...) custom-call(f32[5,32,64]{2,1,0:T(8,128)} %bitcast.4, ...), custom_call_target="tpu_custom_call" | custom-call | flops 200000000 | bytes 1000000 | tf_op jit(solution)/shard_map/pallas_call | solution.py:610
  3.4 0.0 copy-start.1
  3.4 10.3 %all-to-all-start = ((bf16[16,96,128]{2,1,0:T(8,128)(2,1)}), bf16[16,96,128]{2,1,0:T(8,128)(2,1)S(1)}, u32[]{:S(2)}, u32[]{:S(2)}) async-start(bf16[16,96,128]{2,1,0:T(8,128)(2,1)} %get-tuple-element.44), calls=%async_computation | async-start | bytes 786432 | tf_op jit(solution)/shard_map/all_to_all | solution.py:628
  13.7 0.0 copy-start
  13.7 9.0 %all-to-all-done.arrived_ref = bf16[16,96,128]{2,1,0:T(8,128)(2,1)S(1)} async-done(((bf16[16,96,128]{2,1,0:T(8,128)(2,1)}), bf16[16,96,128]{2,1,0:T(8,128)(2,1)S(1)}, u32[]{:S(2)}, u32[]{:S(2)}) %all-to-all-start) | async-done | bytes 393248 | tf_op jit(solution)/shard_map/all_to_all | solution.py:628
  22.8 13.2 %collective-permute-start = (bf16[8,48,128]{2,1,0:T(8,128)(2,1)S(1)}, bf16[8,48,128]{2,1,0:T(8,128)(2,1)S(1)}, u32[]{:S(2)}, u32[]{:S(2)}) collective-permute-start(bf16[8,48,128]{2,1,0:T(8,128)(2,1)S(1)} %slice_select_fusion), channel_id=1, source_target_pairs={{0,8},{8,0},{16,24},{24,16},{32,40},{40,32},{48,56},{56,48},{64,72... | collective-permute-start | bytes 294920 | tf_op jit(solution)/shard_map/ppermute | solution.py:643
  35.9 0.0 copy-done.1
  36.0 0.0 copy-done
  36.0 0.9 %shard_map.87 = (f32[32,384]{1,0:T(8,128)S(1)}, f32[96,384]{1,0:T(8,128)S(1)}, f32[192,128]{1,0:T(8,128)S(1)}, bf16[192,384]{1,0:T(8,128)(2,1)S(1)}, bf16[192,38...) custom-call(f32[32,384]{1,0:T(8,128)S(1)} %get-tuple-element.34.q_re, ...), custom_call_target="tpu_custom_call" | custom-call | flops 200000000 | bytes 1000000 | tf_op jit(solution)/shard_map/pallas_call | solution.py:610
  36.9 0.0 collective-permute-done.chip_ref
  36.9 2.4 %shard_map.88 = (bf16[16,48,128]{2,1,0:T(8,128)(2,1)S(1)}, f32[32,384]{1,0:T(8,128)S(1)}, f32[32,384]{1,0:T(8,128)S(1)}, f32[192,128]{1,0:T(8,128)S(1)}, f32[192...) custom-call(f32[32,384]{1,0:T(8,128)S(1)} %get-tuple-element.41.base_ref, ...), custom_call_target="tpu_custom_call" | custom-call | flops 200000000 | bytes 1000000 | tf_op jit(solution)/shard_map/pallas_call | solution.py:610
  39.3 11.5 %all_to_all.10.arrived_ref = bf16[16,48,128]{2,1,0:T(8,128)(2,1)S(1)} all-to-all(bf16[16,48,128]{2,1,0:T(8,128)(2,1)S(1)} %get-tuple-element.63), channel_id=1, replica_groups={{8,9,10,11,12,13,14,15,16,17,18,19,20,21,22,23},{24,25,26,27,28,29,30,3..., dimensions={0} | all-to-all | bytes 393216 | tf_op jit(solution)/shard_map/all_to_all | solution.py:628
  50.8 6.9 %collective-permute-start.1 = (bf16[8,32,128]{2,1,0:T(8,128)(2,1)S(1)}, bf16[8,32,128]{2,1,0:T(8,128)(2,1)S(1)}, u32[]{:S(2)}, u32[]{:S(2)}) collective-permute-start(bf16[8,32,128]{2,1,0:T(8,128)(2,1)S(1)} %slice_select_fusion.1), channel_id=1, source_target_pairs={{0,8},{8,0},{16,24},{24,16},{32,40},{40,32},{48,56},{56,48},{64,72... | collective-permute-start | bytes 196616 | tf_op jit(solution)/shard_map/ppermute | solution.py:643
  57.7 1.2 %shard_map.89 = (f32[32,384]{1,0:T(8,128)S(1)}, f32[32,384]{1,0:T(8,128)S(1)}) custom-call(f32[32,384]{1,0:T(8,128)S(1)} %get-tuple-element.34.q_ref, f32[32,384]{1,0:T(8,128)S(1)} %get-tuple-element.35.w_ref, f32[192,128]{1,0:T(8,128)S(1)} %get-tuple-element.36.t_ref, f32[32,384]{1,0:T(8,128)S(1)} %get-tuple-element.54.q1_ref, ...), custom_call_target="tpu_custom_call" | custom-call | flops 200000000 | bytes 1000000 | tf_op jit(solution)/shard_map/pallas_call | solution.py:610
  58.9 0.0 collective-permute-done.1.chip_ref
  58.9 1.5 %shard_map.90 = (f32[5,32,64]{2,1,0:T(8,128)}, f32[5,32,64]{2,1,0:T(8,128)}) custom-call(f32[32,384]{1,0:T(8,128)S(1)} %get-tuple-element.61.end_base_ref, f32[32,384]{1,0:T(8,128)S(1)} %get-tuple-element.62.start_base_ref, bf16[8,32,128]{2,1,0:T(8,128)(2,1)S(1)} %collective-permute-done.1.chip_ref, bf16[16,48,128]{2,1,0:T(8,128)(2,1)S(1)} %all_to_all.10.arrived_ref, ...), custom_call_target="tpu_custom_call" | custom-call | flops 200000000 | bytes 1000000 | tf_op jit(solution)/shard_map/pallas_call | solution.py:610
  (2 shorter events, 0.0 us)
Async XLA Ops:
  3.4 32.5 %copy-start.1 = (bf16[384,256]{1,0:T(8,128)(2,1)S(1)}, bf16[384,256]{1,0:T(8,128)(2,1)}, u32[]{:S(2)}) copy-start(bf16[384,256]{1,0:T(8,128)(2,1)} %constant.11.clone.forward_ref) | copy-start | bytes 589828
  3.4 19.3 %all-to-all-start = ((bf16[16,96,128]{2,1,0:T(8,128)(2,1)}), bf16[16,96,128]{2,1,0:T(8,128)(2,1)S(1)}, u32[]{:S(2)}, u32[]{:S(2)}) async-start(bf16[16,96,128]{2,1,0:T(8,128)(2,1)} %get-tuple-element.44), calls=%async_computation | async-start | bytes 786432 | tf_op jit(solution)/shard_map/all_to_all | solution.py:628
  13.7 22.2 %copy-start = (bf16[128,768]{1,0:T(8,128)(2,1)S(1)}, bf16[128,768]{1,0:T(8,128)(2,1)}, u32[]{:S(2)}) copy-start(bf16[128,768]{1,0:T(8,128)(2,1)} %constant.12.clone.backward_ref) | copy-start | bytes 589828
  22.8 14.1 %collective-permute-start = (bf16[8,48,128]{2,1,0:T(8,128)(2,1)S(1)}, bf16[8,48,128]{2,1,0:T(8,128)(2,1)S(1)}, u32[]{:S(2)}, u32[]{:S(2)}) collective-permute-start(bf16[8,48,128]{2,1,0:T(8,128)(2,1)S(1)} %slice_select_fusion), channel_id=1, source_target_pairs={{0,8},{8,0},{16,24},{24,16},{32,40},{40,32},{48,56},{56,48},{64,72... | collective-permute-start | bytes 294920 | tf_op jit(solution)/shard_map/ppermute | solution.py:643
  50.8 8.1 %collective-permute-start.1 = (bf16[8,32,128]{2,1,0:T(8,128)(2,1)S(1)}, bf16[8,32,128]{2,1,0:T(8,128)(2,1)S(1)}, u32[]{:S(2)}, u32[]{:S(2)}) collective-permute-start(bf16[8,32,128]{2,1,0:T(8,128)(2,1)S(1)} %slice_select_fusion.1), channel_id=1, source_target_pairs={{0,8},{8,0},{16,24},{24,16},{32,40},{40,32},{48,56},{56,48},{64,72... | collective-permute-start | bytes 196616 | tf_op jit(solution)/shard_map/ppermute | solution.py:643

commit v6 on v5

--- a/solution.py
+++ b/solution.py
@@ -214,6 +214,28 @@
             part = jnp.where(ends, part, 0.0)
             tiles[tile] = part if tiles[tile] is None else tiles[tile] + part
     return tiles
+
+
+def lifted_traces(x):
+    lane = lanes()
+    wide = lanes(E)
+    v16 = lane & 112
+    r, s = (lane >> 2) & 3, lane & 3
+    wide_r, wide_s = (wide >> 2) & 3, wide & 3
+    rows = []
+    for f in range(6):
+        a, b = f // 2, f % 2
+        total = x[32 * f : 32 * (f + 1)]
+        for place, side in ((0, wide_r), (1, wide_s)):
+            axis = [other for other in range(3) if other != a][place]
+            free = (s, r)[place]
+            node = 12 * b + free if a < [o for o in range(3) if o != axis and o != a][0] else 4 * free + 3 * b
+            index = v16 + node
+            first = take(x[64 * axis : 64 * axis + 32], index)
+            last = take(x[64 * axis + 32 : 64 * axis + 64], index)
+            total = total + jnp.where(side == 0, first, jnp.where(side == 3, last, 0.0))
+        rows.append(total)
+    return jnp.concatenate(rows, axis=0)
 
 
 def by_axis(function, *arrays):
@@ -441,8 +463,8 @@
 
 
 def first_local_kernel(q_ref, w_ref, t_ref, lam_ref, send_ref, ext_ref, perm_ref, forward_ref, backward_ref,
-                       base_ref, z_ref, rest_ref, from_slots_ref, to_columns_ref, local_ref, local_back_ref,
-                       index_ref, kind_ref):
+                       base_ref, t_base_ref, z_ref, rest_ref, u_ref, x_ref, v_ref,
+                       from_slots_ref, to_columns_ref, local_ref, local_back_ref, index_ref, kind_ref):
     faces = Faces()
     send, ext_col, ext_row = peer_tables(send_ref, ext_ref)
     index, _ = orientation(column_of(perm_ref))
@@ -461,14 +483,19 @@
     rest_ref[...] = lam - 0.5 * faces.rest_back(lam)
     u = faces.normal_of(t)
     x, v = exterior(faces, wall, index, local, t, u)
+    u_ref[...] = u
+    x_ref[...] = x
+    v_ref[...] = v
     jump = 0.5 * (faces.flux(t, u) - faces.flux(x, v)) + (x - t)
     faced = lifted(lift_factor * jump)
     inner = volume(q, forward_ref[...])
-    store_tiles(base_ref, [q[j] + step_size * (inner[j] + faced[j]) for j in range(3)])
+    base = [q[j] + step_size * (inner[j] + faced[j]) for j in range(3)]
+    store_tiles(base_ref, base)
+    t_base_ref[...] = traces(base)
     z_ref[...] = derivative_back(load_tiles(w_ref), backward_ref[...])
 
 
-def middle_kernel(base_ref, w_ref, lam_ref, rest_ref, z_ref, chip_ref, arrived_ref,
+def middle_kernel(base_ref, t_base_ref, w_ref, lam_ref, rest_ref, z_ref, chip_ref, arrived_ref,
                   from_slots_ref, to_columns_ref, local_ref, local_back_ref, send_slots_ref, back_slots_ref,
                   index_ref, inverse_ref, kind_ref,
                   out_ref, q1_ref, w1_ref, t1_ref, u1_ref, x1_ref, v1_ref, lam1_ref):
@@ -492,11 +519,12 @@
     ur = jnp.concatenate(
         [take(g0[:64], 96 + node[:64]), take(g0[64:128], 112 + node[64:128]), take(g1[128:], 80 + node[128:])], axis=0)
     pr = take(g1, 96 + node)
-    faced = lifted((lift_factor * step_size) * (xr - 0.5 * faces.flux(xr, ur, pr)))
+    jump = (lift_factor * step_size) * (xr - 0.5 * faces.flux(xr, ur, pr))
+    t1 = t_base_ref[...] + lifted_traces(jump)
+    faced = lifted(jump)
     base = load_tiles(base_ref)
     q1 = [base[j] + faced[j] for j in range(3)]
     store_tiles(q1_ref, q1)
-    t1 = traces(q1)
     t1_ref[...] = t1
     t1_sent = t1.astype(bf16)
     forward = dot(send_slots_ref[...], t1_sent)
@@ -518,11 +546,11 @@
     through = through + mask((lane >= 16) & (lane < 64)) * turn(h0, 64) * sent
     total = total + mask(lane < 80) * through
     inner = volume_back(q1, z_ref[...])
+    w = load_tiles(w_ref)
+    half = [0.5 * w[j] + (0.5 * step_size) * inner[j] for j in range(3)]
+    lam1 = lift_factor * traces(half) + (0.5 * step_size * lift_factor) * lifted_traces(total)
     faced = lifted(total)
-    w = load_tiles(w_ref)
-    w1 = [0.5 * w[j] + (0.5 * step_size) * (inner[j] + faced[j]) for j in range(3)]
-    store_tiles(w1_ref, w1)
-    lam1 = lift_factor * traces(w1)
+    store_tiles(w1_ref, [half[j] + (0.5 * step_size) * faced[j] for j in range(3)])
     lam1_ref[...] = lam1
     bar = lam1 - 0.5 * faces.flux_back(xr, ur, lam1)
     first = take(bar, jnp.where(wide >= 80, inverse - 80, 80))
@@ -538,15 +566,14 @@
         out_ref[own + peer, 16:32] = main[at : at + 16]
         out_ref[own + peer, 32:] = shared[at : at + 16]
         out_ref[other + peer, :16] = main[2 * G + at : 2 * G + at + 16]
-        out_ref[other + peer, 16:32] = last[at : at + 16]
-        out_ref[other + peer, 32:] = jnp.zeros((16, 128), bf16)
-
-
-def second_local_kernel(q_ref, w_ref, t_ref, q1_ref, w1_ref, t1_ref, u1_ref, x1_ref, v1_ref, lam1_ref,
-                        local_ref, local_back_ref, index_ref, inverse_ref, kind_ref,
+        out_ref[other + peer, 16:32] = jnp.zeros((16, 128), bf16)
+        out_ref[other + peer, 32:] = last[at : at + 16]
+
+
+def second_local_kernel(q_ref, w_ref, t_ref, u_ref, x_ref, v_ref, q1_ref, w1_ref, t1_ref, u1_ref, x1_ref, v1_ref,
+                        lam1_ref, local_back_ref, inverse_ref, kind_ref,
                         forward_ref, backward_ref, end_ref, start_ref):
     faces = Faces()
-    index = index_ref[...]
     inverse = inverse_ref[...]
     kind = kind_ref[...]
     wall = kind == 2
@@ -560,8 +587,7 @@
     store_tiles(end_ref, [0.5 * q[j] + 0.5 * (q1[j] + step_size * (inner[j] + faced[j])) for j in range(3)])
     t = t_ref[...]
     lam1 = lam1_ref[...]
-    u = faces.normal_of(t)
-    x, v = exterior(faces, wall, index, local_ref[...], t, u)
+    u, x, v = u_ref[...], x_ref[...], v_ref[...]
     rest = lam1 - 0.5 * faces.rest_back(lam1)
     bar = jnp.where(kind == 1, 0.0, rest - 0.5 * faces.state_back(x, v, lam1))
     total = 0.5 * faces.state_back(t, u, lam1) - rest + jnp.where(wall, faces.mirror(bar), 0.0)
@@ -583,7 +609,7 @@
     shared = jnp.concatenate([
         jnp.where(lane < 32, block_of(chip_ref, 16), zero),
         jnp.where((lane >= 32) & (lane < 64), block_of(arrived_ref, 32, own), zero),
-        jnp.where((lane >= 64) & (lane < 96), block_of(arrived_ref, 16, other), zero)], axis=0)
+        jnp.where((lane >= 64) & (lane < 96), block_of(arrived_ref, 32, other), zero)], axis=0)
     node = index_ref[...] & 15
     g = dot(from_slots_ref[...], main)
     b = dot(to_columns_ref[...], jnp.concatenate([main, shared], axis=1))
@@ -617,10 +643,6 @@
     )(*args)
 
 
-def all_peers(whole):
-    return lax.all_to_all(whole, "sub", split_axis=0, concat_axis=0, tiled=True)
-
-
 def pair_peers(whole):
     count, peers = lax.axis_size("dom"), lax.axis_size("sub")
     groups = [[d % count * peers + peer for d in (first, first + 1) for peer in range(peers)]
@@ -629,14 +651,8 @@
         whole, ("dom", "sub"), split_axis=0, concat_axis=0, tiled=True, axis_index_groups=groups)
 
 
-def own_part(arrived):
-    return jnp.where((lax.axis_index("dom") & 1) == 1, arrived[:8], arrived[8:])
-
-
-def next_partner(value):
-    count = lax.axis_size("dom")
-    pairs = [(d, (d + 1) % count if d % 2 else (d - 1) % count) for d in range(count)]
-    return lax.ppermute(value, "dom", pairs)
+def for_chip(arrived):
+    return arrived[:8] + arrived[8:]
 
 
 def chip_partner(value):
@@ -659,21 +675,21 @@
         *[pltpu.with_memory_space_constraint(x, pltpu.HBM) for x in (state, adjoint_final, send_slot, ext_index, ext_perm)], in_hbm=True,
         scratch=[pltpu.VMEM((5, E, 64), f32), pltpu.VMEM((5, E, 64), f32), pltpu.SemaphoreType.DMA((5,))])
     arrived = pair_peers(out)
-    base, z, rest, from_slots, to_columns, local, local_back, index, kind = call(
+    base, t_base, z, rest, u, x, v, from_slots, to_columns, local, local_back, index, kind = call(
         first_local_kernel,
-        (node, shape(96, 384), face, shape(F, S, dtype=bf16), shape(F, S, dtype=bf16),
+        (node, face, shape(96, 384), face, face, face, face, shape(F, S, dtype=bf16), shape(F, S, dtype=bf16),
          shape(F, F, dtype=bf16), shape(F, F, dtype=bf16), index_face, index_face),
         q, w, t, lam, send_slot, ext_index, ext_perm, forward, backward)
-    from_chip = chip_partner(own_part(arrived[:, 48:]))
+    from_chip = chip_partner(for_chip(arrived[:, 48:]))
     out, q1, w1, t1, u1, x1, v1, lam1 = call(
         middle_kernel, (shape(16, 48, 128, dtype=bf16), node, node, face, face, face, face, face),
-        base, w, lam, rest, z, from_chip, arrived,
+        base, t_base, w, lam, rest, z, from_chip, arrived,
         from_slots, to_columns, local, local_back, send_slots, back_slots, index, inverse, kind)
     arrived = pair_peers(out)
     end_base, start_base = call(
         second_local_kernel, (node, node),
-        q, w, t, q1, w1, t1, u1, x1, v1, lam1, local, local_back, index, inverse, kind, forward, backward)
-    from_chip = chip_partner(own_part(arrived[:, 16:]))
+        q, w, t, u, x, v, q1, w1, t1, u1, x1, v1, lam1, local_back, inverse, kind, forward, backward)
+    from_chip = chip_partner(for_chip(arrived[:, 16:]))
     out = shape(5, E, 64)
     end, start = call(
         last_kernel, (out, out),

time: 60.7 us -> 59.6 us (0.982)
  blocking collectives: 11.5 us -> 30.6 us
  starting transfers between devices: 30.4 us -> 20.2 us
  waiting for transfers between devices: 9.04 us -> 0.01 us
  Pallas kernels: 8.72 us -> 7.75 us
    all_to_all x1 -> x2, blocking collectives: 11.5 us -> 30.6 us  [pair_peers(): lax.all_to_all(whole, ('dom', 'sub'), split_axis=0, concat_axis=0, tiled=...]
    all_to_all x1 -> x0, starting transfers between devices: 10.3 us -> none  [pair_peers(): lax.all_to_all(whole, ('dom', 'sub'), split_axis=0, concat_axis=0, tiled=...]
    all_to_all x1 -> x0, waiting for transfers between devices: 9.03 us -> none  [pair_peers(): lax.all_to_all(whole, ('dom', 'sub'), split_axis=0, concat_axis=0, tiled=...]
    pallas_call x5, Pallas kernels: 8.72 us -> 7.75 us  [call(): pl.pallas_call(kernel, out_shape=outs, in_specs=[pl.BlockSpec(memory_spac...]
  transfers between devices with their start and end apart: 3 -> 2, of which waited for: 1 -> 0; matrix products, arithmetic and copies ran while one was open for 0% -> 0% of each run, Pallas kernels for 3% -> 3%
where the time goes in v6:
time: 59.6 us; the launch traced here: 59.3 us
  blocking collectives  30.6 us (51%)
  starting transfers between devices  20.2 us (34%)
  Pallas kernels  7.75 us (13%)
  between operations  0.72 us (1%)
    all_to_all x2, blocking collectives, pair_peers(): lax.all_to_all(whole, ('dom', 'sub'), split_axis=0, concat_axis=0, tiled=...  30.6 us
    ppermute x2, starting transfers between devices, chip_partner(): lax.ppermute(value, 'dom', [(d, d ^ 1) for d in range(lax.axis_size('dom'...  20.2 us
    pallas_call x5, Pallas kernels, call(): pl.pallas_call(kernel, out_shape=outs, in_specs=[pl.BlockSpec(memory_spac...  7.75 us
  transfers between devices with their start and end apart: 2, of which 0 were waited for; matrix products, arithmetic and copies ran while one was open for 0% of the time, Pallas kernels for 3%

profile of v6, /device:TPU:1, one launch (start us, length us, event | category | flops | bytes accessed | tf_op | source)
XLA Modules:
  0.0 59.3 jit_solution(14666209374593394778)
XLA Ops:
  0.6 2.0 %shard_map.86 = (bf16[16,96,128]{2,1,0:T(8,128)(2,1)S(1)}, f32[32,384]{1,0:T(8,128)S(1)}, f32[32,384]{1,0:T(8,128)S(1)}, f32[192,128]{1,0:T(8,128)S(1)}, f32[192...) custom-call(f32[5,32,64]{2,1,0:T(8,128)} %bitcast.4, ...), custom_call_target="tpu_custom_call" | custom-call | flops 200000000 | bytes 1000000 | tf_op jit(solution)/shard_map/pallas_call | solution.py:636
  2.7 0.0 copy-start.1
  2.7 19.1 %all_to_all.10.arrived_ref = bf16[16,96,128]{2,1,0:T(8,128)(2,1)S(1)} all-to-all(bf16[16,96,128]{2,1,0:T(8,128)(2,1)S(1)} %get-tuple-element.52), channel_id=1, replica_groups={{8,9,10,11,12,13,14,15,16,17,18,19,20,21,22,23},{24,25,26,27,28,29,30,3..., dimensions={0} | all-to-all | bytes 786432 | tf_op jit(solution)/shard_map/all_to_all | solution.py:650
  21.8 0.0 copy-start
  21.8 13.3 %collective-permute-start = (bf16[8,48,128]{2,1,0:T(8,128)(2,1)S(1)}, bf16[8,48,128]{2,1,0:T(8,128)(2,1)S(1)}, u32[]{:S(2)}, u32[]{:S(2)}) collective-permute-start(bf16[8,48,128]{2,1,0:T(8,128)(2,1)S(1)} %slice_add_fusion), channel_id=1, source_target_pairs={{0,8},{8,0},{16,24},{24,16},{32,40},{40,32},{48,56},{56,48},{64,72... | collective-permute-start | bytes 294920 | tf_op jit(solution)/shard_map/ppermute | solution.py:659
  35.1 0.0 copy-done.1
  35.1 0.0 copy-done
  35.1 1.1 %shard_map.87 = (f32[32,384]{1,0:T(8,128)S(1)}, f32[192,128]{1,0:T(8,128)S(1)}, f32[96,384]{1,0:T(8,128)S(1)}, f32[192,128]{1,0:T(8,128)S(1)}, f32[192,128]{1,0:...) custom-call(f32[32,384]{1,0:T(8,128)S(1)} %get-tuple-element.38.q_re, ...), custom_call_target="tpu_custom_call" | custom-call | flops 200000000 | bytes 1000000 | tf_op jit(solution)/shard_map/pallas_call | solution.py:636
  36.2 0.0 collective-permute-done.chip_ref
  36.2 2.3 %shard_map.88 = (bf16[16,48,128]{2,1,0:T(8,128)(2,1)S(1)}, f32[32,384]{1,0:T(8,128)S(1)}, f32[32,384]{1,0:T(8,128)S(1)}, f32[192,128]{1,0:T(8,128)S(1)}, f32[192...) custom-call(f32[32,384]{1,0:T(8,128)S(1)} %get-tuple-element.48.base_ref, ...), custom_call_target="tpu_custom_call" | custom-call | flops 200000000 | bytes 1000000 | tf_op jit(solution)/shard_map/pallas_call | solution.py:636
  38.5 11.5 %all_to_all.11.arrived_ref = bf16[16,48,128]{2,1,0:T(8,128)(2,1)S(1)} all-to-all(bf16[16,48,128]{2,1,0:T(8,128)(2,1)S(1)} %get-tuple-element.71), channel_id=1, replica_groups={{8,9,10,11,12,13,14,15,16,17,18,19,20,21,22,23},{24,25,26,27,28,29,30,3..., dimensions={0} | all-to-all | bytes 393216 | tf_op jit(solution)/shard_map/all_to_all | solution.py:650
  50.0 6.9 %collective-permute-start.1 = (bf16[8,32,128]{2,1,0:T(8,128)(2,1)S(1)}, bf16[8,32,128]{2,1,0:T(8,128)(2,1)S(1)}, u32[]{:S(2)}, u32[]{:S(2)}) collective-permute-start(bf16[8,32,128]{2,1,0:T(8,128)(2,1)S(1)} %slice_add_fusion.1), channel_id=1, source_target_pairs={{0,8},{8,0},{16,24},{24,16},{32,40},{40,32},{48,56},{56,48},{64,72... | collective-permute-start | bytes 196616 | tf_op jit(solution)/shard_map/ppermute | solution.py:659
  56.9 0.9 %shard_map.89 = (f32[32,384]{1,0:T(8,128)S(1)}, f32[32,384]{1,0:T(8,128)S(1)}) custom-call(f32[32,384]{1,0:T(8,128)S(1)} %get-tuple-element.38.q_ref, f32[32,384]{1,0:T(8,128)S(1)} %get-tuple-element.39.w_ref, f32[192,128]{1,0:T(8,128)S(1)} %get-tuple-element.40.t_ref, f32[192,128]{1,0:T(8,128)S(1)} %get-tuple-element.45.u_ref, ...), custom_call_target="tpu_custom_call" | custom-call | flops 200000000 | bytes 1000000 | tf_op jit(solution)/shard_map/pallas_call | solution.py:636
  57.8 0.0 collective-permute-done.1.chip_ref
  57.9 1.5 %shard_map.90 = (f32[5,32,64]{2,1,0:T(8,128)}, f32[5,32,64]{2,1,0:T(8,128)}) custom-call(f32[32,384]{1,0:T(8,128)S(1)} %get-tuple-element.69.end_base_ref, f32[32,384]{1,0:T(8,128)S(1)} %get-tuple-element.70.start_base_ref, bf16[8,32,128]{2,1,0:T(8,128)(2,1)S(1)} %collective-permute-done.1.chip_ref, bf16[16,48,128]{2,1,0:T(8,128)(2,1)S(1)} %all_to_all.11.arrived_ref, ...), custom_call_target="tpu_custom_call" | custom-call | flops 200000000 | bytes 1000000 | tf_op jit(solution)/shard_map/pallas_call | solution.py:636
  (2 shorter events, 0.0 us)
Async XLA Ops:
  2.7 32.4 %copy-start.1 = (bf16[128,768]{1,0:T(8,128)(2,1)S(1)}, bf16[128,768]{1,0:T(8,128)(2,1)}, u32[]{:S(2)}) copy-start(bf16[128,768]{1,0:T(8,128)(2,1)} %constant.5.clone.backward_ref) | copy-start | bytes 589828
  21.8 13.3 %copy-start = (bf16[384,256]{1,0:T(8,128)(2,1)S(1)}, bf16[384,256]{1,0:T(8,128)(2,1)}, u32[]{:S(2)}) copy-start(bf16[384,256]{1,0:T(8,128)(2,1)} %constant.4.clone.forward_ref) | copy-start | bytes 589828
  21.8 14.4 %collective-permute-start = (bf16[8,48,128]{2,1,0:T(8,128)(2,1)S(1)}, bf16[8,48,128]{2,1,0:T(8,128)(2,1)S(1)}, u32[]{:S(2)}, u32[]{:S(2)}) collective-permute-start(bf16[8,48,128]{2,1,0:T(8,128)(2,1)S(1)} %slice_add_fusion), channel_id=1, source_target_pairs={{0,8},{8,0},{16,24},{24,16},{32,40},{40,32},{48,56},{56,48},{64,72... | collective-permute-start | bytes 294920 | tf_op jit(solution)/shard_map/ppermute | solution.py:659
  50.0 7.8 %collective-permute-start.1 = (bf16[8,32,128]{2,1,0:T(8,128)(2,1)S(1)}, bf16[8,32,128]{2,1,0:T(8,128)(2,1)S(1)}, u32[]{:S(2)}, u32[]{:S(2)}) collective-permute-start(bf16[8,32,128]{2,1,0:T(8,128)(2,1)S(1)} %slice_add_fusion.1), channel_id=1, source_target_pairs={{0,8},{8,0},{16,24},{24,16},{32,40},{40,32},{48,56},{56,48},{64,72... | collective-permute-start | bytes 196616 | tf_op jit(solution)/shard_map/ppermute | solution.py:659

commit v7 on v6

--- a/solution.py
+++ b/solution.py
@@ -275,28 +275,26 @@
         return by_axis(along, x, u, p)
 
     def flux_back(self, x, u, w):
-        def along(a, x, u, w):
+        def along(a, x, u, w, h):
             n = take(w, self.normal_index[a])
             c = u + mean_flow if a == 0 else u
-            h = over_fields((x + self.ends) * w)
             return signed(c * w + self.last * n + self.normal[a] * h)
 
-        return by_axis(along, x, u, w)
+        return by_axis(along, x, u, w, over_fields((x + self.ends) * w))
 
     def rest_back(self, w):
-        def along(a, w):
+        def along(a, w, h):
             n = take(w, self.normal_index[a])
-            h = over_fields(self.ends * w)
             part = self.last * n + self.normal[a] * h
             return signed(mean_flow * w + part if a == 0 else part)
 
-        return by_axis(along, w)
+        return by_axis(along, w, over_fields(self.ends * w))
 
     def state_back(self, x, u, w):
-        def along(a, x, u, w):
-            return signed(u * w + self.normal[a] * over_fields(x * w))
-
-        return by_axis(along, x, u, w)
+        def along(a, u, w, h):
+            return signed(u * w + self.normal[a] * h)
+
+        return by_axis(along, u, w, over_fields(x * w))
 
     def shifted(self, d):
         target = self.v + d
@@ -419,7 +417,7 @@
 
 
 def pack_kernel(state_hbm, final_hbm, send_hbm, ext_hbm, perm_hbm,
-                out_ref, q_ref, w_ref, t_ref, lam_ref, send_slots_ref, back_slots_ref, inverse_ref,
+                chip_ref, out_ref, q_ref, w_ref, t_ref, lam_ref, send_slots_ref, back_slots_ref, inverse_ref,
                 send_ref, ext_ref, perm_ref, state_ref, final_ref, sems):
     pairs = ((send_hbm, send_ref), (ext_hbm, ext_ref), (perm_hbm, perm_ref), (final_hbm, final_ref), (state_hbm, state_ref))
     copies = [pltpu.make_async_copy(a, b, sems.at[i]) for i, (a, b) in enumerate(pairs)]
@@ -454,12 +452,10 @@
     whole = jnp.concatenate([back[:, :128], back[:, 128:] + forward], axis=1).astype(bf16)
     own, other = places()
     for peer in range(8):
-        for o, place, start in ((0, own, 48), (1, own, 0), (2, other, 0)):
+        for o, ref, place in ((0, chip_ref, 0), (1, out_ref, own), (2, out_ref, other)):
             at = G * o + 16 * peer
             for j in range(3):
-                row = start + 16 * j
-                out_ref[place + peer, row : row + 16] = whole[at : at + 16, 128 * j : 128 * (j + 1)]
-        out_ref[other + peer, 48:] = jnp.zeros((48, 128), bf16)
+                ref[place + peer, 16 * j : 16 * (j + 1)] = whole[at : at + 16, 128 * j : 128 * (j + 1)]
 
 
 def first_local_kernel(q_ref, w_ref, t_ref, lam_ref, send_ref, ext_ref, perm_ref, forward_ref, backward_ref,
@@ -495,7 +491,7 @@
     z_ref[...] = derivative_back(load_tiles(w_ref), backward_ref[...])
 
 
-def middle_kernel(base_ref, t_base_ref, w_ref, lam_ref, rest_ref, z_ref, chip_ref, arrived_ref,
+def middle_kernel(base_ref, t_base_ref, w_ref, lam_ref, rest_ref, z_ref, arrived_ref,
                   from_slots_ref, to_columns_ref, local_ref, local_back_ref, send_slots_ref, back_slots_ref,
                   index_ref, inverse_ref, kind_ref,
                   out_ref, q1_ref, w1_ref, t1_ref, u1_ref, x1_ref, v1_ref, lam1_ref):
@@ -509,8 +505,8 @@
     node = index & 15
     own, other = places()
     arrived = jnp.concatenate(
-        [jnp.concatenate([block_of(ref, 16 * j, start) for j in range(3)], axis=1)
-         for ref, start in ((chip_ref, 0), (arrived_ref, own), (arrived_ref, other))], axis=0)
+        [jnp.concatenate([block_of(arrived_ref, row + 16 * j, start) for j in range(3)], axis=1)
+         for row, start in ((48, own), (0, own), (0, other))], axis=0)
     g = dot(from_slots_ref[...], arrived[:, 128:])
     sums = dot(to_columns_ref[...], arrived)
     g0, g1 = g[:, :128], g[:, 128:]
@@ -667,23 +663,26 @@
     face = shape(F, 128)
     index_face = shape(F, 128, dtype=i32)
 
-    out, q, w, t, lam, send_slots, back_slots, inverse, send_slot, ext_index, ext_perm = call(
+    to_chip, out, q, w, t, lam, send_slots, back_slots, inverse, send_slot, ext_index, ext_perm = call(
         pack_kernel,
-        (shape(16, 96, 128, dtype=bf16), node, node, face, face,
+        (shape(8, 48, 128, dtype=bf16), shape(16, 96, 128, dtype=bf16), node, node, face, face,
          shape(S, F, dtype=bf16), shape(S, F, dtype=bf16), index_face,
          shape(1, S, dtype=i32), shape(6, E, dtype=i32), shape(6, E, dtype=i32)),
         *[pltpu.with_memory_space_constraint(x, pltpu.HBM) for x in (state, adjoint_final, send_slot, ext_index, ext_perm)], in_hbm=True,
         scratch=[pltpu.VMEM((5, E, 64), f32), pltpu.VMEM((5, E, 64), f32), pltpu.SemaphoreType.DMA((5,))])
-    arrived = pair_peers(out)
+    from_chip = chip_partner(to_chip)
     base, t_base, z, rest, u, x, v, from_slots, to_columns, local, local_back, index, kind = call(
         first_local_kernel,
         (node, face, shape(96, 384), face, face, face, face, shape(F, S, dtype=bf16), shape(F, S, dtype=bf16),
          shape(F, F, dtype=bf16), shape(F, F, dtype=bf16), index_face, index_face),
         q, w, t, lam, send_slot, ext_index, ext_perm, forward, backward)
-    from_chip = chip_partner(for_chip(arrived[:, 48:]))
+    out = lax.dynamic_update_slice(out, from_chip, (0, 48, 0))
+    out = lax.dynamic_update_slice(out, from_chip, (8, 48, 0))
+    out, z = lax.optimization_barrier((out, z))
+    arrived = pair_peers(out)
     out, q1, w1, t1, u1, x1, v1, lam1 = call(
         middle_kernel, (shape(16, 48, 128, dtype=bf16), node, node, face, face, face, face, face),
-        base, t_base, w, lam, rest, z, from_chip, arrived,
+        base, t_base, w, lam, rest, z, arrived,
         from_slots, to_columns, local, local_back, send_slots, back_slots, index, inverse, kind)
     arrived = pair_peers(out)
     end_base, start_base = call(

time: 59.6 us -> 59.1 us (level)
  blocking collectives: 30.6 us -> 26.4 us
  starting transfers between devices: 20.2 us -> 23.9 us
    all_to_all x2, blocking collectives: 30.6 us -> 26.4 us  [pair_peers(): lax.all_to_all(whole, ('dom', 'sub'), split_axis=0, concat_axis=0, tiled=...]
    ppermute x2, starting transfers between devices: 20.2 us -> 23.9 us  [chip_partner(): lax.ppermute(value, 'dom', [(d, d ^ 1) for d in range(lax.axis_size('dom'...]
where the time goes in v7:
time: 59.1 us; the launch traced here: 58.8 us
  blocking collectives  26.4 us (45%)
  starting transfers between devices  23.9 us (40%)
  Pallas kernels  7.75 us (13%)
  between operations  0.74 us (1%)
    all_to_all x2, blocking collectives, pair_peers(): lax.all_to_all(whole, ('dom', 'sub'), split_axis=0, concat_axis=0, tiled=...  26.4 us
    ppermute x2, starting transfers between devices, chip_partner(): lax.ppermute(value, 'dom', [(d, d ^ 1) for d in range(lax.axis_size('dom'...  23.9 us
    pallas_call x5, Pallas kernels, call(): pl.pallas_call(kernel, out_shape=outs, in_specs=[pl.BlockSpec(memory_spac...  7.75 us
  transfers between devices with their start and end apart: 2, of which 0 were waited for; matrix products, arithmetic and copies ran while one was open for 0% of the time, Pallas kernels for 3%

profile of v7, /device:TPU:1, one launch (start us, length us, event | category | flops | bytes accessed | tf_op | source)
XLA Modules:
  0.0 58.8 jit_solution(17823432329670808006)
XLA Ops:
  0.6 0.0 copy-start
  0.6 0.0 copy-start.1
  0.7 2.1 %shard_map.86 = (bf16[8,48,128]{2,1,0:T(8,128)(2,1)S(1)}, bf16[16,96,128]{2,1,0:T(8,128)(2,1)S(1)}, f32[32,384]{1,0:T(8,128)S(1)}, f32[32,384]{1,0:T(8,128)S(1)}...) custom-call(f32[5,32,64]{2,1,0:T(8,128)} %bitcast.4, ...), custom_call_target="tpu_custom_call" | custom-call | flops 200000000 | bytes 1000000 | tf_op jit(solution)/shard_map/pallas_call | solution.py:632
  2.7 12.4 %collective-permute-start = (bf16[8,48,128]{2,1,0:T(8,128)(2,1)S(1)}, bf16[8,48,128]{2,1,0:T(8,128)(2,1)S(1)}, u32[]{:S(2)}, u32[]{:S(2)}) collective-permute-start(bf16[8,48,128]{2,1,0:T(8,128)(2,1)S(1)} %get-tuple-element.55), channel_id=1, source_target_pairs={{0,8},{8,0},{16,24},{24,16},{32,40},{40,32},{48,56},{56,48},{64,72... | collective-permute-start | bytes 294920 | tf_op jit(solution)/shard_map/ppermute | solution.py:655
  15.2 0.0 copy-done
  15.2 0.0 copy-done.1
  15.2 1.1 %shard_map.87 = (f32[32,384]{1,0:T(8,128)S(1)}, f32[192,128]{1,0:T(8,128)S(1)}, f32[96,384]{1,0:T(8,128)S(1)}, f32[192,128]{1,0:T(8,128)S(1)}, f32[192,128]{1,0:...) custom-call(f32[32,384]{1,0:T(8,128)S(1)} %get-tuple-element.41.q_re, ...), custom_call_target="tpu_custom_call" | custom-call | flops 200000000 | bytes 1000000 | tf_op jit(solution)/shard_map/pallas_call | solution.py:632
  16.2 0.0 collective-permute-done
  16.3 11.6 %all_to_all.10.arrived_ref = bf16[16,96,128]{2,1,0:T(8,128)(2,1)S(1)} all-to-all(bf16[16,96,128]{2,1,0:T(8,128)(2,1)S(1)} %constant_dynamic-update-slice_fusion), channel_id=1, replica_groups={{8,9,10,11,12,13,14,15,16,17,18,19,20,21,22,23},{24,25,26,27,28,29,30,3..., dimensions={0} | all-to-all | bytes 786432 | tf_op jit(solution)/shard_map/all_to_all | solution.py:646
  28.0 2.3 %shard_map.88 = (bf16[16,48,128]{2,1,0:T(8,128)(2,1)S(1)}, f32[32,384]{1,0:T(8,128)S(1)}, f32[32,384]{1,0:T(8,128)S(1)}, f32[192,128]{1,0:T(8,128)S(1)}, f32[192...) custom-call(f32[32,384]{1,0:T(8,128)S(1)} %get-tuple-element.51.base_ref, ...), custom_call_target="tpu_custom_call" | custom-call | flops 200000000 | bytes 1000000 | tf_op jit(solution)/shard_map/pallas_call | solution.py:632
  30.2 14.8 %all_to_all.11.arrived_ref = bf16[16,48,128]{2,1,0:T(8,128)(2,1)S(1)} all-to-all(bf16[16,48,128]{2,1,0:T(8,128)(2,1)S(1)} %get-tuple-element.77), channel_id=1, replica_groups={{8,9,10,11,12,13,14,15,16,17,18,19,20,21,22,23},{24,25,26,27,28,29,30,3..., dimensions={0} | all-to-all | bytes 393216 | tf_op jit(solution)/shard_map/all_to_all | solution.py:646
  45.0 11.4 %collective-permute-start.1 = (bf16[8,32,128]{2,1,0:T(8,128)(2,1)S(1)}, bf16[8,32,128]{2,1,0:T(8,128)(2,1)S(1)}, u32[]{:S(2)}, u32[]{:S(2)}) collective-permute-start(bf16[8,32,128]{2,1,0:T(8,128)(2,1)S(1)} %slice_add_fusion), channel_id=1, source_target_pairs={{0,8},{8,0},{16,24},{24,16},{32,40},{40,32},{48,56},{56,48},{64,72... | collective-permute-start | bytes 196616 | tf_op jit(solution)/shard_map/ppermute | solution.py:655
  56.5 0.9 %shard_map.89 = (f32[32,384]{1,0:T(8,128)S(1)}, f32[32,384]{1,0:T(8,128)S(1)}) custom-call(f32[32,384]{1,0:T(8,128)S(1)} %get-tuple-element.41.q_ref, f32[32,384]{1,0:T(8,128)S(1)} %get-tuple-element.42.w_ref, f32[192,128]{1,0:T(8,128)S(1)} %get-tuple-element.43.t_ref, f32[192,128]{1,0:T(8,128)S(1)} %get-tuple-element.48.u_ref, ...), custom_call_target="tpu_custom_call" | custom-call | flops 200000000 | bytes 1000000 | tf_op jit(solution)/shard_map/pallas_call | solution.py:632
  57.4 0.0 collective-permute-done.1.chip_ref
  57.4 1.5 %shard_map.90 = (f32[5,32,64]{2,1,0:T(8,128)}, f32[5,32,64]{2,1,0:T(8,128)}) custom-call(f32[32,384]{1,0:T(8,128)S(1)} %get-tuple-element.75.end_base_ref, f32[32,384]{1,0:T(8,128)S(1)} %get-tuple-element.76.start_base_ref, bf16[8,32,128]{2,1,0:T(8,128)(2,1)S(1)} %collective-permute-done.1.chip_ref, bf16[16,48,128]{2,1,0:T(8,128)(2,1)S(1)} %all_to_all.11.arrived_ref, ...), custom_call_target="tpu_custom_call" | custom-call | flops 200000000 | bytes 1000000 | tf_op jit(solution)/shard_map/pallas_call | solution.py:632
  (3 shorter events, 0.0 us)
Async XLA Ops:
  0.6 14.5 %copy-start = (bf16[128,768]{1,0:T(8,128)(2,1)S(1)}, bf16[128,768]{1,0:T(8,128)(2,1)}, u32[]{:S(2)}) copy-start(bf16[128,768]{1,0:T(8,128)(2,1)} %constant.11.clone.backward_ref) | copy-start | bytes 589828
  0.6 14.5 %copy-start.1 = (bf16[384,256]{1,0:T(8,128)(2,1)S(1)}, bf16[384,256]{1,0:T(8,128)(2,1)}, u32[]{:S(2)}) copy-start(bf16[384,256]{1,0:T(8,128)(2,1)} %constant.10.clone.forward_ref) | copy-start | bytes 589828
  2.7 13.5 %collective-permute-start = (bf16[8,48,128]{2,1,0:T(8,128)(2,1)S(1)}, bf16[8,48,128]{2,1,0:T(8,128)(2,1)S(1)}, u32[]{:S(2)}, u32[]{:S(2)}) collective-permute-start(bf16[8,48,128]{2,1,0:T(8,128)(2,1)S(1)} %get-tuple-element.55), channel_id=1, source_target_pairs={{0,8},{8,0},{16,24},{24,16},{32,40},{40,32},{48,56},{56,48},{64,72... | collective-permute-start | bytes 294920 | tf_op jit(solution)/shard_map/ppermute | solution.py:655
  45.0 12.4 %collective-permute-start.1 = (bf16[8,32,128]{2,1,0:T(8,128)(2,1)S(1)}, bf16[8,32,128]{2,1,0:T(8,128)(2,1)S(1)}, u32[]{:S(2)}, u32[]{:S(2)}) collective-permute-start(bf16[8,32,128]{2,1,0:T(8,128)(2,1)S(1)} %slice_add_fusion), channel_id=1, source_target_pairs={{0,8},{8,0},{16,24},{24,16},{32,40},{40,32},{48,56},{56,48},{64,72... | collective-permute-start | bytes 196616 | tf_op jit(solution)/shard_map/ppermute | solution.py:655

commit v8 on v7

--- a/solution.py
+++ b/solution.py
@@ -494,7 +494,7 @@
 def middle_kernel(base_ref, t_base_ref, w_ref, lam_ref, rest_ref, z_ref, arrived_ref,
                   from_slots_ref, to_columns_ref, local_ref, local_back_ref, send_slots_ref, back_slots_ref,
                   index_ref, inverse_ref, kind_ref,
-                  out_ref, q1_ref, w1_ref, t1_ref, u1_ref, x1_ref, v1_ref, lam1_ref):
+                  chip_ref, out_ref, q1_ref, w1_ref, t1_ref, u1_ref, x1_ref, v1_ref, lam1_ref):
     faces = Faces()
     index = index_ref[...]
     inverse = inverse_ref[...]
@@ -554,16 +554,16 @@
     back = dot(back_slots_ref[...], jnp.concatenate([first, second], axis=1).astype(bf16))
     main = (back[:, :128] + forward).astype(bf16)
     tail = [back[G * o : G * (o + 1), 128:] for o in range(3)]
-    shared = (tail[0] + turn(tail[1], 32)).astype(bf16)
-    last = turn(tail[2], 64).astype(bf16)
+    tail = [tail[0].astype(bf16), turn(tail[1], 32).astype(bf16), turn(tail[2], 64).astype(bf16)]
+    zero = jnp.zeros((16, 128), bf16)
     for peer in range(8):
         at = 16 * peer
-        out_ref[own + peer, :16] = main[G + at : G + at + 16]
-        out_ref[own + peer, 16:32] = main[at : at + 16]
-        out_ref[own + peer, 32:] = shared[at : at + 16]
-        out_ref[other + peer, :16] = main[2 * G + at : 2 * G + at + 16]
-        out_ref[other + peer, 16:32] = jnp.zeros((16, 128), bf16)
-        out_ref[other + peer, 32:] = last[at : at + 16]
+        chip_ref[peer, :16] = main[at : at + 16]
+        chip_ref[peer, 16:] = tail[0][at : at + 16]
+        for o, place in ((1, own), (2, other)):
+            out_ref[place + peer, :16] = main[G * o + at : G * o + at + 16]
+            out_ref[place + peer, 16:32] = zero
+            out_ref[place + peer, 32:] = tail[o][at : at + 16]
 
 
 def second_local_kernel(q_ref, w_ref, t_ref, u_ref, x_ref, v_ref, q1_ref, w1_ref, t1_ref, u1_ref, x1_ref, v1_ref,
@@ -595,15 +595,16 @@
     store_tiles(start_ref, [0.5 * w[j] + w1[j] + step_size * (inner[j] + faced[j]) for j in range(3)])
 
 
-def last_kernel(end_base_ref, start_base_ref, chip_ref, arrived_ref, from_slots_ref, to_columns_ref, index_ref,
+def last_kernel(end_base_ref, start_base_ref, arrived_ref, from_slots_ref, to_columns_ref, index_ref,
                 end_ref, start_ref):
     faces = Faces()
     own, other = places()
-    main = jnp.concatenate([block_of(chip_ref, 0), block_of(arrived_ref, 0, own), block_of(arrived_ref, 0, other)], axis=0)
+    main = jnp.concatenate(
+        [block_of(arrived_ref, 16, own), block_of(arrived_ref, 0, own), block_of(arrived_ref, 0, other)], axis=0)
     lane = lanes(G)
     zero = jnp.zeros((G, 128), bf16)
     shared = jnp.concatenate([
-        jnp.where(lane < 32, block_of(chip_ref, 16), zero),
+        jnp.where(lane < 32, block_of(arrived_ref, 32, own), zero),
         jnp.where((lane >= 32) & (lane < 64), block_of(arrived_ref, 32, own), zero),
         jnp.where((lane >= 64) & (lane < 96), block_of(arrived_ref, 32, other), zero)], axis=0)
     node = index_ref[...] & 15
@@ -647,10 +648,6 @@
         whole, ("dom", "sub"), split_axis=0, concat_axis=0, tiled=True, axis_index_groups=groups)
 
 
-def for_chip(arrived):
-    return arrived[:8] + arrived[8:]
-
-
 def chip_partner(value):
     return lax.ppermute(value, "dom", [(d, d ^ 1) for d in range(lax.axis_size("dom"))])
 
@@ -680,19 +677,22 @@
     out = lax.dynamic_update_slice(out, from_chip, (8, 48, 0))
     out, z = lax.optimization_barrier((out, z))
     arrived = pair_peers(out)
-    out, q1, w1, t1, u1, x1, v1, lam1 = call(
-        middle_kernel, (shape(16, 48, 128, dtype=bf16), node, node, face, face, face, face, face),
+    to_chip, out, q1, w1, t1, u1, x1, v1, lam1 = call(
+        middle_kernel, (shape(8, 32, 128, dtype=bf16), shape(16, 48, 128, dtype=bf16), node, node, face, face, face, face, face),
         base, t_base, w, lam, rest, z, arrived,
         from_slots, to_columns, local, local_back, send_slots, back_slots, index, inverse, kind)
-    arrived = pair_peers(out)
+    from_chip = chip_partner(to_chip)
     end_base, start_base = call(
         second_local_kernel, (node, node),
         q, w, t, u, x, v, q1, w1, t1, u1, x1, v1, lam1, local_back, inverse, kind, forward, backward)
-    from_chip = chip_partner(for_chip(arrived[:, 16:]))
+    out = lax.dynamic_update_slice(out, out[:8, 16:] + from_chip, (0, 16, 0))
+    out = lax.dynamic_update_slice(out, out[8:, 16:] + from_chip, (8, 16, 0))
+    out, end_base = lax.optimization_barrier((out, end_base))
+    arrived = pair_peers(out)
     out = shape(5, E, 64)
     end, start = call(
         last_kernel, (out, out),
-        end_base, start_base, from_chip, arrived, from_slots, to_columns, index)
+        end_base, start_base, arrived, from_slots, to_columns, index)
     return jnp.swapaxes(end, 1, 2), jnp.swapaxes(start, 1, 2)
 
 

time: 59.1 us -> 58.1 us (0.983)
  the two profiles are of different devices: /device:TPU:1 before, /device:TPU:8 now
where the time goes in v8:
time: 58.1 us; the launch traced here: 57.9 us
  blocking collectives  45 us (77%)
  Pallas kernels  7.74 us (13%)
  starting transfers between devices  3.84 us (7%)
  between operations  0.72 us (1%)
    all_to_all x2, blocking collectives, pair_peers(): lax.all_to_all(whole, ('dom', 'sub'), split_axis=0, concat_axis=0, tiled=...  45 us
    pallas_call x5, Pallas kernels, call(): pl.pallas_call(kernel, out_shape=outs, in_specs=[pl.BlockSpec(memory_spac...  7.74 us
    ppermute x2, starting transfers between devices, chip_partner(): lax.ppermute(value, 'dom', [(d, d ^ 1) for d in range(lax.axis_size('dom'...  3.84 us
  transfers between devices with their start and end apart: 2, of which 2 were waited for; matrix products, arithmetic and copies ran while one was open for 0% of the time, Pallas kernels for 3%

profile of v8, /device:TPU:8, one launch (start us, length us, event | category | flops | bytes accessed | tf_op | source)
XLA Modules:
  0.0 57.9 jit_solution(14658846130831346817)
XLA Ops:
  0.6 0.0 copy-start
  0.6 0.0 copy-start.1
  0.7 2.1 %shard_map.86 = (bf16[8,48,128]{2,1,0:T(8,128)(2,1)S(1)}, bf16[16,96,128]{2,1,0:T(8,128)(2,1)S(1)}, f32[32,384]{1,0:T(8,128)S(1)}, f32[32,384]{1,0:T(8,128)S(1)}...) custom-call(f32[5,32,64]{2,1,0:T(8,128)} %bitcast.4, ...), custom_call_target="tpu_custom_call" | custom-call | flops 200000000 | bytes 1000000 | tf_op jit(solution)/shard_map/pallas_call | solution.py:633
  2.7 1.9 %collective-permute-start = (bf16[8,48,128]{2,1,0:T(8,128)(2,1)S(1)}, bf16[8,48,128]{2,1,0:T(8,128)(2,1)S(1)}, u32[]{:S(2)}, u32[]{:S(2)}) collective-permute-start(bf16[8,48,128]{2,1,0:T(8,128)(2,1)S(1)} %get-tuple-element.55), channel_id=1, source_target_pairs={{0,8},{8,0},{16,24},{24,16},{32,40},{40,32},{48,56},{56,48},{64,72... | collective-permute-start | bytes 294920 | tf_op jit(solution)/shard_map/ppermute | solution.py:652
  4.7 0.0 copy-done
  4.7 0.0 copy-done.1
  4.7 1.1 %shard_map.87 = (f32[32,384]{1,0:T(8,128)S(1)}, f32[192,128]{1,0:T(8,128)S(1)}, f32[96,384]{1,0:T(8,128)S(1)}, f32[192,128]{1,0:T(8,128)S(1)}, f32[192,128]{1,0:...) custom-call(f32[32,384]{1,0:T(8,128)S(1)} %get-tuple-element.44.q_re, ...), custom_call_target="tpu_custom_call" | custom-call | flops 200000000 | bytes 1000000 | tf_op jit(solution)/shard_map/pallas_call | solution.py:633
  5.7 0.2 collective-permute-done
  6.0 29.4 %all_to_all.10.arrived_ref = bf16[16,96,128]{2,1,0:T(8,128)(2,1)S(1)} all-to-all(bf16[16,96,128]{2,1,0:T(8,128)(2,1)S(1)} %constant_dynamic-update-slice_fusion), channel_id=1, replica_groups={{8,9,10,11,12,13,14,15,16,17,18,19,20,21,22,23},{24,25,26,27,28,29,30,3..., dimensions={0} | all-to-all | bytes 786432 | tf_op jit(solution)/shard_map/all_to_all | solution.py:647
  35.3 2.3 %shard_map.88 = (bf16[8,32,128]{2,1,0:T(8,128)(2,1)S(1)}, bf16[16,48,128]{2,1,0:T(8,128)(2,1)S(1)}, f32[32,384]{1,0:T(8,128)S(1)}, f32[32,384]{1,0:T(8,128)S(1)}...) custom-call(f32[32,384]{1,0:T(8,128)S(1)} %get-tuple-element.51.base, ...), custom_call_target="tpu_custom_call" | custom-call | flops 200000000 | bytes 1000000 | tf_op jit(solution)/shard_map/pallas_call | solution.py:633
  37.6 1.9 %collective-permute-start.1 = (bf16[8,32,128]{2,1,0:T(8,128)(2,1)S(1)}, bf16[8,32,128]{2,1,0:T(8,128)(2,1)S(1)}, u32[]{:S(2)}, u32[]{:S(2)}) collective-permute-start(bf16[8,32,128]{2,1,0:T(8,128)(2,1)S(1)} %get-tuple-element.69), channel_id=1, source_target_pairs={{0,8},{8,0},{16,24},{24,16},{32,40},{40,32},{48,56},{56,48},{64,72... | collective-permute-start | bytes 196616 | tf_op jit(solution)/shard_map/ppermute | solution.py:652
  39.6 0.9 %shard_map.89 = (f32[32,384]{1,0:T(8,128)S(1)}, f32[32,384]{1,0:T(8,128)S(1)}) custom-call(f32[32,384]{1,0:T(8,128)S(1)} %get-tuple-element.44.q_ref, f32[32,384]{1,0:T(8,128)S(1)} %get-tuple-element.45.w_ref, f32[192,128]{1,0:T(8,128)S(1)} %get-tuple-element.46.t_ref, f32[192,128]{1,0:T(8,128)S(1)} %get-tuple-element.70.u_ref, ...), custom_call_target="tpu_custom_call" | custom-call | flops 200000000 | bytes 1000000 | tf_op jit(solution)/shard_map/pallas_call | solution.py:633
  40.5 0.3 collective-permute-done.1
  40.8 15.6 %all_to_all.11.arrived_ref = bf16[16,48,128]{2,1,0:T(8,128)(2,1)S(1)} all-to-all(bf16[16,48,128]{2,1,0:T(8,128)(2,1)S(1)} %fusion), channel_id=1, replica_groups={{8,9,10,11,12,13,14,15,16,17,18,19,20,21,22,23},{24,25,26,27,28,29,30,3..., dimensions={0} | all-to-all | bytes 393216 | tf_op jit(solution)/shard_map/all_to_all | solution.py:647
  56.4 1.4 %shard_map.90 = (f32[5,32,64]{2,1,0:T(8,128)}, f32[5,32,64]{2,1,0:T(8,128)}) custom-call(f32[32,384]{1,0:T(8,128)S(1)} %get-tuple-element.81.end_base_ref, f32[32,384]{1,0:T(8,128)S(1)} %get-tuple-element.82.start_base_ref, bf16[16,48,128]{2,1,0:T(8,128)(2,1)S(1)} %all_to_all.11.arrived_ref, bf16[192,384]{1,0:T(8,128)(2,1)S(1)} %get-tuple-element.59.from_slots_ref, ...), custom_call_target="tpu_custom_call" | custom-call | flops 200000000 | bytes 1000000 | tf_op jit(solution)/shard_map/pallas_call | solution.py:633
  (4 shorter events, 0.1 us)
Async XLA Ops:
  0.6 4.0 %copy-start = (bf16[128,768]{1,0:T(8,128)(2,1)S(1)}, bf16[128,768]{1,0:T(8,128)(2,1)}, u32[]{:S(2)}) copy-start(bf16[128,768]{1,0:T(8,128)(2,1)} %constant.13.clone.backward_ref) | copy-start | bytes 589828
  0.6 4.0 %copy-start.1 = (bf16[384,256]{1,0:T(8,128)(2,1)S(1)}, bf16[384,256]{1,0:T(8,128)(2,1)}, u32[]{:S(2)}) copy-start(bf16[384,256]{1,0:T(8,128)(2,1)} %constant.12.clone.forward_ref) | copy-start | bytes 589828
  2.7 3.2 %collective-permute-start = (bf16[8,48,128]{2,1,0:T(8,128)(2,1)S(1)}, bf16[8,48,128]{2,1,0:T(8,128)(2,1)S(1)}, u32[]{:S(2)}, u32[]{:S(2)}) collective-permute-start(bf16[8,48,128]{2,1,0:T(8,128)(2,1)S(1)} %get-tuple-element.55), channel_id=1, source_target_pairs={{0,8},{8,0},{16,24},{24,16},{32,40},{40,32},{48,56},{56,48},{64,72... | collective-permute-start | bytes 294920 | tf_op jit(solution)/shard_map/ppermute | solution.py:652
  37.6 3.1 %collective-permute-start.1 = (bf16[8,32,128]{2,1,0:T(8,128)(2,1)S(1)}, bf16[8,32,128]{2,1,0:T(8,128)(2,1)S(1)}, u32[]{:S(2)}, u32[]{:S(2)}) collective-permute-start(bf16[8,32,128]{2,1,0:T(8,128)(2,1)S(1)} %get-tuple-element.69), channel_id=1, source_target_pairs={{0,8},{8,0},{16,24},{24,16},{32,40},{40,32},{48,56},{56,48},{64,72... | collective-permute-start | bytes 196616 | tf_op jit(solution)/shard_map/ppermute | solution.py:652

commit v9 on v8

--- a/solution.py
+++ b/solution.py
@@ -393,9 +393,9 @@
 
 
 def packed(x):
-    tail = lanes(F) >= 80
-    first = jnp.where(tail, turn(x, 80), 0.0)
-    second = jnp.where(tail, turn(x, 32), 0.0)
+    lane = lanes(F)
+    first = jnp.where(lane >= 64, turn(x, 64), 0.0)
+    second = jnp.where((lane >= 80) & (lane < 96), turn(x, 16), 0.0)
     return jnp.concatenate([first, second], axis=1).astype(bf16)
 
 
@@ -407,13 +407,21 @@
     return x, jnp.where(wall, -u, v)
 
 
+def folded(x):
+    y = x.reshape(8, 16, 128)
+    return (y[:, :8].reshape(64, 128) + turn(y[:, 8:].reshape(64, 128), 64)).reshape(8, 8, 128)
+
+
+def unfolded(z):
+    z = z.reshape(64, 128)
+    low = mask(lanes() < 64)
+    halves = [(low * part).reshape(8, 8, 128) for part in (z, turn(z, 64))]
+    return jnp.concatenate(halves, axis=1).reshape(G, 128)
+
+
 def places():
     own = jnp.where((lax.axis_index("dom") & 1) == 1, 0, 8)
     return own, 8 - own
-
-
-def block_of(ref, row, start=0):
-    return ref[pl.ds(start, 8), row : row + 16].reshape(G, 128)
 
 
 def pack_kernel(state_hbm, final_hbm, send_hbm, ext_hbm, perm_hbm,
@@ -449,13 +457,19 @@
     stack = jnp.concatenate([x.astype(bf16) for x in (first, faces.hessian(1, y), faces.hessian(2, y))], axis=1)
     back = dot(back_slots, stack)
     forward = dot(send_slots, packed(t))
-    whole = jnp.concatenate([back[:, :128], back[:, 128:] + forward], axis=1).astype(bf16)
+    parts = [back[:, :128], back[:, 128:256] + forward[:, :128], back[:, 256:] + forward[:, 128:]]
     own, other = places()
+    lane = lanes()
+    guest = mask(lane >= 96) * turn(parts[2][:G], 32)
+    rest = folded(mask(lane < 64) * parts[2][:G])
     for peer in range(8):
-        for o, ref, place in ((0, chip_ref, 0), (1, out_ref, own), (2, out_ref, other)):
+        at = 16 * peer
+        chip_ref[peer] = jnp.concatenate(
+            [guest[at : at + 16], parts[0][at : at + 16], parts[1][at : at + 16], rest[peer]], axis=0).astype(bf16)
+        for o, place in ((1, own), (2, other)):
             at = G * o + 16 * peer
             for j in range(3):
-                ref[place + peer, 16 * j : 16 * (j + 1)] = whole[at : at + 16, 128 * j : 128 * (j + 1)]
+                out_ref[place + peer, 16 * j : 16 * (j + 1)] = parts[j][at : at + 16].astype(bf16)
 
 
 def first_local_kernel(q_ref, w_ref, t_ref, lam_ref, send_ref, ext_ref, perm_ref, forward_ref, backward_ref,
@@ -504,17 +518,25 @@
     lane = lanes()
     node = index & 15
     own, other = places()
-    arrived = jnp.concatenate(
-        [jnp.concatenate([block_of(arrived_ref, row + 16 * j, start) for j in range(3)], axis=1)
-         for row, start in ((48, own), (0, own), (0, other))], axis=0)
-    g = dot(from_slots_ref[...], arrived[:, 128:])
-    sums = dot(to_columns_ref[...], arrived)
+    mine, theirs = arrived_ref[pl.ds(own, 8)], arrived_ref[pl.ds(other, 8)]
+    third = mine[:, 32:48].reshape(G, 128)
+    guest = mask((lane >= 64) & (lane < 96)) * turn(third.astype(f32), 96)
+    rest = unfolded(mine[:, 80:].astype(f32))
+    kept = lanes(G) < 96
+    zero = jnp.zeros((G, 128), bf16)
+    third = jnp.concatenate(
+        [jnp.where(kept, third, zero), jnp.where(kept, theirs[:, 32:48].reshape(G, 128), zero)], axis=0)
+    tiles = [jnp.concatenate([x.reshape(G, 128) for x in blocks], axis=0) for blocks in (
+        (mine[:, 48:64], mine[:, :16], theirs[:, :16]), (mine[:, 64:80], mine[:, 16:32], theirs[:, 16:32]))]
+    g = dot(from_slots_ref[...], jnp.concatenate(
+        [tiles[1], jnp.concatenate([guest.astype(bf16), third], axis=0)], axis=1))
+    sums = dot(to_columns_ref[...], jnp.concatenate(
+        tiles + [jnp.concatenate([(guest + rest).astype(bf16), third], axis=0)], axis=1))
     g0, g1 = g[:, :128], g[:, 128:]
-    place = jnp.where(wide < 48, index + 80, jnp.where(wide < 80, index + 32, 112 + node))
-    xr = jnp.where(wide < 48, take(g0, place), take(g1, place))
-    ur = jnp.concatenate(
-        [take(g0[:64], 96 + node[:64]), take(g0[64:128], 112 + node[64:128]), take(g1[128:], 80 + node[128:])], axis=0)
-    pr = take(g1, 96 + node)
+    place = jnp.where(wide < 64, index + 64, jnp.where(wide < 80, index + 16, 96 + node))
+    xr = jnp.where(wide < 64, take(g0, place), take(g1, place))
+    ur = by_axis(lambda a, g, node: take(g, 80 + 16 * a + node), g0, node)
+    pr = take(g1, 80 + node)
     jump = (lift_factor * step_size) * (xr - 0.5 * faces.flux(xr, ur, pr))
     t1 = t_base_ref[...] + lifted_traces(jump)
     faced = lifted(jump)
@@ -535,7 +557,7 @@
     total = 0.5 * faces.state_back(t1, u1, lam) - rest + jnp.where(wall, faces.mirror(bar), 0.0)
     total = total + select_rows(local_back_ref[...], take(bar, inverse))
     sent = t1_sent.astype(f32)
-    h0, h1, h2 = sums[:, :128], sums[:, 128:256], sums[:, 256:]
+    h0, h1, h2 = sums[:, :128], mask(lane < 64) * sums[:, 128:256], sums[:, 256:]
     ahead1, ahead2, behind2, behind1 = [faces.shifted(d)[1] for d in (1, 2, 3, 4)]
     through = h0 + h1 * take(sent, ahead1) + h2 * take(sent, ahead2)
     through = through + take(h1 * sent, behind1) + take(h2 * sent, behind2)
@@ -552,18 +574,15 @@
     first = take(bar, jnp.where(wide >= 80, inverse - 80, 80))
     second = take(bar, jnp.where(wide < 32, inverse + 48, 80))
     back = dot(back_slots_ref[...], jnp.concatenate([first, second], axis=1).astype(bf16))
-    main = (back[:, :128] + forward).astype(bf16)
-    tail = [back[G * o : G * (o + 1), 128:] for o in range(3)]
-    tail = [tail[0].astype(bf16), turn(tail[1], 32).astype(bf16), turn(tail[2], 64).astype(bf16)]
-    zero = jnp.zeros((16, 128), bf16)
+    main = back[:, :128] + forward
+    tail = [folded(back[:G, 128:])] + [folded(turn(back[G * o : G * (o + 1), 128:], 32)) for o in (1, 2)]
+    zero = jnp.zeros((16, 128), f32)
     for peer in range(8):
         at = 16 * peer
-        chip_ref[peer, :16] = main[at : at + 16]
-        chip_ref[peer, 16:] = tail[0][at : at + 16]
+        chip_ref[peer] = jnp.concatenate([main[at : at + 16], tail[0][peer]], axis=0).astype(bf16)
         for o, place in ((1, own), (2, other)):
-            out_ref[place + peer, :16] = main[G * o + at : G * o + at + 16]
-            out_ref[place + peer, 16:32] = zero
-            out_ref[place + peer, 32:] = tail[o][at : at + 16]
+            at = G * o + 16 * peer
+            out_ref[place + peer] = jnp.concatenate([main[at : at + 16], zero, tail[o][peer]], axis=0).astype(bf16)
 
 
 def second_local_kernel(q_ref, w_ref, t_ref, u_ref, x_ref, v_ref, q1_ref, w1_ref, t1_ref, u1_ref, x1_ref, v1_ref,
@@ -599,14 +618,13 @@
                 end_ref, start_ref):
     faces = Faces()
     own, other = places()
+    mine, theirs = arrived_ref[pl.ds(own, 8)], arrived_ref[pl.ds(other, 8)]
     main = jnp.concatenate(
-        [block_of(arrived_ref, 16, own), block_of(arrived_ref, 0, own), block_of(arrived_ref, 0, other)], axis=0)
-    lane = lanes(G)
-    zero = jnp.zeros((G, 128), bf16)
-    shared = jnp.concatenate([
-        jnp.where(lane < 32, block_of(arrived_ref, 32, own), zero),
-        jnp.where((lane >= 32) & (lane < 64), block_of(arrived_ref, 32, own), zero),
-        jnp.where((lane >= 64) & (lane < 96), block_of(arrived_ref, 32, other), zero)], axis=0)
+        [mine[:, 16:32].reshape(G, 128), mine[:, :16].reshape(G, 128), theirs[:, :16].reshape(G, 128)], axis=0)
+    lane = lanes()
+    tail, next_tail = unfolded(mine[:, 32:].astype(f32)), unfolded(theirs[:, 32:].astype(f32))
+    late = mask(lane >= 32)
+    shared = jnp.concatenate([mask(lane < 32) * tail, late * tail, late * next_tail], axis=0).astype(bf16)
     node = index_ref[...] & 15
     g = dot(from_slots_ref[...], main)
     b = dot(to_columns_ref[...], jnp.concatenate([main, shared], axis=1))
@@ -618,7 +636,7 @@
     faced = lifted((0.5 * step_size * lift_factor) * (xr - 0.5 * faces.flux(xr, ur, pr)))
     base = load_tiles(end_base_ref)
     from_tiles([base[j] + faced[j] for j in range(3)], end_ref)
-    high = turn(b[:, 128:], 48) + turn(b[:, 128:], 16) + turn(b[:, 128:], 112)
+    high = turn(b[:, 128:], 48) + turn(b[:, 128:], 16)
     bar = mask(lane < 48) * turn(b[:, :128], 48) + mask((lane >= 48) & (lane < 80)) * high
     faced = lifted(step_size * bar)
     base = load_tiles(start_base_ref)
@@ -662,7 +680,7 @@
 
     to_chip, out, q, w, t, lam, send_slots, back_slots, inverse, send_slot, ext_index, ext_perm = call(
         pack_kernel,
-        (shape(8, 48, 128, dtype=bf16), shape(16, 96, 128, dtype=bf16), node, node, face, face,
+        (shape(8, 56, 128, dtype=bf16), shape(16, 88, 128, dtype=bf16), node, node, face, face,
          shape(S, F, dtype=bf16), shape(S, F, dtype=bf16), index_face,
          shape(1, S, dtype=i32), shape(6, E, dtype=i32), shape(6, E, dtype=i32)),
         *[pltpu.with_memory_space_constraint(x, pltpu.HBM) for x in (state, adjoint_final, send_slot, ext_index, ext_perm)], in_hbm=True,
@@ -673,12 +691,13 @@
         (node, face, shape(96, 384), face, face, face, face, shape(F, S, dtype=bf16), shape(F, S, dtype=bf16),
          shape(F, F, dtype=bf16), shape(F, F, dtype=bf16), index_face, index_face),
         q, w, t, lam, send_slot, ext_index, ext_perm, forward, backward)
-    out = lax.dynamic_update_slice(out, from_chip, (0, 48, 0))
-    out = lax.dynamic_update_slice(out, from_chip, (8, 48, 0))
+    for start in (0, 8):
+        out = lax.dynamic_update_slice(out, from_chip[:, 16:], (start, 48, 0))
+        out = lax.dynamic_update_slice(out, out[start : start + 8, 32:48] + from_chip[:, :16], (start, 32, 0))
     out, z = lax.optimization_barrier((out, z))
     arrived = pair_peers(out)
     to_chip, out, q1, w1, t1, u1, x1, v1, lam1 = call(
-        middle_kernel, (shape(8, 32, 128, dtype=bf16), shape(16, 48, 128, dtype=bf16), node, node, face, face, face, face, face),
+        middle_kernel, (shape(8, 24, 128, dtype=bf16), shape(16, 40, 128, dtype=bf16), node, node, face, face, face, face, face),
         base, t_base, w, lam, rest, z, arrived,
         from_slots, to_columns, local, local_back, send_slots, back_slots, index, inverse, kind)
     from_chip = chip_partner(to_chip)

time: 58.1 us -> 57.5 us (0.990)
  blocking collectives: 45 us -> 44.2 us
    all_to_all x2, blocking collectives: 45 us -> 44.2 us  [pair_peers(): lax.all_to_all(whole, ('dom', 'sub'), split_axis=0, concat_axis=0, tiled=...]
where the time goes in v9:
time: 57.5 us; the launch traced here: 57.3 us
  blocking collectives  44.2 us (77%)
  Pallas kernels  7.9 us (14%)
  starting transfers between devices  3.84 us (7%)
  between operations  0.73 us (1%)
    all_to_all x2, blocking collectives, pair_peers(): lax.all_to_all(whole, ('dom', 'sub'), split_axis=0, concat_axis=0, tiled=...  44.2 us
    pallas_call x5, Pallas kernels, call(): pl.pallas_call(kernel, out_shape=outs, in_specs=[pl.BlockSpec(memory_spac...  7.9 us
    ppermute x2, starting transfers between devices, chip_partner(): lax.ppermute(value, 'dom', [(d, d ^ 1) for d in range(lax.axis_size('dom'...  3.84 us
  transfers between devices with their start and end apart: 2, of which 2 were waited for; matrix products, arithmetic and copies ran while one was open for 0% of the time, Pallas kernels for 3%

profile of v9, /device:TPU:8, one launch (start us, length us, event | category | flops | bytes accessed | tf_op | source)
XLA Modules:
  0.0 57.3 jit_solution(361925194525499804)
XLA Ops:
  0.6 0.0 copy-start
  0.6 0.0 copy-start.1
  0.7 2.1 %shard_map.86 = (bf16[8,56,128]{2,1,0:T(8,128)(2,1)S(1)}, bf16[16,88,128]{2,1,0:T(8,128)(2,1)S(1)}, f32[32,384]{1,0:T(8,128)S(1)}, f32[32,384]{1,0:T(8,128)S(1)}...) custom-call(f32[5,32,64]{2,1,0:T(8,128)} %bitcast.4, ...), custom_call_target="tpu_custom_call" | custom-call | flops 200000000 | bytes 1000000 | tf_op jit(solution)/shard_map/pallas_call | solution.py:651
  2.7 1.9 %collective-permute-start = (bf16[8,56,128]{2,1,0:T(8,128)(2,1)S(1)}, bf16[8,56,128]{2,1,0:T(8,128)(2,1)S(1)}, u32[]{:S(2)}, u32[]{:S(2)}) collective-permute-start(bf16[8,56,128]{2,1,0:T(8,128)(2,1)S(1)} %get-tuple-element.55), channel_id=1, source_target_pairs={{0,8},{8,0},{16,24},{24,16},{32,40},{40,32},{48,56},{56,48},{64,72... | collective-permute-start | bytes 344072 | tf_op jit(solution)/shard_map/ppermute | solution.py:670
  4.7 0.0 copy-done
  4.7 0.0 copy-done.1
  4.7 1.1 %shard_map.87 = (f32[32,384]{1,0:T(8,128)S(1)}, f32[192,128]{1,0:T(8,128)S(1)}, f32[96,384]{1,0:T(8,128)S(1)}, f32[192,128]{1,0:T(8,128)S(1)}, f32[192,128]{1,0:...) custom-call(f32[32,384]{1,0:T(8,128)S(1)} %get-tuple-element.44.q_re, ...), custom_call_target="tpu_custom_call" | custom-call | flops 200000000 | bytes 1000000 | tf_op jit(solution)/shard_map/pallas_call | solution.py:651
  5.7 0.2 collective-permute-done
  6.0 28.9 %all_to_all.10.arrived_ref = bf16[16,88,128]{2,1,0:T(8,128)(2,1)S(1)} all-to-all(bf16[16,88,128]{2,1,0:T(8,128)(2,1)S(1)} %fusion.1), channel_id=1, replica_groups={{8,9,10,11,12,13,14,15,16,17,18,19,20,21,22,23},{24,25,26,27,28,29,30,3..., dimensions={0} | all-to-all | bytes 720896 | tf_op jit(solution)/shard_map/all_to_all | solution.py:665
  35.0 2.5 %shard_map.88 = (bf16[8,24,128]{2,1,0:T(8,128)(2,1)S(1)}, bf16[16,40,128]{2,1,0:T(8,128)(2,1)S(1)}, f32[32,384]{1,0:T(8,128)S(1)}, f32[32,384]{1,0:T(8,128)S(1)}...) custom-call(f32[32,384]{1,0:T(8,128)S(1)} %get-tuple-element.51.base, ...), custom_call_target="tpu_custom_call" | custom-call | flops 200000000 | bytes 1000000 | tf_op jit(solution)/shard_map/pallas_call | solution.py:651
  37.4 1.9 %collective-permute-start.1 = (bf16[8,24,128]{2,1,0:T(8,128)(2,1)S(1)}, bf16[8,24,128]{2,1,0:T(8,128)(2,1)S(1)}, u32[]{:S(2)}, u32[]{:S(2)}) collective-permute-start(bf16[8,24,128]{2,1,0:T(8,128)(2,1)S(1)} %get-tuple-element.69), channel_id=1, source_target_pairs={{0,8},{8,0},{16,24},{24,16},{32,40},{40,32},{48,56},{56,48},{64,72... | collective-permute-start | bytes 147464 | tf_op jit(solution)/shard_map/ppermute | solution.py:670
  39.4 0.9 %shard_map.89 = (f32[32,384]{1,0:T(8,128)S(1)}, f32[32,384]{1,0:T(8,128)S(1)}) custom-call(f32[32,384]{1,0:T(8,128)S(1)} %get-tuple-element.44.q_ref, f32[32,384]{1,0:T(8,128)S(1)} %get-tuple-element.45.w_ref, f32[192,128]{1,0:T(8,128)S(1)} %get-tuple-element.46.t_ref, f32[192,128]{1,0:T(8,128)S(1)} %get-tuple-element.70.u_ref, ...), custom_call_target="tpu_custom_call" | custom-call | flops 200000000 | bytes 1000000 | tf_op jit(solution)/shard_map/pallas_call | solution.py:651
  40.3 0.3 collective-permute-done.1
  40.6 15.3 %all_to_all.11.arrived_ref = bf16[16,40,128]{2,1,0:T(8,128)(2,1)S(1)} all-to-all(bf16[16,40,128]{2,1,0:T(8,128)(2,1)S(1)} %fusion), channel_id=1, replica_groups={{8,9,10,11,12,13,14,15,16,17,18,19,20,21,22,23},{24,25,26,27,28,29,30,3..., dimensions={0} | all-to-all | bytes 327680 | tf_op jit(solution)/shard_map/all_to_all | solution.py:665
  55.9 1.4 %shard_map.90 = (f32[5,32,64]{2,1,0:T(8,128)}, f32[5,32,64]{2,1,0:T(8,128)}) custom-call(f32[32,384]{1,0:T(8,128)S(1)} %get-tuple-element.81.end_base_ref, f32[32,384]{1,0:T(8,128)S(1)} %get-tuple-element.82.start_base_ref, bf16[16,40,128]{2,1,0:T(8,128)(2,1)S(1)} %all_to_all.11.arrived_ref, bf16[192,384]{1,0:T(8,128)(2,1)S(1)} %get-tuple-element.59.from_slots_ref, ...), custom_call_target="tpu_custom_call" | custom-call | flops 200000000 | bytes 1000000 | tf_op jit(solution)/shard_map/pallas_call | solution.py:651
  (6 shorter events, 0.1 us)
Async XLA Ops:
  0.6 4.0 %copy-start = (bf16[128,768]{1,0:T(8,128)(2,1)S(1)}, bf16[128,768]{1,0:T(8,128)(2,1)}, u32[]{:S(2)}) copy-start(bf16[128,768]{1,0:T(8,128)(2,1)} %constant.15.clone.backward_ref) | copy-start | bytes 589828
  0.6 4.0 %copy-start.1 = (bf16[384,256]{1,0:T(8,128)(2,1)S(1)}, bf16[384,256]{1,0:T(8,128)(2,1)}, u32[]{:S(2)}) copy-start(bf16[384,256]{1,0:T(8,128)(2,1)} %constant.14.clone.forward_ref) | copy-start | bytes 589828
  2.7 3.2 %collective-permute-start = (bf16[8,56,128]{2,1,0:T(8,128)(2,1)S(1)}, bf16[8,56,128]{2,1,0:T(8,128)(2,1)S(1)}, u32[]{:S(2)}, u32[]{:S(2)}) collective-permute-start(bf16[8,56,128]{2,1,0:T(8,128)(2,1)S(1)} %get-tuple-element.55), channel_id=1, source_target_pairs={{0,8},{8,0},{16,24},{24,16},{32,40},{40,32},{48,56},{56,48},{64,72... | collective-permute-start | bytes 344072 | tf_op jit(solution)/shard_map/ppermute | solution.py:670
  37.4 3.1 %collective-permute-start.1 = (bf16[8,24,128]{2,1,0:T(8,128)(2,1)S(1)}, bf16[8,24,128]{2,1,0:T(8,128)(2,1)S(1)}, u32[]{:S(2)}, u32[]{:S(2)}) collective-permute-start(bf16[8,24,128]{2,1,0:T(8,128)(2,1)S(1)} %get-tuple-element.69), channel_id=1, source_target_pairs={{0,8},{8,0},{16,24},{24,16},{32,40},{40,32},{48,56},{56,48},{64,72... | collective-permute-start | bytes 147464 | tf_op jit(solution)/shard_map/ppermute | solution.py:670

commit v10 on v9

--- a/solution.py
+++ b/solution.py
@@ -410,6 +410,13 @@
 def folded(x):
     y = x.reshape(8, 16, 128)
     return (y[:, :8].reshape(64, 128) + turn(y[:, 8:].reshape(64, 128), 64)).reshape(8, 8, 128)
+
+
+def folded_copies(x, at):
+    y = x.reshape(8, 16, 128)
+    group = lanes() >> 5
+    low, high = mask(group == at), mask(group == at + 2)
+    return (low * y[:, :8].reshape(64, 128) + high * y[:, 8:].reshape(64, 128)).reshape(8, 8, 128)
 
 
 def unfolded(z):
@@ -572,10 +579,10 @@
     lam1_ref[...] = lam1
     bar = lam1 - 0.5 * faces.flux_back(xr, ur, lam1)
     first = take(bar, jnp.where(wide >= 80, inverse - 80, 80))
-    second = take(bar, jnp.where(wide < 32, inverse + 48, 80))
+    second = take(bar, (inverse & 15) + 48 + (wide & 16))
     back = dot(back_slots_ref[...], jnp.concatenate([first, second], axis=1).astype(bf16))
     main = back[:, :128] + forward
-    tail = [folded(back[:G, 128:])] + [folded(turn(back[G * o : G * (o + 1), 128:], 32)) for o in (1, 2)]
+    tail = [folded_copies(back[G * o : G * (o + 1), 128:], min(o, 1)) for o in range(3)]
     zero = jnp.zeros((16, 128), f32)
     for peer in range(8):
         at = 16 * peer
@@ -627,7 +634,7 @@
     shared = jnp.concatenate([mask(lane < 32) * tail, late * tail, late * next_tail], axis=0).astype(bf16)
     node = index_ref[...] & 15
     g = dot(from_slots_ref[...], main)
-    b = dot(to_columns_ref[...], jnp.concatenate([main, shared], axis=1))
+    b = jnp.concatenate([dot(to_columns_ref[...], main), dot(to_columns_ref[...], shared)], axis=1)
     lane = lanes()
     valid = mask(lane < 80)
     xr = valid * take(g, index_ref[...])

time: 57.5 us -> 57.4 us (level)
  no operation moved by 1% of the time
where the time goes in v10:
time: 57.4 us; the launch traced here: 57.1 us
  blocking collectives  44.2 us (77%)
  Pallas kernels  7.73 us (13%)
  starting transfers between devices  3.84 us (7%)
  between operations  0.73 us (1%)
    all_to_all x2, blocking collectives, pair_peers(): lax.all_to_all(whole, ('dom', 'sub'), split_axis=0, concat_axis=0, tiled=...  44.2 us
    pallas_call x5, Pallas kernels, call(): pl.pallas_call(kernel, out_shape=outs, in_specs=[pl.BlockSpec(memory_spac...  7.73 us
    ppermute x2, starting transfers between devices, chip_partner(): lax.ppermute(value, 'dom', [(d, d ^ 1) for d in range(lax.axis_size('dom'...  3.84 us
  transfers between devices with their start and end apart: 2, of which 2 were waited for; matrix products, arithmetic and copies ran while one was open for 0% of the time, Pallas kernels for 3%

profile of v10, /device:TPU:8, one launch (start us, length us, event | category | flops | bytes accessed | tf_op | source)
XLA Modules:
  0.0 57.1 jit_solution(13177914574211153032)
XLA Ops:
  0.6 0.0 copy-start
  0.6 0.0 copy-start.1
  0.7 2.1 %shard_map.86 = (bf16[8,56,128]{2,1,0:T(8,128)(2,1)S(1)}, bf16[16,88,128]{2,1,0:T(8,128)(2,1)S(1)}, f32[32,384]{1,0:T(8,128)S(1)}, f32[32,384]{1,0:T(8,128)S(1)}...) custom-call(f32[5,32,64]{2,1,0:T(8,128)} %bitcast.4, ...), custom_call_target="tpu_custom_call" | custom-call | flops 200000000 | bytes 1000000 | tf_op jit(solution)/shard_map/pallas_call | solution.py:658
  2.7 1.9 %collective-permute-start = (bf16[8,56,128]{2,1,0:T(8,128)(2,1)S(1)}, bf16[8,56,128]{2,1,0:T(8,128)(2,1)S(1)}, u32[]{:S(2)}, u32[]{:S(2)}) collective-permute-start(bf16[8,56,128]{2,1,0:T(8,128)(2,1)S(1)} %get-tuple-element.55), channel_id=1, source_target_pairs={{0,8},{8,0},{16,24},{24,16},{32,40},{40,32},{48,56},{56,48},{64,72... | collective-permute-start | bytes 344072 | tf_op jit(solution)/shard_map/ppermute | solution.py:677
  4.7 0.0 copy-done
  4.7 0.0 copy-done.1
  4.7 1.1 %shard_map.87 = (f32[32,384]{1,0:T(8,128)S(1)}, f32[192,128]{1,0:T(8,128)S(1)}, f32[96,384]{1,0:T(8,128)S(1)}, f32[192,128]{1,0:T(8,128)S(1)}, f32[192,128]{1,0:...) custom-call(f32[32,384]{1,0:T(8,128)S(1)} %get-tuple-element.44.q_re, ...), custom_call_target="tpu_custom_call" | custom-call | flops 200000000 | bytes 1000000 | tf_op jit(solution)/shard_map/pallas_call | solution.py:658
  5.7 0.2 collective-permute-done
  6.0 28.9 %all_to_all.10.arrived_ref = bf16[16,88,128]{2,1,0:T(8,128)(2,1)S(1)} all-to-all(bf16[16,88,128]{2,1,0:T(8,128)(2,1)S(1)} %fusion.1), channel_id=1, replica_groups={{8,9,10,11,12,13,14,15,16,17,18,19,20,21,22,23},{24,25,26,27,28,29,30,3..., dimensions={0} | all-to-all | bytes 720896 | tf_op jit(solution)/shard_map/all_to_all | solution.py:672
  35.0 2.3 %shard_map.88 = (bf16[8,24,128]{2,1,0:T(8,128)(2,1)S(1)}, bf16[16,40,128]{2,1,0:T(8,128)(2,1)S(1)}, f32[32,384]{1,0:T(8,128)S(1)}, f32[32,384]{1,0:T(8,128)S(1)}...) custom-call(f32[32,384]{1,0:T(8,128)S(1)} %get-tuple-element.51.base, ...), custom_call_target="tpu_custom_call" | custom-call | flops 200000000 | bytes 1000000 | tf_op jit(solution)/shard_map/pallas_call | solution.py:658
  37.3 1.9 %collective-permute-start.1 = (bf16[8,24,128]{2,1,0:T(8,128)(2,1)S(1)}, bf16[8,24,128]{2,1,0:T(8,128)(2,1)S(1)}, u32[]{:S(2)}, u32[]{:S(2)}) collective-permute-start(bf16[8,24,128]{2,1,0:T(8,128)(2,1)S(1)} %get-tuple-element.69), channel_id=1, source_target_pairs={{0,8},{8,0},{16,24},{24,16},{32,40},{40,32},{48,56},{56,48},{64,72... | collective-permute-start | bytes 147464 | tf_op jit(solution)/shard_map/ppermute | solution.py:677
  39.2 0.9 %shard_map.89 = (f32[32,384]{1,0:T(8,128)S(1)}, f32[32,384]{1,0:T(8,128)S(1)}) custom-call(f32[32,384]{1,0:T(8,128)S(1)} %get-tuple-element.44.q_ref, f32[32,384]{1,0:T(8,128)S(1)} %get-tuple-element.45.w_ref, f32[192,128]{1,0:T(8,128)S(1)} %get-tuple-element.46.t_ref, f32[192,128]{1,0:T(8,128)S(1)} %get-tuple-element.70.u_ref, ...), custom_call_target="tpu_custom_call" | custom-call | flops 200000000 | bytes 1000000 | tf_op jit(solution)/shard_map/pallas_call | solution.py:658
  40.1 0.3 collective-permute-done.1
  40.4 15.3 %all_to_all.11.arrived_ref = bf16[16,40,128]{2,1,0:T(8,128)(2,1)S(1)} all-to-all(bf16[16,40,128]{2,1,0:T(8,128)(2,1)S(1)} %fusion), channel_id=1, replica_groups={{8,9,10,11,12,13,14,15,16,17,18,19,20,21,22,23},{24,25,26,27,28,29,30,3..., dimensions={0} | all-to-all | bytes 327680 | tf_op jit(solution)/shard_map/all_to_all | solution.py:672
  55.7 1.4 %shard_map.90 = (f32[5,32,64]{2,1,0:T(8,128)}, f32[5,32,64]{2,1,0:T(8,128)}) custom-call(f32[32,384]{1,0:T(8,128)S(1)} %get-tuple-element.81.end_base_ref, f32[32,384]{1,0:T(8,128)S(1)} %get-tuple-element.82.start_base_ref, bf16[16,40,128]{2,1,0:T(8,128)(2,1)S(1)} %all_to_all.11.arrived_ref, bf16[192,384]{1,0:T(8,128)(2,1)S(1)} %get-tuple-element.59.from_slots_ref, ...), custom_call_target="tpu_custom_call" | custom-call | flops 200000000 | bytes 1000000 | tf_op jit(solution)/shard_map/pallas_call | solution.py:658
  (6 shorter events, 0.1 us)
Async XLA Ops:
  0.6 4.0 %copy-start = (bf16[128,768]{1,0:T(8,128)(2,1)S(1)}, bf16[128,768]{1,0:T(8,128)(2,1)}, u32[]{:S(2)}) copy-start(bf16[128,768]{1,0:T(8,128)(2,1)} %constant.15.clone.backward_ref) | copy-start | bytes 589828
  0.6 4.0 %copy-start.1 = (bf16[384,256]{1,0:T(8,128)(2,1)S(1)}, bf16[384,256]{1,0:T(8,128)(2,1)}, u32[]{:S(2)}) copy-start(bf16[384,256]{1,0:T(8,128)(2,1)} %constant.14.clone.forward_ref) | copy-start | bytes 589828
  2.7 3.2 %collective-permute-start = (bf16[8,56,128]{2,1,0:T(8,128)(2,1)S(1)}, bf16[8,56,128]{2,1,0:T(8,128)(2,1)S(1)}, u32[]{:S(2)}, u32[]{:S(2)}) collective-permute-start(bf16[8,56,128]{2,1,0:T(8,128)(2,1)S(1)} %get-tuple-element.55), channel_id=1, source_target_pairs={{0,8},{8,0},{16,24},{24,16},{32,40},{40,32},{48,56},{56,48},{64,72... | collective-permute-start | bytes 344072 | tf_op jit(solution)/shard_map/ppermute | solution.py:677
  37.3 3.1 %collective-permute-start.1 = (bf16[8,24,128]{2,1,0:T(8,128)(2,1)S(1)}, bf16[8,24,128]{2,1,0:T(8,128)(2,1)S(1)}, u32[]{:S(2)}, u32[]{:S(2)}) collective-permute-start(bf16[8,24,128]{2,1,0:T(8,128)(2,1)S(1)} %get-tuple-element.69), channel_id=1, source_target_pairs={{0,8},{8,0},{16,24},{24,16},{32,40},{40,32},{48,56},{56,48},{64,72... | collective-permute-start | bytes 147464 | tf_op jit(solution)/shard_map/ppermute | solution.py:677

commit v11 on v10

--- a/solution.py
+++ b/solution.py
@@ -488,7 +488,7 @@
     index_ref[...] = index
     ext_wide = jnp.broadcast_to(ext_col, (F, 128))
     wall = ext_wide == F + S
-    kind_ref[...] = jnp.where(wall, 2, jnp.where(ext_wide >= F, 1, 0))
+    kind_ref[...] = jnp.where(wall, 2, jnp.where(ext_wide >= F + G, 1, jnp.where(ext_wide >= F, 3, 0)))
     from_slots_ref[...] = faces_from_slots(ext_col)
     to_columns_ref[...] = columns_from_slots(send)
     local = faces_from_columns(ext_col)
@@ -526,7 +526,7 @@
     node = index & 15
     own, other = places()
     mine, theirs = arrived_ref[pl.ds(own, 8)], arrived_ref[pl.ds(other, 8)]
-    third = mine[:, 32:48].reshape(G, 128)
+    third = raw = mine[:, 32:48].reshape(G, 128)
     guest = mask((lane >= 64) & (lane < 96)) * turn(third.astype(f32), 96)
     rest = unfolded(mine[:, 80:].astype(f32))
     kept = lanes(G) < 96
@@ -536,14 +536,15 @@
     tiles = [jnp.concatenate([x.reshape(G, 128) for x in blocks], axis=0) for blocks in (
         (mine[:, 48:64], mine[:, :16], theirs[:, :16]), (mine[:, 64:80], mine[:, 16:32], theirs[:, 16:32]))]
     g = dot(from_slots_ref[...], jnp.concatenate(
-        [tiles[1], jnp.concatenate([guest.astype(bf16), third], axis=0)], axis=1))
+        [tiles[1], jnp.concatenate([raw, raw, theirs[:, 32:48].reshape(G, 128)], axis=0)], axis=1))
     sums = dot(to_columns_ref[...], jnp.concatenate(
         tiles + [jnp.concatenate([(guest + rest).astype(bf16), third], axis=0)], axis=1))
     g0, g1 = g[:, :128], g[:, 128:]
-    place = jnp.where(wide < 64, index + 64, jnp.where(wide < 80, index + 16, 96 + node))
-    xr = jnp.where(wide < 64, take(g0, place), take(g1, place))
+    guest_at = (kind & 2) * 16
+    place = jnp.where(wide < 64, index + 64, 80 + guest_at + node)
+    xr = jnp.where(wide < 64, take(g0, place), mask(lane < 80) * take(g1, place))
     ur = by_axis(lambda a, g, node: take(g, 80 + 16 * a + node), g0, node)
-    pr = take(g1, 80 + node)
+    pr = take(g1, 80 + guest_at + node)
     jump = (lift_factor * step_size) * (xr - 0.5 * faces.flux(xr, ur, pr))
     t1 = t_base_ref[...] + lifted_traces(jump)
     faced = lifted(jump)
@@ -560,7 +561,7 @@
     x1, v1 = exterior(faces, wall, index, local_ref[...], t1, u1)
     x1_ref[...] = x1
     v1_ref[...] = v1
-    bar = jnp.where(kind == 1, 0.0, rest - 0.5 * faces.state_back(x1, v1, lam))
+    bar = jnp.where((kind & 1) == 1, 0.0, rest - 0.5 * faces.state_back(x1, v1, lam))
     total = 0.5 * faces.state_back(t1, u1, lam) - rest + jnp.where(wall, faces.mirror(bar), 0.0)
     total = total + select_rows(local_back_ref[...], take(bar, inverse))
     sent = t1_sent.astype(f32)
@@ -611,7 +612,7 @@
     lam1 = lam1_ref[...]
     u, x, v = u_ref[...], x_ref[...], v_ref[...]
     rest = lam1 - 0.5 * faces.rest_back(lam1)
-    bar = jnp.where(kind == 1, 0.0, rest - 0.5 * faces.state_back(x, v, lam1))
+    bar = jnp.where((kind & 1) == 1, 0.0, rest - 0.5 * faces.state_back(x, v, lam1))
     total = 0.5 * faces.state_back(t, u, lam1) - rest + jnp.where(wall, faces.mirror(bar), 0.0)
     total = total + select_rows(local_back_ref[...], take(bar, inverse))
     w = load_tiles(w_ref)

time: 57.4 us -> 57.3 us (level)
  no operation moved by 1% of the time
where the time goes in v11:
time: 57.3 us; the launch traced here: 57.1 us
  blocking collectives  44.2 us (77%)
  Pallas kernels  7.67 us (13%)
  starting transfers between devices  3.84 us (7%)
  between operations  0.73 us (1%)
    all_to_all x2, blocking collectives, pair_peers(): lax.all_to_all(whole, ('dom', 'sub'), split_axis=0, concat_axis=0, tiled=...  44.2 us
    pallas_call x5, Pallas kernels, call(): pl.pallas_call(kernel, out_shape=outs, in_specs=[pl.BlockSpec(memory_spac...  7.67 us
    ppermute x2, starting transfers between devices, chip_partner(): lax.ppermute(value, 'dom', [(d, d ^ 1) for d in range(lax.axis_size('dom'...  3.84 us
  transfers between devices with their start and end apart: 2, of which 2 were waited for; matrix products, arithmetic and copies ran while one was open for 0% of the time, Pallas kernels for 3%

profile of v11, /device:TPU:8, one launch (start us, length us, event | category | flops | bytes accessed | tf_op | source)
XLA Modules:
  0.0 57.1 jit_solution(13035561490868954731)
XLA Ops:
  0.6 0.0 copy-start
  0.6 0.0 copy-start.1
  0.7 2.1 %shard_map.86 = (bf16[8,56,128]{2,1,0:T(8,128)(2,1)S(1)}, bf16[16,88,128]{2,1,0:T(8,128)(2,1)S(1)}, f32[32,384]{1,0:T(8,128)S(1)}, f32[32,384]{1,0:T(8,128)S(1)}...) custom-call(f32[5,32,64]{2,1,0:T(8,128)} %bitcast.4, ...), custom_call_target="tpu_custom_call" | custom-call | flops 200000000 | bytes 1000000 | tf_op jit(solution)/shard_map/pallas_call | solution.py:659
  2.7 1.9 %collective-permute-start = (bf16[8,56,128]{2,1,0:T(8,128)(2,1)S(1)}, bf16[8,56,128]{2,1,0:T(8,128)(2,1)S(1)}, u32[]{:S(2)}, u32[]{:S(2)}) collective-permute-start(bf16[8,56,128]{2,1,0:T(8,128)(2,1)S(1)} %get-tuple-element.55), channel_id=1, source_target_pairs={{0,8},{8,0},{16,24},{24,16},{32,40},{40,32},{48,56},{56,48},{64,72... | collective-permute-start | bytes 344072 | tf_op jit(solution)/shard_map/ppermute | solution.py:678
  4.7 0.0 copy-done
  4.7 0.0 copy-done.1
  4.7 1.1 %shard_map.87 = (f32[32,384]{1,0:T(8,128)S(1)}, f32[192,128]{1,0:T(8,128)S(1)}, f32[96,384]{1,0:T(8,128)S(1)}, f32[192,128]{1,0:T(8,128)S(1)}, f32[192,128]{1,0:...) custom-call(f32[32,384]{1,0:T(8,128)S(1)} %get-tuple-element.44.q_re, ...), custom_call_target="tpu_custom_call" | custom-call | flops 200000000 | bytes 1000000 | tf_op jit(solution)/shard_map/pallas_call | solution.py:659
  5.7 0.2 collective-permute-done
  6.0 28.9 %all_to_all.10.arrived_ref = bf16[16,88,128]{2,1,0:T(8,128)(2,1)S(1)} all-to-all(bf16[16,88,128]{2,1,0:T(8,128)(2,1)S(1)} %fusion.1), channel_id=1, replica_groups={{8,9,10,11,12,13,14,15,16,17,18,19,20,21,22,23},{24,25,26,27,28,29,30,3..., dimensions={0} | all-to-all | bytes 720896 | tf_op jit(solution)/shard_map/all_to_all | solution.py:673
  35.0 2.2 %shard_map.88 = (bf16[8,24,128]{2,1,0:T(8,128)(2,1)S(1)}, bf16[16,40,128]{2,1,0:T(8,128)(2,1)S(1)}, f32[32,384]{1,0:T(8,128)S(1)}, f32[32,384]{1,0:T(8,128)S(1)}...) custom-call(f32[32,384]{1,0:T(8,128)S(1)} %get-tuple-element.51.base, ...), custom_call_target="tpu_custom_call" | custom-call | flops 200000000 | bytes 1000000 | tf_op jit(solution)/shard_map/pallas_call | solution.py:659
  37.2 1.9 %collective-permute-start.1 = (bf16[8,24,128]{2,1,0:T(8,128)(2,1)S(1)}, bf16[8,24,128]{2,1,0:T(8,128)(2,1)S(1)}, u32[]{:S(2)}, u32[]{:S(2)}) collective-permute-start(bf16[8,24,128]{2,1,0:T(8,128)(2,1)S(1)} %get-tuple-element.69), channel_id=1, source_target_pairs={{0,8},{8,0},{16,24},{24,16},{32,40},{40,32},{48,56},{56,48},{64,72... | collective-permute-start | bytes 147464 | tf_op jit(solution)/shard_map/ppermute | solution.py:678
  39.1 0.9 %shard_map.89 = (f32[32,384]{1,0:T(8,128)S(1)}, f32[32,384]{1,0:T(8,128)S(1)}) custom-call(f32[32,384]{1,0:T(8,128)S(1)} %get-tuple-element.44.q_ref, f32[32,384]{1,0:T(8,128)S(1)} %get-tuple-element.45.w_ref, f32[192,128]{1,0:T(8,128)S(1)} %get-tuple-element.46.t_ref, f32[192,128]{1,0:T(8,128)S(1)} %get-tuple-element.70.u_ref, ...), custom_call_target="tpu_custom_call" | custom-call | flops 200000000 | bytes 1000000 | tf_op jit(solution)/shard_map/pallas_call | solution.py:659
  40.0 0.3 collective-permute-done.1
  40.4 15.3 %all_to_all.11.arrived_ref = bf16[16,40,128]{2,1,0:T(8,128)(2,1)S(1)} all-to-all(bf16[16,40,128]{2,1,0:T(8,128)(2,1)S(1)} %fusion), channel_id=1, replica_groups={{8,9,10,11,12,13,14,15,16,17,18,19,20,21,22,23},{24,25,26,27,28,29,30,3..., dimensions={0} | all-to-all | bytes 327680 | tf_op jit(solution)/shard_map/all_to_all | solution.py:673
  55.6 1.4 %shard_map.90 = (f32[5,32,64]{2,1,0:T(8,128)}, f32[5,32,64]{2,1,0:T(8,128)}) custom-call(f32[32,384]{1,0:T(8,128)S(1)} %get-tuple-element.81.end_base_ref, f32[32,384]{1,0:T(8,128)S(1)} %get-tuple-element.82.start_base_ref, bf16[16,40,128]{2,1,0:T(8,128)(2,1)S(1)} %all_to_all.11.arrived_ref, bf16[192,384]{1,0:T(8,128)(2,1)S(1)} %get-tuple-element.59.from_slots_ref, ...), custom_call_target="tpu_custom_call" | custom-call | flops 200000000 | bytes 1000000 | tf_op jit(solution)/shard_map/pallas_call | solution.py:659
  (6 shorter events, 0.1 us)
Async XLA Ops:
  0.6 4.0 %copy-start = (bf16[128,768]{1,0:T(8,128)(2,1)S(1)}, bf16[128,768]{1,0:T(8,128)(2,1)}, u32[]{:S(2)}) copy-start(bf16[128,768]{1,0:T(8,128)(2,1)} %constant.15.clone.backward_ref) | copy-start | bytes 589828
  0.6 4.0 %copy-start.1 = (bf16[384,256]{1,0:T(8,128)(2,1)S(1)}, bf16[384,256]{1,0:T(8,128)(2,1)}, u32[]{:S(2)}) copy-start(bf16[384,256]{1,0:T(8,128)(2,1)} %constant.14.clone.forward_ref) | copy-start | bytes 589828
  2.7 3.2 %collective-permute-start = (bf16[8,56,128]{2,1,0:T(8,128)(2,1)S(1)}, bf16[8,56,128]{2,1,0:T(8,128)(2,1)S(1)}, u32[]{:S(2)}, u32[]{:S(2)}) collective-permute-start(bf16[8,56,128]{2,1,0:T(8,128)(2,1)S(1)} %get-tuple-element.55), channel_id=1, source_target_pairs={{0,8},{8,0},{16,24},{24,16},{32,40},{40,32},{48,56},{56,48},{64,72... | collective-permute-start | bytes 344072 | tf_op jit(solution)/shard_map/ppermute | solution.py:678
  37.2 3.1 %collective-permute-start.1 = (bf16[8,24,128]{2,1,0:T(8,128)(2,1)S(1)}, bf16[8,24,128]{2,1,0:T(8,128)(2,1)S(1)}, u32[]{:S(2)}, u32[]{:S(2)}) collective-permute-start(bf16[8,24,128]{2,1,0:T(8,128)(2,1)S(1)} %get-tuple-element.69), channel_id=1, source_target_pairs={{0,8},{8,0},{16,24},{24,16},{32,40},{40,32},{48,56},{56,48},{64,72... | collective-permute-start | bytes 147464 | tf_op jit(solution)/shard_map/ppermute | solution.py:678
